TPU v7x, 1024 devices: a whole 4x8x16 slice. The times are simulated.
1024 devices in a mesh: img: 128 (over y_lo, z, x), dp: 8 (over y_hi, core).
Axes of the slice: x: 4, y: 8 (y_hi: 4, y_lo: 2; y = y_hi * 2 + y_lo), z: 16, core: 2. Of those that a mesh axis runs over, the one named last changes fastest.
Arguments:
- image_feats: bfloat16 [8, 24576, 1152], P('dp', 'img'), may hold values from -6 to 6
- text_feats: bfloat16 [8, 24576, 1152], P('dp', 'img'), may hold values from -6 to 6
- gains: float32 [2, 1152], replicated, may hold values from 0.5 to 1.5
- shifts: float32 [2, 1152], replicated, may hold values from -1 to 1
- log_scale: float32 [1], replicated, may hold values from 3 to 4
- logit_bias: float32 [1], replicated, may hold values from -3 to -1
Outputs:
- image_grad: bfloat16 [8, 24576, 1152], P('dp', 'img')
- text_grad: bfloat16 [8, 24576, 1152], P('dp', 'img')
- gain_grads: float32 [2, 1152], replicated
- shift_grads: float32 [2, 1152], replicated
- row_loss: float32 [8, 24576], P('dp', 'img')
All inputs are finite; a program needn't handle non-finite values.
Results may differ from a plain program's by a relative error of at most 0.0036.
Values may be sent and summed in bfloat16 or wider, within the bound.
No kernel may reach another device: no remote copies, remote signals or barrier semaphores. Data moves between devices by JAX's collectives and lax.ppermute only.
A program may use at most 32 MiB of HBM per device.

v0:
```python
import jax
import jax.numpy as jnp
from jax import lax
from jax.sharding import PartitionSpec as P

LEVELS = 3


def from_partner(value, axis, stride):
    mask = 2**stride
    pairs = [(source, source ^ mask) for source in range(lax.axis_size(axis))]
    return lax.ppermute(value, axis, pairs)


def final_norm(feats, gain_row, shift_row):
    center = jnp.mean(feats, axis=-1, keepdims=True)
    offset = feats - center
    spread = jnp.mean(offset * offset, axis=-1, keepdims=True)
    normed = offset * lax.rsqrt(spread + 1e-06)
    unnormed = normed * gain_row + shift_row
    return unnormed * lax.rsqrt(jnp.sum(unnormed * unnormed, axis=-1, keepdims=True) + 1e-06)


def tile_terms(left_emb, right_emb, left_first, logit_scale, logit_shift):
    logits = (
        logit_scale * jnp.dot(left_emb, right_emb.T, preferred_element_type=jnp.float32)
        + logit_shift
    )
    left_index = left_first + jnp.arange(left_emb.shape[0], dtype=jnp.int32)
    right_index = jnp.arange(right_emb.shape[0], dtype=jnp.int32)
    labels = jnp.where(left_index[:, None] == right_index[None, :], 1.0, -1.0).astype(jnp.float32)
    row_mean = jnp.mean(jax.nn.softplus(-labels * logits), axis=1)
    coeff_tile = (-labels * jax.nn.sigmoid(-labels * logits)).astype(jnp.bfloat16)
    return (row_mean, coeff_tile)


def own_bit(position):
    return lax.axis_index("img") >> position & 1


def gather_texts(block, lowest):
    for level in range(LEVELS):
        partner = from_partner(block, "img", lowest + level)
        block = jnp.where(
            own_bit(lowest + level) == 0,
            jnp.concatenate([block, partner], axis=0),
            jnp.concatenate([partner, block], axis=0),
        )
    return block


def halve_partials(partials, lowest):
    for level in reversed(range(LEVELS)):
        half_rows = partials.shape[0] // 2
        lower = partials[:half_rows]
        upper = partials[half_rows:]
        keep_low = own_bit(lowest + level) == 0
        sending = jnp.where(keep_low, upper, lower)
        keeping = jnp.where(keep_low, lower, upper)
        partials = keeping + from_partner(sending, "img", lowest + level)
    return partials


def body(image_feats, text_feats, gains, shifts, log_scale, logit_bias):
    logit_scale = jnp.exp(log_scale[0])
    logit_shift = logit_bias[0]
    image_unit, image_pull = jax.vjp(
        final_norm, image_feats[0].astype(jnp.float32), gains[0], shifts[0]
    )
    text_unit, text_pull = jax.vjp(
        final_norm, text_feats[0].astype(jnp.float32), gains[1], shifts[1]
    )
    image_emb = image_unit.astype(jnp.bfloat16)
    text_emb = text_unit.astype(jnp.bfloat16)
    row_count = image_emb.shape[0]
    group_stride = lax.axis_size("img") // 2**LEVELS
    lowest = group_stride.bit_length() - 1
    member = lax.axis_index("img") // group_stride
    own_first = member * row_count
    texts_all = gather_texts(text_emb, lowest)
    row_mean, coeff_tile = tile_terms(image_emb, texts_all, own_first, logit_scale, logit_shift)
    image_acc = jnp.dot(coeff_tile, texts_all, preferred_element_type=jnp.float32)
    partials = jnp.dot(coeff_tile.T, image_emb, preferred_element_type=jnp.float32)
    text_acc = halve_partials(partials, lowest)
    image_feat_grad, image_gain, image_shift = image_pull(logit_scale * image_acc)
    text_feat_grad, text_gain, text_shift = text_pull(logit_scale * text_acc)
    gain_local = jnp.stack([image_gain, text_gain])
    shift_local = jnp.stack([image_shift, text_shift])
    gain_grads, shift_grads = lax.psum((gain_local, shift_local), ("img", "dp"))
    image_grad = image_feat_grad.astype(jnp.bfloat16)[None]
    text_grad = text_feat_grad.astype(jnp.bfloat16)[None]
    return (image_grad, text_grad, gain_grads, shift_grads, row_mean[None])


def solution(mesh):
    placed = (P("dp", "img", None), P("dp", "img", None), P(), P(), P(), P())
    return jax.shard_map(
        body,
        mesh=mesh,
        in_specs=placed,
        out_specs=(P("dp", "img", None), P("dp", "img", None), P(), P(), P("dp", "img")),
        check_vma=False,
    )
```

profile of v0, /device:TPU:6, one launch (start us, length us, event | category | flops | bytes accessed | tf_op | source)
XLA Modules:
  0.0 580.4 jit_solution(18069927125406338928)
XLA Ops:
  0.6 1.2 convert_reduce_fusion
  1.8 1.3 fusion.37
  3.1 0.8 slice_reduce_fusion.2
  3.9 1.4 fusion.33
  5.3 1.3 fusion.34
  6.6 10.9 %collective-permute-start = (bf16[192,1152]{1,0:T(8,128)(2,1)S(1)}, bf16[192,1152]{1,0:T(8,128)(2,1)S(1)}, u32[]{:S(2)}, u32[]{:S(2)}) collective-permute-start(bf16[192,1152]{1,0:T(8,128)(2,1)S(1)} %fusion.34), channel_id=1, source_target_pairs={{0,128},{8,136},{16,144},{24,152},{32,160},{40,168},{48,176},{56,1... | collective-permute-start | bytes 1327112 | tf_op jit(solution)/shard_map/ppermute | solution.py:12
  17.5 38.6 %collective-permute-done = bf16[192,1152]{1,0:T(8,128)(2,1)S(1)} collective-permute-done((bf16[192,1152]{1,0:T(8,128)(2,1)S(1)}, bf16[192,1152]{1,0:T(8,128)(2,1)S(1)}, u32[]{:S(2)}, u32[]{:S(2)}) %collective-permute-start) | collective-permute-done | bytes 442400 | tf_op jit(solution)/shard_map/ppermute | solution.py:12
  56.1 0.3 maximum_select_fusion.2
  56.4 35.1 %collective-permute-start.1 = (bf16[384,1152]{1,0:T(8,128)(2,1)S(1)}, bf16[384,1152]{1,0:T(8,128)(2,1)}, u32[]{:S(2)}, u32[]{:S(2)}) collective-permute-start(bf16[384,1152]{1,0:T(8,128)(2,1)S(1)} %maximum_select_fusion.2), channel_id=1, source_target_pairs={{0,256},{8,264},{16,272},{24,280},{32,288},{40,296},{48,304},{56,3... | collective-permute-start | bytes 2654216 | tf_op jit(solution)/shard_map/ppermute | solution.py:12
  91.5 0.0 copy-start.1
  91.5 56.0 %collective-permute-done.1 = bf16[384,1152]{1,0:T(8,128)(2,1)} collective-permute-done((bf16[384,1152]{1,0:T(8,128)(2,1)S(1)}, bf16[384,1152]{1,0:T(8,128)(2,1)}, u32[]{:S(2)}, u32[]{:S(2)}) %collective-permute-start.1) | collective-permute-done | bytes 884768 | tf_op jit(solution)/shard_map/ppermute | solution.py:12
  147.6 2.0 maximum_select_fusion.1
  149.5 3.5 collective-permute-start.2
  154.4 0.0 copy-done.1
  154.4 0.1 convert_reduce_fusion.1
  154.6 0.3 fusion.19
  154.8 0.4 fusion.15
  155.2 36.8 %collective-permute-done.2 = bf16[768,1152]{1,0:T(8,128)(2,1)} collective-permute-done((bf16[768,1152]{1,0:T(8,128)(2,1)S(1)}, bf16[768,1152]{1,0:T(8,128)(2,1)}, u32[]{:S(2)}, u32[]{:S(2)}) %collective-permute-start.2) | collective-permute-done | bytes 1769504 | tf_op jit(solution)/shard_map/ppermute | solution.py:12
  192.0 4.4 fusion.2
  196.3 1.6 fusion.45
  198.0 0.4 slice_select_fusion
  198.4 3.5 collective-permute-start.3
  201.8 75.9 %collective-permute-done.3 = f32[768,1152]{1,0:T(8,128)S(1)} collective-permute-done((f32[768,1152]{1,0:T(8,128)S(1)}, f32[768,1152]{1,0:T(8,128)S(1)}, u32[]{:S(2)}, u32[]{:S(2)}) %collective-permute-start.3) | collective-permute-done | bytes 3538976 | tf_op jit(solution)/shard_map/ppermute | solution.py:12
  277.7 0.5 select_add_fusion
  278.2 0.2 slice_select_fusion.1
  278.4 9.1 %collective-permute-start.4 = (f32[384,1152]{1,0:T(8,128)S(1)}, f32[384,1152]{1,0:T(8,128)S(1)}, u32[]{:S(2)}, u32[]{:S(2)}) collective-permute-start(f32[384,1152]{1,0:T(8,128)S(1)} %slice_select_fusion.1), channel_id=1, source_target_pairs={{0,256},{8,264},{16,272},{24,280},{32,288},{40,296},{48,304},{56,3... | collective-permute-start | bytes 5308424 | tf_op jit(solution)/shard_map/ppermute | solution.py:12
  287.5 3.8 fusion.17
  291.3 0.7 fusion.18
  292.0 0.4 fusion.49
  292.4 90.2 %collective-permute-done.4 = f32[384,1152]{1,0:T(8,128)S(1)} collective-permute-done((f32[384,1152]{1,0:T(8,128)S(1)}, f32[384,1152]{1,0:T(8,128)S(1)}, u32[]{:S(2)}, u32[]{:S(2)}) %collective-permute-start.4) | collective-permute-done | bytes 1769504 | tf_op jit(solution)/shard_map/ppermute | solution.py:12
  382.6 0.3 select_add_fusion.1
  382.9 0.0 copy-start
  382.9 0.1 slice_select_fusion.2
  383.0 19.7 %collective-permute-start.5 = (f32[192,1152]{1,0:T(8,128)S(1)}, f32[192,1152]{1,0:T(8,128)S(1)}, u32[]{:S(2)}, u32[]{:S(2)}) collective-permute-start(f32[192,1152]{1,0:T(8,128)S(1)} %slice_select_fusion.2), channel_id=1, source_target_pairs={{0,128},{8,136},{16,144},{24,152},{32,160},{40,168},{48,176},{56,1... | collective-permute-start | bytes 2654216 | tf_op jit(solution)/shard_map/ppermute | solution.py:12
  402.8 0.6 broadcast_multiply_fusion
  403.3 0.9 fusion.39
  404.2 52.3 %collective-permute-done.5 = f32[192,1152]{1,0:T(8,128)S(1)} collective-permute-done((f32[192,1152]{1,0:T(8,128)S(1)}, f32[192,1152]{1,0:T(8,128)S(1)}, u32[]{:S(2)}, u32[]{:S(2)}) %collective-permute-start.5) | collective-permute-done | bytes 884768 | tf_op jit(solution)/shard_map/ppermute | solution.py:12
  456.5 0.0 copy-done
  456.5 0.5 fusion.35
  457.0 0.7 fusion.36
  457.7 0.4 fusion.48
  458.2 0.9 fusion.40
  459.0 121.4 %all-reduce = (f32[2,1152]{1,0:T(2,128)}, f32[2,1152]{1,0:T(2,128)}) all-reduce(f32[2,1152]{1,0:T(2,128)S(1)} %pad_maximum_fusion, f32[2,1152]{1,0:T(2,128)S(1)} %pad_maximum_fusion.1), channel_id=1, replica_groups=mesh['img'=128,'dp'=8] {'img','dp'}, use_global_device_ids=true, to_apply=%region_14.15 | all-reduce | flops 4608 | bytes 36864 | tf_op jit(solution)/shard_map/psum | solution.py:89
  (19 shorter events, 0.1 us)
Async XLA Ops:
  6.6 49.5 %collective-permute-start = (bf16[192,1152]{1,0:T(8,128)(2,1)S(1)}, bf16[192,1152]{1,0:T(8,128)(2,1)S(1)}, u32[]{:S(2)}, u32[]{:S(2)}) collective-permute-start(bf16[192,1152]{1,0:T(8,128)(2,1)S(1)} %fusion.34), channel_id=1, source_target_pairs={{0,128},{8,136},{16,144},{24,152},{32,160},{40,168},{48,176},{56,1... | collective-permute-start | bytes 1327112 | tf_op jit(solution)/shard_map/ppermute | solution.py:12
  56.4 91.2 %collective-permute-start.1 = (bf16[384,1152]{1,0:T(8,128)(2,1)S(1)}, bf16[384,1152]{1,0:T(8,128)(2,1)}, u32[]{:S(2)}, u32[]{:S(2)}) collective-permute-start(bf16[384,1152]{1,0:T(8,128)(2,1)S(1)} %maximum_select_fusion.2), channel_id=1, source_target_pairs={{0,256},{8,264},{16,272},{24,280},{32,288},{40,296},{48,304},{56,3... | collective-permute-start | bytes 2654216 | tf_op jit(solution)/shard_map/ppermute | solution.py:12
  91.5 62.9 %copy-start.1 = (bf16[1,192,1152]{2,1,0:T(8,128)(2,1)S(1)}, bf16[1,192,1152]{2,1,0:T(8,128)(2,1)}, u32[]{:S(2)}) copy-start(bf16[1,192,1152]{2,1,0:T(8,128)(2,1)} %param.6) | copy-start | bytes 1327108
  149.5 42.4 %collective-permute-start.2 = (bf16[768,1152]{1,0:T(8,128)(2,1)S(1)}, bf16[768,1152]{1,0:T(8,128)(2,1)}, u32[]{:S(2)}, u32[]{:S(2)}) collective-permute-start(bf16[768,1152]{1,0:T(8,128)(2,1)S(1)} %maximum_select_fusion.1), channel_id=1, source_target_pairs={{0,512},{8,520},{16,528},{24,536},{32,544},{40,552},{48,560},{56,5... | collective-permute-start | bytes 5308424 | tf_op jit(solution)/shard_map/ppermute | solution.py:12
  198.4 79.4 %collective-permute-start.3 = (f32[768,1152]{1,0:T(8,128)S(1)}, f32[768,1152]{1,0:T(8,128)S(1)}, u32[]{:S(2)}, u32[]{:S(2)}) collective-permute-start(f32[768,1152]{1,0:T(8,128)S(1)} %slice_select_fusion), channel_id=1, source_target_pairs={{0,512},{8,520},{16,528},{24,536},{32,544},{40,552},{48,560},{56,5... | collective-permute-start | bytes 10616840 | tf_op jit(solution)/shard_map/ppermute | solution.py:12
  278.4 104.2 %collective-permute-start.4 = (f32[384,1152]{1,0:T(8,128)S(1)}, f32[384,1152]{1,0:T(8,128)S(1)}, u32[]{:S(2)}, u32[]{:S(2)}) collective-permute-start(f32[384,1152]{1,0:T(8,128)S(1)} %slice_select_fusion.1), channel_id=1, source_target_pairs={{0,256},{8,264},{16,272},{24,280},{32,288},{40,296},{48,304},{56,3... | collective-permute-start | bytes 5308424 | tf_op jit(solution)/shard_map/ppermute | solution.py:12
  382.9 73.6 %copy-start = (bf16[1,192,1152]{2,1,0:T(8,128)(2,1)S(1)}, bf16[1,192,1152]{2,1,0:T(8,128)(2,1)}, u32[]{:S(2)}) copy-start(bf16[1,192,1152]{2,1,0:T(8,128)(2,1)} %param.7) | copy-start | bytes 1327108
  383.0 73.5 %collective-permute-start.5 = (f32[192,1152]{1,0:T(8,128)S(1)}, f32[192,1152]{1,0:T(8,128)S(1)}, u32[]{:S(2)}, u32[]{:S(2)}) collective-permute-start(f32[192,1152]{1,0:T(8,128)S(1)} %slice_select_fusion.2), channel_id=1, source_target_pairs={{0,128},{8,136},{16,144},{24,152},{32,160},{40,168},{48,176},{56,1... | collective-permute-start | bytes 2654216 | tf_op jit(solution)/shard_map/ppermute | solution.py:12
where the time goes:
time: 584 us; the launch traced here: 580 us
  waiting for transfers between devices  350 us (60%)
  blocking collectives  121 us (21%)
  starting transfers between devices  81.9 us (14%)
  other arithmetic  14.6 us (2%)
  matrix products  9.76 us (2%)
    ppermute x6, waiting for transfers between devices, from_partner(): return lax.ppermute(value, axis, pairs)  350 us
    psum x1, blocking collectives, body(): gain_grads, shift_grads = lax.psum((gain_local, shift_local), ('img', 'dp'))  121 us
    ppermute x6, starting transfers between devices, from_partner(): return lax.ppermute(value, axis, pairs)  81.9 us
  transfers between devices with their start and end apart: 6, of which 6 were waited for; matrix products, arithmetic and copies ran while one was open for 1% of the time, Pallas kernels for 0%

commit v1 on v0

v1 whole, which is shorter than its diff:
```python
import jax
import jax.numpy as jnp
from jax import lax
from jax.sharding import PartitionSpec as P

AXES = ("img", "dp")
RING = 4
X_CHIPS = 4
Z_BLOCK = 4
Y_HIGH = 4


def final_norm(feats, gain_row, shift_row):
    center = jnp.mean(feats, axis=-1, keepdims=True)
    offset = feats - center
    spread = jnp.mean(offset * offset, axis=-1, keepdims=True)
    normed = offset * lax.rsqrt(spread + 1e-06)
    unnormed = normed * gain_row + shift_row
    return unnormed * lax.rsqrt(jnp.sum(unnormed * unnormed, axis=-1, keepdims=True) + 1e-06)


def near(place):
    return place ^ 1


def far(place):
    return RING - 1 - place


class Routes:
    def __init__(self, sizes):
        self.sizes = sizes
        y_lo, z_hi, z_lo, x, y_hi, core = sizes
        self.count = y_lo * z_hi * z_lo * x * y_hi * core

    def split(self, index):
        place = []
        for size in reversed(self.sizes):
            place.append(index % size)
            index //= size
        return place[::-1]

    def join(self, place):
        index = 0
        for size, at in zip(self.sizes, place):
            index = index * size + at
        return index

    def pairs(self, move):
        out = []
        for index in range(self.count):
            place = self.split(index)
            out.append((index, self.join(move(list(place)))))
        return out

    def along(self, axis, step):
        def move(place):
            place[axis] = step(place[axis])
            return place

        return self.pairs(move)

    def across_y(self):
        return self.along(0, near)

    def towers(self):
        def text(place):
            place[1] = far(place[1]) if place[5] == 0 else near(place[1])
            return place

        def image(place):
            place[1] = near(place[1]) if place[5] == 0 else far(place[1])
            return place

        return self.pairs(text), self.pairs(image)

    def everyone(self):
        steps = []
        for axis in (5, 3, 2, 0, 4, 1):
            if self.sizes[axis] >= 2:
                steps.append(self.along(axis, near))
            if self.sizes[axis] == 4:
                steps.append(self.along(axis, far))
        return steps


def send(value, pairs):
    return lax.ppermute(value, AXES, pairs)


def sum_everywhere(value, steps):
    for pairs in steps:
        value = value + send(value, pairs)
    return value


def make_body(routes):
    text_pairs, image_pairs = routes.towers()
    y_pairs = routes.across_y()
    steps = routes.everyone()
    group_rows = 2 * RING

    def body(image_feats, text_feats, gains, shifts, log_scale, logit_bias):
        logit_scale = jnp.exp(log_scale[0])
        logit_shift = logit_bias[0]
        text_unit, text_pull = jax.vjp(
            final_norm, text_feats[0].astype(jnp.float32), gains[1], shifts[1]
        )
        text_emb = text_unit.astype(jnp.bfloat16)
        image_unit, image_pull = jax.vjp(
            final_norm, image_feats[0].astype(jnp.float32), gains[0], shifts[0]
        )
        image_emb = image_unit.astype(jnp.bfloat16)
        rows = image_emb.shape[0]

        text_z = send(text_emb, text_pairs)
        image_z = send(image_emb, image_pairs)
        text_y = send(text_emb, y_pairs)
        text_zy = send(text_z, y_pairs)

        images = jnp.concatenate([image_emb, image_z], axis=0)
        texts = jnp.concatenate([text_emb, text_z, text_y, text_zy], axis=0)
        logits = (
            logit_scale * jnp.dot(images, texts.T, preferred_element_type=jnp.float32)
            + logit_shift
        )
        row_at = lax.broadcasted_iota(jnp.int32, logits.shape, 0)
        column_at = lax.broadcasted_iota(jnp.int32, logits.shape, 1)
        signs = jnp.where((row_at == column_at) & (row_at < rows), -1.0, 1.0)
        loss_sums = jnp.sum(jax.nn.softplus(signs * logits), axis=1)
        coeff = (signs * jax.nn.sigmoid(signs * logits)).astype(jnp.bfloat16)

        text_parts = jnp.dot(coeff.T, images, preferred_element_type=jnp.float32)
        text_zy_back = send(text_parts[3 * rows :].astype(jnp.bfloat16), y_pairs)
        image_parts = jnp.dot(coeff, texts, preferred_element_type=jnp.float32)
        image_back = send(image_parts[rows:].astype(jnp.bfloat16), image_pairs)
        loss_back = send(loss_sums[rows:], image_pairs)
        text_y_back = send(text_parts[2 * rows : 3 * rows].astype(jnp.bfloat16), y_pairs)
        text_z_sum = text_parts[rows : 2 * rows] + text_zy_back.astype(jnp.float32)
        text_z_back = send(text_z_sum.astype(jnp.bfloat16), text_pairs)

        image_acc = image_parts[:rows] + image_back.astype(jnp.float32)
        text_acc = (
            text_parts[:rows] + text_y_back.astype(jnp.float32) + text_z_back.astype(jnp.float32)
        )
        row_mean = (loss_sums[:rows] + loss_back) / (group_rows * rows)

        image_feat_grad, image_gain, image_shift = image_pull(logit_scale * image_acc)
        text_feat_grad, text_gain, text_shift = text_pull(logit_scale * text_acc)
        sums = sum_everywhere(jnp.stack([image_gain, text_gain, image_shift, text_shift]), steps)
        image_grad = image_feat_grad.astype(jnp.bfloat16)[None]
        text_grad = text_feat_grad.astype(jnp.bfloat16)[None]
        return (image_grad, text_grad, sums[:2], sums[2:], row_mean[None])

    return body


def build(mesh, sizes):
    placed = (P("dp", "img", None), P("dp", "img", None), P(), P(), P(), P())
    return jax.shard_map(
        make_body(Routes(sizes)),
        mesh=mesh,
        in_specs=placed,
        out_specs=(P("dp", "img", None), P("dp", "img", None), P(), P(), P("dp", "img")),
        check_vma=False,
    )


def solution(mesh):
    y_high, cores = Y_HIGH, mesh.shape["dp"] // Y_HIGH
    y_low = mesh.shape["img"] // (RING * Z_BLOCK * X_CHIPS)
    return build(mesh, (y_low, RING, Z_BLOCK, X_CHIPS, y_high, cores))
```

time: 584 us -> 208 us (0.36)
  waiting for transfers between devices: 350 us -> 72.5 us
  blocking collectives: 121 us -> 0 us
  starting transfers between devices: 81.9 us -> 113 us
  matrix products: 9.76 us -> 3.84 us
    ppermute x6 -> x19, waiting for transfers between devices: 350 us -> 72.5 us  [send(): return lax.ppermute(value, AXES, pairs)]
    psum x1 -> x0, blocking collectives: 121 us -> none  [body(): gain_grads, shift_grads = lax.psum((gain_local, shift_local), ('img', 'dp'))]
    ppermute x6 -> x19, starting transfers between devices: 81.9 us -> 113 us  [send(): return lax.ppermute(value, AXES, pairs)]
    dot_general x3, matrix products: 9.76 us -> 3.84 us  [the longest x1 1.49 us: body(): jnp.dot(images, texts.T, preferred_element_type=jnp.float32)]
  transfers between devices with their start and end apart: 6 -> 19, of which waited for: 6 -> 13; matrix products, arithmetic and copies ran while one was open for 1% -> 3% of each run, Pallas kernels for 0% -> 0%
where the time goes in v1:
time: 208 us; the launch traced here: 206 us
  starting transfers between devices  113 us (54%)
  waiting for transfers between devices  72.5 us (35%)
  other arithmetic  12.2 us (6%)
  matrix products  3.84 us (2%)
  between operations  2.35 us (1%)
    ppermute x19, starting transfers between devices, send(): return lax.ppermute(value, AXES, pairs)  113 us
    ppermute x19, waiting for transfers between devices, send(): return lax.ppermute(value, AXES, pairs)  72.5 us
  transfers between devices with their start and end apart: 19, of which 13 were waited for; matrix products, arithmetic and copies ran while one was open for 3% of the time, Pallas kernels for 0%

profile of v1, /device:TPU:6, one launch (start us, length us, event | category | flops | bytes accessed | tf_op | source)
XLA Modules:
  0.0 205.6 jit_solution(16748913402403657085)
XLA Ops:
  0.6 1.2 convert_reduce_fusion
  1.9 1.3 fusion.38
  3.1 0.8 slice_reduce_fusion.2
  4.0 1.4 fusion.34
  5.4 1.3 fusion.35
  6.7 3.5 %collective-permute-start.2 = (bf16[192,1152]{1,0:T(8,128)(2,1)S(1)}, bf16[192,1152]{1,0:T(8,128)(2,1)S(1)}, u32[]{:S(2)}, u32[]{:S(2)}) collective-permute-start(bf16[192,1152]{1,0:T(8,128)(2,1)S(1)} %fusion.35), channel_id=1, source_target_pairs={{0,512},{1,513},{2,514},{3,515},{4,516},{5,517},{6,518},{7,519},{8... | collective-permute-start | bytes 1327112 | tf_op jit(solution)/shard_map/ppermute | solution.py:88
  10.2 18.2 %collective-permute-start.1 = (bf16[192,1152]{1,0:T(8,128)(2,1)S(1)}, bf16[192,1152]{1,0:T(8,128)(2,1)S(1)}, u32[]{:S(2)}, u32[]{:S(2)}) collective-permute-start(bf16[192,1152]{1,0:T(8,128)(2,1)S(1)} %fusion.35), channel_id=1, source_target_pairs={{0,384},{1,129},{2,386},{3,131},{4,388},{5,133},{6,390},{7,135},{8... | collective-permute-start | bytes 1327112 | tf_op jit(solution)/shard_map/ppermute | solution.py:88
  28.4 0.1 convert_reduce_fusion.1
  28.5 0.3 fusion.20
  28.8 0.4 fusion.16
  29.2 0.3 fusion.17
  29.5 3.6 %collective-permute-start = (bf16[192,1152]{1,0:T(8,128)(2,1)S(1)}, bf16[192,1152]{1,0:T(8,128)(2,1)S(1)}, u32[]{:S(2)}, u32[]{:S(2)}) collective-permute-start(bf16[192,1152]{1,0:T(8,128)(2,1)S(1)} %fusion.17), channel_id=1, source_target_pairs={{0,128},{1,385},{2,130},{3,387},{4,132},{5,389},{6,134},{7,391},{8... | collective-permute-start | bytes 1327112 | tf_op jit(solution)/shard_map/ppermute | solution.py:88
  33.1 17.9 %collective-permute-done.1 = bf16[192,1152]{1,0:T(8,128)(2,1)S(1)} collective-permute-done((bf16[192,1152]{1,0:T(8,128)(2,1)S(1)}, bf16[192,1152]{1,0:T(8,128)(2,1)S(1)}, u32[]{:S(2)}, u32[]{:S(2)}) %collective-permute-start.1) | collective-permute-done | bytes 442400 | tf_op jit(solution)/shard_map/ppermute | solution.py:88
  51.0 2.3 %collective-permute-start.3 = (bf16[192,1152]{1,0:T(8,128)(2,1)S(1)}, bf16[192,1152]{1,0:T(8,128)(2,1)S(1)}, u32[]{:S(2)}, u32[]{:S(2)}) collective-permute-start(bf16[192,1152]{1,0:T(8,128)(2,1)S(1)} %collective-permute-done.1), channel_id=1, source_target_pairs={{0,512},{1,513},{2,514},{3,515},{4,516},{5,517},{6,518},{7,519},{8... | collective-permute-start | bytes 1327112 | tf_op jit(solution)/shard_map/ppermute | solution.py:88
  54.7 1.6 collective-permute-done
  56.3 0.0 collective-permute-done.2
  56.3 4.9 %collective-permute-done.3 = bf16[192,1152]{1,0:T(8,128)(2,1)S(1)} collective-permute-done((bf16[192,1152]{1,0:T(8,128)(2,1)S(1)}, bf16[192,1152]{1,0:T(8,128)(2,1)S(1)}, u32[]{:S(2)}, u32[]{:S(2)}) %collective-permute-start.3) | collective-permute-done | bytes 442400 | tf_op jit(solution)/shard_map/ppermute | solution.py:88
  61.2 1.5 fusion.2
  62.7 1.3 fusion.60
  64.0 0.1 fusion.58
  64.0 2.4 %collective-permute-start.6 = (bf16[192,1152]{1,0:T(8,128)(2,1)S(1)}, bf16[192,1152]{1,0:T(8,128)(2,1)S(1)}, u32[]{:S(2)}, u32[]{:S(2)}) collective-permute-start(bf16[192,1152]{1,0:T(8,128)(2,1)S(1)} %get-tuple-element.22), channel_id=1, source_target_pairs={{0,512},{1,513},{2,514},{3,515},{4,516},{5,517},{6,518},{7,519},{8... | collective-permute-start | bytes 1327112 | tf_op jit(solution)/shard_map/ppermute | solution.py:88
  66.4 1.1 fusion.47
  67.5 0.1 slice.92
  67.5 22.1 %collective-permute-start.4 = (bf16[192,1152]{1,0:T(8,128)(2,1)S(1)}, bf16[192,1152]{1,0:T(8,128)(2,1)S(1)}, u32[]{:S(2)}, u32[]{:S(2)}) collective-permute-start(bf16[192,1152]{1,0:T(8,128)(2,1)S(1)} %slice.92), channel_id=1, source_target_pairs={{0,128},{1,385},{2,130},{3,387},{4,132},{5,389},{6,134},{7,391},{8... | collective-permute-start | bytes 1327112 | tf_op jit(solution)/shard_map/ppermute | solution.py:88
  89.7 3.5 %collective-permute-start.5 = (bf16[192,1152]{1,0:T(8,128)(2,1)S(1)}, bf16[192,1152]{1,0:T(8,128)(2,1)S(1)}, u32[]{:S(2)}, u32[]{:S(2)}) collective-permute-start(bf16[192,1152]{1,0:T(8,128)(2,1)S(1)} %get-tuple-element.21), channel_id=1, source_target_pairs={{0,512},{1,513},{2,514},{3,515},{4,516},{5,517},{6,518},{7,519},{8... | collective-permute-start | bytes 1327112 | tf_op jit(solution)/shard_map/ppermute | solution.py:88
  93.2 0.0 collective-permute-done.6
  93.2 0.1 fusion.40
  93.3 8.7 %collective-permute-start.7 = (bf16[192,1152]{1,0:T(8,128)(2,1)S(1)}, bf16[192,1152]{1,0:T(8,128)(2,1)S(1)}, u32[]{:S(2)}, u32[]{:S(2)}) collective-permute-start(bf16[192,1152]{1,0:T(8,128)(2,1)S(1)} %fusion.40), channel_id=1, source_target_pairs={{0,384},{1,129},{2,386},{3,131},{4,388},{5,133},{6,390},{7,135},{8... | collective-permute-start | bytes 1327112 | tf_op jit(solution)/shard_map/ppermute | solution.py:88
  102.0 20.8 %collective-permute-done.4 = bf16[192,1152]{1,0:T(8,128)(2,1)S(1)} collective-permute-done((bf16[192,1152]{1,0:T(8,128)(2,1)S(1)}, bf16[192,1152]{1,0:T(8,128)(2,1)S(1)}, u32[]{:S(2)}, u32[]{:S(2)}) %collective-permute-start.4) | collective-permute-done | bytes 442400 | tf_op jit(solution)/shard_map/ppermute | solution.py:88
  122.8 0.4 fusion.18
  123.2 0.0 copy-start.1
  123.3 0.8 fusion.19
  124.1 0.0 collective-permute-done.5
  124.1 0.0 collective-permute-done.7
  124.1 0.2 copy-done.1
  124.2 0.5 fusion.36
  124.7 0.8 fusion.37
  125.6 1.9 collective-permute-start.8
  127.6 0.1 slice.58
  127.6 2.6 %collective-permute-start.18 = (f32[192]{0:T(256)S(1)}, f32[192]{0:T(256)S(1)}, u32[]{:S(2)}, u32[]{:S(2)}) collective-permute-start(f32[192]{0:T(256)S(1)} %slice.58), channel_id=1, source_target_pairs={{0,128},{1,385},{2,130},{3,387},{4,132},{5,389},{6,134},{7,391},{8... | collective-permute-start | bytes 2312 | tf_op jit(solution)/shard_map/ppermute | solution.py:88
  130.3 2.8 %collective-permute-start.9 = (f32[4,1152]{1,0:T(4,128)S(1)}, f32[4,1152]{1,0:T(4,128)S(1)}, u32[]{:S(2)}, u32[]{:S(2)}) collective-permute-start(f32[4,1152]{1,0:T(4,128)S(1)} %fusion.53), channel_id=1, source_target_pairs={{0,8},{1,9},{2,10},{3,11},{4,12},{5,13},{6,14},{7,15},{8,0},{9,1},... | collective-permute-start | bytes 55304 | tf_op jit(solution)/shard_map/ppermute | solution.py:88
  133.0 4.0 %collective-permute-done.18 = f32[192]{0:T(256)S(1)} collective-permute-done((f32[192]{0:T(256)S(1)}, f32[192]{0:T(256)S(1)}, u32[]{:S(2)}, u32[]{:S(2)}) %collective-permute-start.18) | collective-permute-done | bytes 800 | tf_op jit(solution)/shard_map/ppermute | solution.py:88
  137.0 0.6 add_multiply_fusion
  137.6 7.9 %collective-permute-start.10 = (f32[4,1152]{1,0:T(4,128)S(1)}, f32[4,1152]{1,0:T(4,128)S(1)}, u32[]{:S(2)}, u32[]{:S(2)}) collective-permute-start(f32[4,1152]{1,0:T(4,128)S(1)} %fusion.61), channel_id=1, source_target_pairs={{0,24},{1,25},{2,26},{3,27},{4,28},{5,29},{6,30},{7,31},{8,16},{9,... | collective-permute-start | bytes 55304 | tf_op jit(solution)/shard_map/ppermute | solution.py:88
  145.5 1.7 collective-permute-done.10
  147.3 5.3 %collective-permute-start.11 = (f32[4,1152]{1,0:T(4,128)S(1)}, f32[4,1152]{1,0:T(4,128)S(1)}, u32[]{:S(2)}, u32[]{:S(2)}) collective-permute-start(f32[4,1152]{1,0:T(4,128)S(1)} %add.137), channel_id=1, source_target_pairs={{0,32},{1,33},{2,34},{3,35},{4,36},{5,37},{6,38},{7,39},{8,40},{9,... | collective-permute-start | bytes 55304 | tf_op jit(solution)/shard_map/ppermute | solution.py:88
  152.5 0.4 fusion.57
  152.9 1.3 collective-permute-done.11
  154.3 9.7 %collective-permute-start.12 = (f32[4,1152]{1,0:T(4,128)S(1)}, f32[4,1152]{1,0:T(4,128)S(1)}, u32[]{:S(2)}, u32[]{:S(2)}) collective-permute-start(f32[4,1152]{1,0:T(4,128)S(1)} %add.138), channel_id=1, source_target_pairs={{0,96},{1,97},{2,98},{3,99},{4,100},{5,101},{6,102},{7,103},{8,104... | collective-permute-start | bytes 55304 | tf_op jit(solution)/shard_map/ppermute | solution.py:88
  164.0 1.7 collective-permute-done.12
  165.7 1.9 collective-permute-start.13
  167.6 0.9 fusion.45
  168.5 2.8 %collective-permute-done.13 = f32[4,1152]{1,0:T(4,128)S(1)} collective-permute-done((f32[4,1152]{1,0:T(4,128)S(1)}, f32[4,1152]{1,0:T(4,128)S(1)}, u32[]{:S(2)}, u32[]{:S(2)}) %collective-permute-start.13) | collective-permute-done | bytes 18464 | tf_op jit(solution)/shard_map/ppermute | solution.py:88
  171.4 3.2 %collective-permute-start.14 = (f32[4,1152]{1,0:T(4,128)S(1)}, f32[4,1152]{1,0:T(4,128)S(1)}, u32[]{:S(2)}, u32[]{:S(2)}) collective-permute-start(f32[4,1152]{1,0:T(4,128)S(1)} %add.140), channel_id=1, source_target_pairs={{0,2},{1,3},{2,0},{3,1},{4,6},{5,7},{6,4},{7,5},{8,10},{9,11},{10,... | collective-permute-start | bytes 55304 | tf_op jit(solution)/shard_map/ppermute | solution.py:88
  174.6 3.3 %collective-permute-done.14 = f32[4,1152]{1,0:T(4,128)S(1)} collective-permute-done((f32[4,1152]{1,0:T(4,128)S(1)}, f32[4,1152]{1,0:T(4,128)S(1)}, u32[]{:S(2)}, u32[]{:S(2)}) %collective-permute-start.14) | collective-permute-done | bytes 18464 | tf_op jit(solution)/shard_map/ppermute | solution.py:88
  177.9 3.1 %collective-permute-start.15 = (f32[4,1152]{1,0:T(4,128)S(1)}, f32[4,1152]{1,0:T(4,128)S(1)}, u32[]{:S(2)}, u32[]{:S(2)}) collective-permute-start(f32[4,1152]{1,0:T(4,128)S(1)} %add.141), channel_id=1, source_target_pairs={{0,6},{1,7},{2,4},{3,5},{4,2},{5,3},{6,0},{7,1},{8,14},{9,15},{10,... | collective-permute-start | bytes 55304 | tf_op jit(solution)/shard_map/ppermute | solution.py:88
  181.0 0.4 fusion.56
  181.4 4.3 %collective-permute-done.15 = f32[4,1152]{1,0:T(4,128)S(1)} collective-permute-done((f32[4,1152]{1,0:T(4,128)S(1)}, f32[4,1152]{1,0:T(4,128)S(1)}, u32[]{:S(2)}, u32[]{:S(2)}) %collective-permute-start.15) | collective-permute-done | bytes 18464 | tf_op jit(solution)/shard_map/ppermute | solution.py:88
  185.7 4.2 %collective-permute-start.16 = (f32[4,1152]{1,0:T(4,128)S(1)}, f32[4,1152]{1,0:T(4,128)S(1)}, u32[]{:S(2)}, u32[]{:S(2)}) collective-permute-start(f32[4,1152]{1,0:T(4,128)S(1)} %add.142), channel_id=1, source_target_pairs={{0,128},{1,129},{2,130},{3,131},{4,132},{5,133},{6,134},{7,135},{8... | collective-permute-start | bytes 55304 | tf_op jit(solution)/shard_map/ppermute | solution.py:88
  189.9 5.5 %collective-permute-done.16 = f32[4,1152]{1,0:T(4,128)S(1)} collective-permute-done((f32[4,1152]{1,0:T(4,128)S(1)}, f32[4,1152]{1,0:T(4,128)S(1)}, u32[]{:S(2)}, u32[]{:S(2)}) %collective-permute-start.16) | collective-permute-done | bytes 18464 | tf_op jit(solution)/shard_map/ppermute | solution.py:88
  195.4 5.9 %collective-permute-start.17 = (f32[4,1152]{1,0:T(4,128)S(1)}, f32[4,1152]{1,0:T(4,128)S(1)}, u32[]{:S(2)}, u32[]{:S(2)}) collective-permute-start(f32[4,1152]{1,0:T(4,128)S(1)} %add.143), channel_id=1, source_target_pairs={{0,384},{1,385},{2,386},{3,387},{4,388},{5,389},{6,390},{7,391},{8... | collective-permute-start | bytes 55304 | tf_op jit(solution)/shard_map/ppermute | solution.py:88
  201.4 0.9 fusion.46
  202.3 2.7 %collective-permute-done.17 = f32[4,1152]{1,0:T(4,128)S(1)} collective-permute-done((f32[4,1152]{1,0:T(4,128)S(1)}, f32[4,1152]{1,0:T(4,128)S(1)}, u32[]{:S(2)}, u32[]{:S(2)}) %collective-permute-start.17) | collective-permute-done | bytes 18464 | tf_op jit(solution)/shard_map/ppermute | solution.py:88
  205.0 0.6 fusion.59
  (32 shorter events, 0.3 us)
Async XLA Ops:
  0.6 27.7 %copy-start = (bf16[1,192,1152]{2,1,0:T(8,128)(2,1)S(1)}, bf16[1,192,1152]{2,1,0:T(8,128)(2,1)}, u32[]{:S(2)}) copy-start(bf16[1,192,1152]{2,1,0:T(8,128)(2,1)} %param.6) | copy-start | bytes 1327108
  6.7 49.6 %collective-permute-start.2 = (bf16[192,1152]{1,0:T(8,128)(2,1)S(1)}, bf16[192,1152]{1,0:T(8,128)(2,1)S(1)}, u32[]{:S(2)}, u32[]{:S(2)}) collective-permute-start(bf16[192,1152]{1,0:T(8,128)(2,1)S(1)} %fusion.35), channel_id=1, source_target_pairs={{0,512},{1,513},{2,514},{3,515},{4,516},{5,517},{6,518},{7,519},{8... | collective-permute-start | bytes 1327112 | tf_op jit(solution)/shard_map/ppermute | solution.py:88
  10.2 40.8 %collective-permute-start.1 = (bf16[192,1152]{1,0:T(8,128)(2,1)S(1)}, bf16[192,1152]{1,0:T(8,128)(2,1)S(1)}, u32[]{:S(2)}, u32[]{:S(2)}) collective-permute-start(bf16[192,1152]{1,0:T(8,128)(2,1)S(1)} %fusion.35), channel_id=1, source_target_pairs={{0,384},{1,129},{2,386},{3,131},{4,388},{5,133},{6,390},{7,135},{8... | collective-permute-start | bytes 1327112 | tf_op jit(solution)/shard_map/ppermute | solution.py:88
  29.5 26.8 %collective-permute-start = (bf16[192,1152]{1,0:T(8,128)(2,1)S(1)}, bf16[192,1152]{1,0:T(8,128)(2,1)S(1)}, u32[]{:S(2)}, u32[]{:S(2)}) collective-permute-start(bf16[192,1152]{1,0:T(8,128)(2,1)S(1)} %fusion.17), channel_id=1, source_target_pairs={{0,128},{1,385},{2,130},{3,387},{4,132},{5,389},{6,134},{7,391},{8... | collective-permute-start | bytes 1327112 | tf_op jit(solution)/shard_map/ppermute | solution.py:88
  51.0 10.2 %collective-permute-start.3 = (bf16[192,1152]{1,0:T(8,128)(2,1)S(1)}, bf16[192,1152]{1,0:T(8,128)(2,1)S(1)}, u32[]{:S(2)}, u32[]{:S(2)}) collective-permute-start(bf16[192,1152]{1,0:T(8,128)(2,1)S(1)} %collective-permute-done.1), channel_id=1, source_target_pairs={{0,512},{1,513},{2,514},{3,515},{4,516},{5,517},{6,518},{7,519},{8... | collective-permute-start | bytes 1327112 | tf_op jit(solution)/shard_map/ppermute | solution.py:88
  64.0 29.1 %collective-permute-start.6 = (bf16[192,1152]{1,0:T(8,128)(2,1)S(1)}, bf16[192,1152]{1,0:T(8,128)(2,1)S(1)}, u32[]{:S(2)}, u32[]{:S(2)}) collective-permute-start(bf16[192,1152]{1,0:T(8,128)(2,1)S(1)} %get-tuple-element.22), channel_id=1, source_target_pairs={{0,512},{1,513},{2,514},{3,515},{4,516},{5,517},{6,518},{7,519},{8... | collective-permute-start | bytes 1327112 | tf_op jit(solution)/shard_map/ppermute | solution.py:88
  67.5 55.3 %collective-permute-start.4 = (bf16[192,1152]{1,0:T(8,128)(2,1)S(1)}, bf16[192,1152]{1,0:T(8,128)(2,1)S(1)}, u32[]{:S(2)}, u32[]{:S(2)}) collective-permute-start(bf16[192,1152]{1,0:T(8,128)(2,1)S(1)} %slice.92), channel_id=1, source_target_pairs={{0,128},{1,385},{2,130},{3,387},{4,132},{5,389},{6,134},{7,391},{8... | collective-permute-start | bytes 1327112 | tf_op jit(solution)/shard_map/ppermute | solution.py:88
  89.7 34.4 %collective-permute-start.5 = (bf16[192,1152]{1,0:T(8,128)(2,1)S(1)}, bf16[192,1152]{1,0:T(8,128)(2,1)S(1)}, u32[]{:S(2)}, u32[]{:S(2)}) collective-permute-start(bf16[192,1152]{1,0:T(8,128)(2,1)S(1)} %get-tuple-element.21), channel_id=1, source_target_pairs={{0,512},{1,513},{2,514},{3,515},{4,516},{5,517},{6,518},{7,519},{8... | collective-permute-start | bytes 1327112 | tf_op jit(solution)/shard_map/ppermute | solution.py:88
  93.3 30.8 %collective-permute-start.7 = (bf16[192,1152]{1,0:T(8,128)(2,1)S(1)}, bf16[192,1152]{1,0:T(8,128)(2,1)S(1)}, u32[]{:S(2)}, u32[]{:S(2)}) collective-permute-start(bf16[192,1152]{1,0:T(8,128)(2,1)S(1)} %fusion.40), channel_id=1, source_target_pairs={{0,384},{1,129},{2,386},{3,131},{4,388},{5,133},{6,390},{7,135},{8... | collective-permute-start | bytes 1327112 | tf_op jit(solution)/shard_map/ppermute | solution.py:88
  123.2 1.0 copy-start.1
  125.6 4.6 %collective-permute-start.8 = (f32[4,1152]{1,0:T(4,128)S(1)}, f32[4,1152]{1,0:T(4,128)S(1)}, u32[]{:S(2)}, u32[]{:S(2)}) collective-permute-start(f32[4,1152]{1,0:T(4,128)S(1)} %pad_maximum_fusion.6), channel_id=1, source_target_pairs={{0,1},{1,0},{2,3},{3,2},{4,5},{5,4},{6,7},{7,6},{8,9},{9,8},{10,11... | collective-permute-start | bytes 55304 | tf_op jit(solution)/shard_map/ppermute | solution.py:88
  127.6 9.4 %collective-permute-start.18 = (f32[192]{0:T(256)S(1)}, f32[192]{0:T(256)S(1)}, u32[]{:S(2)}, u32[]{:S(2)}) collective-permute-start(f32[192]{0:T(256)S(1)} %slice.58), channel_id=1, source_target_pairs={{0,128},{1,385},{2,130},{3,387},{4,132},{5,389},{6,134},{7,391},{8... | collective-permute-start | bytes 2312 | tf_op jit(solution)/shard_map/ppermute | solution.py:88
  130.3 7.3 %collective-permute-start.9 = (f32[4,1152]{1,0:T(4,128)S(1)}, f32[4,1152]{1,0:T(4,128)S(1)}, u32[]{:S(2)}, u32[]{:S(2)}) collective-permute-start(f32[4,1152]{1,0:T(4,128)S(1)} %fusion.53), channel_id=1, source_target_pairs={{0,8},{1,9},{2,10},{3,11},{4,12},{5,13},{6,14},{7,15},{8,0},{9,1},... | collective-permute-start | bytes 55304 | tf_op jit(solution)/shard_map/ppermute | solution.py:88
  137.6 9.7 %collective-permute-start.10 = (f32[4,1152]{1,0:T(4,128)S(1)}, f32[4,1152]{1,0:T(4,128)S(1)}, u32[]{:S(2)}, u32[]{:S(2)}) collective-permute-start(f32[4,1152]{1,0:T(4,128)S(1)} %fusion.61), channel_id=1, source_target_pairs={{0,24},{1,25},{2,26},{3,27},{4,28},{5,29},{6,30},{7,31},{8,16},{9,... | collective-permute-start | bytes 55304 | tf_op jit(solution)/shard_map/ppermute | solution.py:88
  147.3 7.0 %collective-permute-start.11 = (f32[4,1152]{1,0:T(4,128)S(1)}, f32[4,1152]{1,0:T(4,128)S(1)}, u32[]{:S(2)}, u32[]{:S(2)}) collective-permute-start(f32[4,1152]{1,0:T(4,128)S(1)} %add.137), channel_id=1, source_target_pairs={{0,32},{1,33},{2,34},{3,35},{4,36},{5,37},{6,38},{7,39},{8,40},{9,... | collective-permute-start | bytes 55304 | tf_op jit(solution)/shard_map/ppermute | solution.py:88
  154.3 11.5 %collective-permute-start.12 = (f32[4,1152]{1,0:T(4,128)S(1)}, f32[4,1152]{1,0:T(4,128)S(1)}, u32[]{:S(2)}, u32[]{:S(2)}) collective-permute-start(f32[4,1152]{1,0:T(4,128)S(1)} %add.138), channel_id=1, source_target_pairs={{0,96},{1,97},{2,98},{3,99},{4,100},{5,101},{6,102},{7,103},{8,104... | collective-permute-start | bytes 55304 | tf_op jit(solution)/shard_map/ppermute | solution.py:88
  165.7 5.6 %collective-permute-start.13 = (f32[4,1152]{1,0:T(4,128)S(1)}, f32[4,1152]{1,0:T(4,128)S(1)}, u32[]{:S(2)}, u32[]{:S(2)}) collective-permute-start(f32[4,1152]{1,0:T(4,128)S(1)} %add.139), channel_id=1, source_target_pairs={{0,512},{1,513},{2,514},{3,515},{4,516},{5,517},{6,518},{7,519},{8... | collective-permute-start | bytes 55304 | tf_op jit(solution)/shard_map/ppermute | solution.py:88
  171.4 6.5 %collective-permute-start.14 = (f32[4,1152]{1,0:T(4,128)S(1)}, f32[4,1152]{1,0:T(4,128)S(1)}, u32[]{:S(2)}, u32[]{:S(2)}) collective-permute-start(f32[4,1152]{1,0:T(4,128)S(1)} %add.140), channel_id=1, source_target_pairs={{0,2},{1,3},{2,0},{3,1},{4,6},{5,7},{6,4},{7,5},{8,10},{9,11},{10,... | collective-permute-start | bytes 55304 | tf_op jit(solution)/shard_map/ppermute | solution.py:88
  177.9 7.8 %collective-permute-start.15 = (f32[4,1152]{1,0:T(4,128)S(1)}, f32[4,1152]{1,0:T(4,128)S(1)}, u32[]{:S(2)}, u32[]{:S(2)}) collective-permute-start(f32[4,1152]{1,0:T(4,128)S(1)} %add.141), channel_id=1, source_target_pairs={{0,6},{1,7},{2,4},{3,5},{4,2},{5,3},{6,0},{7,1},{8,14},{9,15},{10,... | collective-permute-start | bytes 55304 | tf_op jit(solution)/shard_map/ppermute | solution.py:88
  185.7 9.7 %collective-permute-start.16 = (f32[4,1152]{1,0:T(4,128)S(1)}, f32[4,1152]{1,0:T(4,128)S(1)}, u32[]{:S(2)}, u32[]{:S(2)}) collective-permute-start(f32[4,1152]{1,0:T(4,128)S(1)} %add.142), channel_id=1, source_target_pairs={{0,128},{1,129},{2,130},{3,131},{4,132},{5,133},{6,134},{7,135},{8... | collective-permute-start | bytes 55304 | tf_op jit(solution)/shard_map/ppermute | solution.py:88
  195.4 9.6 %collective-permute-start.17 = (f32[4,1152]{1,0:T(4,128)S(1)}, f32[4,1152]{1,0:T(4,128)S(1)}, u32[]{:S(2)}, u32[]{:S(2)}) collective-permute-start(f32[4,1152]{1,0:T(4,128)S(1)} %add.143), channel_id=1, source_target_pairs={{0,384},{1,385},{2,386},{3,387},{4,388},{5,389},{6,390},{7,391},{8... | collective-permute-start | bytes 55304 | tf_op jit(solution)/shard_map/ppermute | solution.py:88

commit v2 on v1

v2 whole, which is shorter than its diff:
```python
import functools

import jax
import jax.numpy as jnp
from jax import lax
from jax.experimental import pallas as pl
from jax.experimental.pallas import tpu as pltpu
from jax.sharding import PartitionSpec as P

AXES = ("img", "dp")
RING = 4
X_CHIPS = 4
Z_BLOCK = 4
Y_HIGH = 4

VMEM_LIMIT = 60 << 20
TILE_VMEM_LIMIT = 24 << 20
ROW_BLOCK = 16
UNROLL = 4
EPS = 1e-06
EXTRA = 16
LANES = 256
NT = (((1,), (1,)), ((), ()))
TN = (((0,), (0,)), ((), ()))


def to_lanes(column):
    count = column.shape[0]
    on = lax.broadcasted_iota(jnp.int32, (count, count), 0) == lax.broadcasted_iota(
        jnp.int32, (count, count), 1
    )
    return jnp.sum(jnp.where(on, column, 0.0), axis=0, keepdims=True)


def to_rows(line):
    count = line.shape[1]
    on = lax.broadcasted_iota(jnp.int32, (count, count), 0) == lax.broadcasted_iota(
        jnp.int32, (count, count), 1
    )
    return jnp.sum(jnp.where(on, line, 0.0), axis=1, keepdims=True)


def put_line(ref, line):
    count = line.shape[1]
    rows = ref.shape[0] - EXTRA
    ref[rows:, :] = jnp.zeros((EXTRA, ref.shape[1]), ref.dtype)
    for term in range(3):
        piece = line.astype(jnp.bfloat16)
        line = line - piece.astype(jnp.float32)
        ref[rows:, term * LANES : term * LANES + count] = jnp.broadcast_to(piece, (EXTRA, count))


def get_line(block, count):
    terms = [
        block[:1, term * LANES : term * LANES + count].astype(jnp.float32) for term in range(3)
    ]
    return terms[0] + (terms[1] + terms[2])


def norm_rows(feats, gain, shift):
    center = jnp.mean(feats, axis=-1, keepdims=True)
    offset = feats - center
    spread = jnp.mean(offset * offset, axis=-1, keepdims=True)
    rstd = lax.rsqrt(spread + EPS)
    normed = offset * rstd
    unnormed = normed * gain + shift
    inverse = lax.rsqrt(jnp.sum(unnormed * unnormed, axis=-1, keepdims=True) + EPS)
    return normed, rstd, unnormed, inverse


def forward_kernel(image_ref, text_ref, gains_ref, shifts_ref, image_emb_ref, text_emb_ref, keep):
    for tower, (feats_ref, emb_ref) in enumerate(
        ((image_ref, image_emb_ref), (text_ref, text_emb_ref))
    ):
        gain = gains_ref[tower : tower + 1, :]
        shift = shifts_ref[tower : tower + 1, :]

        @pl.loop(0, feats_ref.shape[0] // ROW_BLOCK, unroll=UNROLL)
        def _(step):
            rows = pl.ds(pl.multiple_of(step * ROW_BLOCK, ROW_BLOCK), ROW_BLOCK)
            feats = feats_ref[rows, :].astype(jnp.float32)
            _, _, unnormed, inverse = norm_rows(feats, gain, shift)
            emb_ref[rows, :] = (unnormed * inverse).astype(jnp.bfloat16)
            keep[rows, :] = jnp.broadcast_to(inverse, (ROW_BLOCK, 128))

        put_line(emb_ref, to_lanes(keep[:, :1]))


def forward_norms(image_feats, text_feats, gains, shifts):
    rows, width = image_feats.shape
    emb = jax.ShapeDtypeStruct((rows + EXTRA, width), jnp.bfloat16)
    return pl.pallas_call(
        forward_kernel,
        out_shape=(emb, emb),
        scratch_shapes=[pltpu.VMEM((rows, 128), jnp.float32)],
        compiler_params=pltpu.CompilerParams(vmem_limit_bytes=VMEM_LIMIT),
        cost_estimate=pl.CostEstimate(
            flops=40 * rows * width, bytes_accessed=8 * rows * width, transcendentals=0
        ),
        name="forward_norms",
    )(image_feats, text_feats, gains, shifts)


def add_sums(units, parts, inverses):
    along = jnp.sum(units * parts, axis=-1, keepdims=True)
    pulled = parts - units * along
    return (
        jnp.sum(units * pulled, axis=0, keepdims=True),
        jnp.sum(inverses * pulled, axis=0, keepdims=True),
    )


def tile_kernel(final, scalars_ref, gains_ref, shifts_ref, *refs):
    blocks = refs[:4]
    if final:
        image_before, loss_before, sums_before = refs[4:7]
        text_a_ref, text_b_ref, image_ref, back_ref, loss_ref, sums_ref = refs[7:13]
    else:
        text_a_ref, text_b_ref, image_ref, loss_ref, sums_ref = refs[4:9]
    images, texts, coeff = refs[-3:]
    rows = loss_ref.shape[1]
    for at in range(2):
        own = slice(at * rows, (at + 1) * rows)
        images[own, :] = blocks[at][:rows, :]
        texts[own, :] = blocks[2 + at][:rows, :]
    losses = []
    for at in range(2):
        own = slice(at * rows, (at + 1) * rows)
        logits = lax.dot_general(
            images[own, :], texts[...], NT, preferred_element_type=jnp.float32
        )
        logits = scalars_ref[0] * logits + scalars_ref[1]
        diagonal = at == 0 and not final
        if diagonal:
            row_at = lax.broadcasted_iota(jnp.int32, logits.shape, 0)
            column_at = lax.broadcasted_iota(jnp.int32, logits.shape, 1)
            signs = jnp.where(row_at == column_at, -1.0, 1.0)
            logits = signs * logits
        small = jnp.exp(-jnp.abs(logits))
        terms = jnp.maximum(logits, 0.0) + jnp.log1p(small)
        slopes = jnp.where(logits >= 0.0, 1.0, small) / (1.0 + small)
        if diagonal:
            slopes = signs * slopes
        coeff[own, :] = slopes.astype(jnp.bfloat16)
        losses.append(to_lanes(jnp.sum(terms, axis=1, keepdims=True)))
    if final:
        loss_ref[...] = loss_before[:1, :] + losses[0]
        put_line(back_ref, loss_before[1:2, :] + losses[1])
    else:
        for at in range(2):
            loss_ref[at : at + 1, :] = losses[at]

    def inverses(at):
        return to_rows(get_line(blocks[at][rows:, :], rows))

    def finish(tower, unit_sum, shift_sum):
        gain = gains_ref[tower : tower + 1, :]
        shift = shifts_ref[tower : tower + 1, :]
        sums_ref[tower : tower + 1, :] = scalars_ref[0] * (unit_sum - shift * shift_sum) / gain
        sums_ref[2 + tower : 3 + tower, :] = scalars_ref[0] * shift_sum

    unit_sum, shift_sum = 0.0, 0.0
    if final:
        unit_sum, shift_sum = sums_before[:1, :], sums_before[1:2, :]
    for at, part_ref in ((1, text_b_ref), (0, text_a_ref)):
        own = slice(at * rows, (at + 1) * rows)
        part = lax.dot_general(
            coeff[:, own], images[...], TN, preferred_element_type=jnp.float32
        )
        part_ref[...] = part.astype(part_ref.dtype)
        unit_add, shift_add = add_sums(texts[own, :].astype(jnp.float32), part, inverses(2 + at))
        unit_sum, shift_sum = unit_sum + unit_add, shift_sum + shift_add
    if not final:
        sums_ref[:1, :] = unit_sum
        sums_ref[1:2, :] = shift_sum
        image_ref[...] = jnp.dot(coeff[...], texts[...], preferred_element_type=jnp.float32)
        return
    finish(1, unit_sum, shift_sum)
    unit_sum, shift_sum = 0.0, 0.0
    for at in range(2):
        own = slice(at * rows, (at + 1) * rows)
        part = image_before[own, :] + jnp.dot(
            coeff[own, :], texts[...], preferred_element_type=jnp.float32
        )
        if at == 0:
            image_ref[...] = part
        else:
            back_ref[:rows, :] = part.astype(jnp.bfloat16)
        unit_add, shift_add = add_sums(images[own, :].astype(jnp.float32), part, inverses(at))
        unit_sum, shift_sum = unit_sum + unit_add, shift_sum + shift_add
    finish(0, unit_sum, shift_sum)


def tile(scalars, gains, shifts, images, texts, before=()):
    rows, width = images[0].shape[0] - EXTRA, images[0].shape[1]
    final = len(before) > 0
    whole = pl.BlockSpec(memory_space=pltpu.VMEM)

    def wide(count, kind):
        return jax.ShapeDtypeStruct((count, width), kind)

    if final:
        outs = [wide(rows, jnp.bfloat16)] * 2
        outs += [wide(rows, jnp.float32), wide(rows + EXTRA, jnp.bfloat16)]
        outs += [jax.ShapeDtypeStruct((1, rows), jnp.float32), wide(4, jnp.float32)]
    else:
        outs = [wide(rows, jnp.float32)] * 2 + [wide(2 * rows, jnp.float32)]
        outs += [jax.ShapeDtypeStruct((2, rows), jnp.float32), wide(2, jnp.float32)]
    return pl.pallas_call(
        functools.partial(tile_kernel, final),
        out_shape=tuple(outs),
        in_specs=[pl.BlockSpec(memory_space=pltpu.SMEM)] + [whole] * (6 + len(before)),
        out_specs=(whole,) * len(outs),
        scratch_shapes=[
            pltpu.VMEM((2 * rows, width), jnp.bfloat16),
            pltpu.VMEM((2 * rows, width), jnp.bfloat16),
            pltpu.VMEM((2 * rows, 2 * rows), jnp.bfloat16),
        ],
        compiler_params=pltpu.CompilerParams(vmem_limit_bytes=TILE_VMEM_LIMIT),
        cost_estimate=pl.CostEstimate(
            flops=24 * rows * rows * width,
            bytes_accessed=24 * rows * width,
            transcendentals=12 * rows * rows,
        ),
        name="last_tile" if final else "first_tile",
    )(scalars, gains, shifts, *images, *texts, *before)


def backward_kernel(feats_ref, gain_ref, shift_ref, scale_ref, *refs):
    *part_refs, grad_ref = refs

    @pl.loop(0, feats_ref.shape[0] // ROW_BLOCK, unroll=UNROLL)
    def _(step):
        rows = pl.ds(pl.multiple_of(step * ROW_BLOCK, ROW_BLOCK), ROW_BLOCK)
        feats = feats_ref[rows, :].astype(jnp.float32)
        gain = gain_ref[...]
        normed, rstd, unnormed, inverse = norm_rows(feats, gain, shift_ref[...])
        unit = unnormed * inverse
        pulled = part_refs[0][rows, :].astype(jnp.float32)
        for part_ref in part_refs[1:]:
            pulled = pulled + part_ref[rows, :].astype(jnp.float32)
        pulled = pulled * scale_ref[0]
        along = jnp.sum(unit * pulled, axis=-1, keepdims=True)
        pulled = inverse * (pulled - unit * along) * gain
        pulled = pulled - normed * jnp.mean(pulled * normed, axis=-1, keepdims=True)
        pulled = rstd * (pulled - jnp.mean(pulled, axis=-1, keepdims=True))
        grad_ref[rows, :] = pulled.astype(jnp.bfloat16)


def backward_norm(feats, gain, shift, scale, parts):
    rows, width = feats.shape
    whole = pl.BlockSpec(memory_space=pltpu.VMEM)
    return pl.pallas_call(
        backward_kernel,
        out_shape=jax.ShapeDtypeStruct((rows, width), jnp.bfloat16),
        in_specs=[whole] * 3 + [pl.BlockSpec(memory_space=pltpu.SMEM)] + [whole] * len(parts),
        out_specs=whole,
        compiler_params=pltpu.CompilerParams(vmem_limit_bytes=VMEM_LIMIT),
        cost_estimate=pl.CostEstimate(
            flops=40 * rows * width, bytes_accessed=12 * rows * width, transcendentals=0
        ),
        name="backward_norm",
    )(feats, gain, shift, scale, *parts)


def near(place):
    return place ^ 1


def far(place):
    return RING - 1 - place


class Routes:
    def __init__(self, sizes):
        self.sizes = sizes
        y_lo, z_hi, z_lo, x, y_hi, core = sizes
        self.count = y_lo * z_hi * z_lo * x * y_hi * core

    def split(self, index):
        place = []
        for size in reversed(self.sizes):
            place.append(index % size)
            index //= size
        return place[::-1]

    def join(self, place):
        index = 0
        for size, at in zip(self.sizes, place):
            index = index * size + at
        return index

    def pairs(self, move):
        out = []
        for index in range(self.count):
            place = self.split(index)
            out.append((index, self.join(move(list(place)))))
        return out

    def along(self, axis, step):
        def move(place):
            place[axis] = step(place[axis])
            return place

        return self.pairs(move)

    def across_y(self):
        return self.along(0, near)

    def towers(self):
        def text(place):
            place[1] = far(place[1]) if place[5] == 0 else near(place[1])
            return place

        def image(place):
            place[1] = near(place[1]) if place[5] == 0 else far(place[1])
            return place

        return self.pairs(text), self.pairs(image)

    def ring(self, high, low):
        size = self.sizes[low] * (1 if high is None else self.sizes[high])
        steps = []
        reach = -1
        while 2 ** len(steps) < size:

            def move(place, reach=reach):
                at = place[low] + (0 if high is None else place[high] * self.sizes[low])
                at = (at + (reach if at % 2 else -reach)) % size
                place[low] = at % self.sizes[low]
                if high is not None:
                    place[high] = at // self.sizes[low]
                return place

            steps.append(self.pairs(move))
            reach = -2 * reach - 1
        return steps


def send(value, pairs):
    return lax.ppermute(value, AXES, pairs)


def sum_over(value, steps, turns):
    def one(carry):
        turn, value = carry
        for pairs in steps:
            value = value + send(value, pairs)
        return turn + 1, value

    return lax.while_loop(lambda carry: carry[0] < turns, one, (jnp.int32(0), value))[1]


def make_body(routes):
    text_pairs, image_pairs = routes.towers()
    y_pairs = routes.across_y()
    z_steps = routes.ring(1, 2)
    flat_steps = [routes.along(5, near), *routes.ring(None, 3), *routes.ring(4, 0)]
    early_steps, middle_steps = flat_steps[:2], flat_steps[2:]
    group_rows = 2 * RING

    def body(image_feats, text_feats, gains, shifts, log_scale, logit_bias):
        scale = jnp.exp(log_scale)
        scalars = jnp.concatenate([scale, logit_bias])
        turns = jnp.where(log_scale[0] == log_scale[0], 1, 0)
        image, text = forward_norms(image_feats[0], text_feats[0], gains, shifts)
        rows = image_feats.shape[1]

        text_z = send(text, text_pairs)
        image_z = send(image, image_pairs)
        text_y = send(text, y_pairs)
        text_zy = send(text_z, y_pairs)
        images = [image, image_z]
        text_part, text_z_part, *before = tile(scalars, gains, shifts, images, [text, text_z])
        text_y_part, text_zy_part, image_part, image_z_part, loss_own, sums = tile(
            scalars, gains, shifts, images, [text_y, text_zy], before
        )

        text_zy_back = send(text_zy_part, y_pairs)
        image_back = send(image_z_part, image_pairs)
        sums = sum_over(sums, early_steps, turns)
        sums, text_zy_back, text_y_part = lax.optimization_barrier(
            (sums, text_zy_back, text_y_part)
        )
        text_z_sum = text_z_part + text_zy_back.astype(jnp.float32)
        text_z_back = send(text_z_sum.astype(jnp.bfloat16), text_pairs)
        text_y_back = send(text_y_part, y_pairs)
        sums = sum_over(sums, middle_steps, turns)
        sums, image_back = lax.optimization_barrier((sums, image_back))
        image_grad = backward_norm(
            image_feats[0], gains[:1], shifts[:1], scale, [image_part, image_back]
        )
        for pairs in z_steps:
            sums = sums + send(sums, pairs)
        text_grad = backward_norm(
            text_feats[0],
            gains[1:],
            shifts[1:],
            scale,
            [text_part, text_y_back, text_z_back],
        )

        row_mean = (loss_own + get_line(image_back[rows:], rows)) / (group_rows * rows)
        return (image_grad[None], text_grad[None], sums[:2], sums[2:], row_mean)

    return body


def build(mesh, sizes):
    placed = (P("dp", "img", None), P("dp", "img", None), P(), P(), P(), P())
    return jax.shard_map(
        make_body(Routes(sizes)),
        mesh=mesh,
        in_specs=placed,
        out_specs=(P("dp", "img", None), P("dp", "img", None), P(), P(), P("dp", "img")),
        check_vma=False,
    )


def solution(mesh):
    y_high, cores = Y_HIGH, mesh.shape["dp"] // Y_HIGH
    y_low = mesh.shape["img"] // (RING * Z_BLOCK * X_CHIPS)
    return build(mesh, (y_low, RING, Z_BLOCK, X_CHIPS, y_high, cores))
```

time: 208 us -> 178 us (0.86)
  the two profiles are of different devices: /device:TPU:6 before, /device:TPU:64 now
where the time goes in v2:
time: 178 us; the launch traced here: 177 us
  starting transfers between devices  87.7 us (49%)
  waiting for transfers between devices  60.1 us (34%)
  Pallas kernels  18.9 us (11%)
  local copies, waits for them, and re-layouts  7.44 us (4%)
  between operations  2.17 us (1%)
    ppermute x18, starting transfers between devices, send(): return lax.ppermute(value, AXES, pairs)  87.7 us
    ppermute x18, waiting for transfers between devices, send(): return lax.ppermute(value, AXES, pairs)  60.1 us
    pallas_call x2, Pallas kernels, backward_norm(): pl.pallas_call(backward_kernel, out_shape=jax.ShapeDtypeStruct((rows, wid...  8.16 us
    pallas_call x2, Pallas kernels, tile(): pl.pallas_call(functools.partial(tile_kernel, final), out_shape=tuple(out...  6.61 us
    unnamed x22, local copies, waits for them, and re-layouts  6.21 us
    pallas_call x1, Pallas kernels, forward_norms(): pl.pallas_call(forward_kernel, out_shape=(emb, emb), scratch_shapes=[pltp...  4.13 us
  transfers between devices with their start and end apart: 18, of which 11 were waited for; matrix products, arithmetic and copies ran while one was open for 1% of the time, Pallas kernels for 4%

profile of v2, /device:TPU:64, one launch (start us, length us, event | category | flops | bytes accessed | tf_op | source)
XLA Modules:
  0.0 177.1 jit_solution(6360679810179415279)
XLA Ops:
  0.6 4.1 %forward_norms.1 = (bf16[208,1152]{1,0:T(8,128)(2,1)}, bf16[208,1152]{1,0:T(8,128)(2,1)}) custom-call(bf16[192,1152]{1,0:T(8,128)(2,1)} %bitcast.5, bf16[192,1152]{1,0:T(8,128)(2,1)} %bitcast.7, f32[2,1152]{1,0:T(2,128)} %gains_ref.5, f32[2,1152]{1,0:T(2,128)} %shifts_ref.5), custom_call_target="tpu_custom_call" | custom-call | flops 8847360 | bytes 1769472 | tf_op jit(solution)/shard_map/forward_norms/pallas_call | solution.py:92
  4.8 17.3 %collective-permute-start.8 = (bf16[208,1152]{1,0:T(8,128)(2,1)}, bf16[208,1152]{1,0:T(8,128)(2,1)S(1)}, u32[]{:S(2)}, u32[]{:S(2)}) collective-permute-start(bf16[208,1152]{1,0:T(8,128)(2,1)} %get-tuple-element.60.refs_2_), channel_id=1, source_target_pairs={{0,384},{1,129},{2,386},{3,131},{4,388},{5,133},{6,390},{7,135},{8... | collective-permute-start | bytes 1437704 | tf_op jit(solution)/shard_map/ppermute | solution.py:341
  22.0 3.6 %collective-permute-start.6 = (bf16[208,1152]{1,0:T(8,128)(2,1)}, bf16[208,1152]{1,0:T(8,128)(2,1)S(1)}, u32[]{:S(2)}, u32[]{:S(2)}) collective-permute-start(bf16[208,1152]{1,0:T(8,128)(2,1)} %get-tuple-element.59.refs_0_), channel_id=1, source_target_pairs={{0,128},{1,385},{2,130},{3,387},{4,132},{5,389},{6,134},{7,391},{8... | collective-permute-start | bytes 1437704 | tf_op jit(solution)/shard_map/ppermute | solution.py:341
  25.7 3.5 %collective-permute-start.7 = (bf16[208,1152]{1,0:T(8,128)(2,1)}, bf16[208,1152]{1,0:T(8,128)(2,1)S(1)}, u32[]{:S(2)}, u32[]{:S(2)}) collective-permute-start(bf16[208,1152]{1,0:T(8,128)(2,1)} %get-tuple-element.60.refs_2_), channel_id=1, source_target_pairs={{0,512},{1,513},{2,514},{3,515},{4,516},{5,517},{6,518},{7,519},{8... | collective-permute-start | bytes 1437704 | tf_op jit(solution)/shard_map/ppermute | solution.py:341
  29.2 32.4 %collective-permute-done.8.refs_3_ = bf16[208,1152]{1,0:T(8,128)(2,1)S(1)} collective-permute-done((bf16[208,1152]{1,0:T(8,128)(2,1)}, bf16[208,1152]{1,0:T(8,128)(2,1)S(1)}, u32[]{:S(2)}, u32[]{:S(2)}) %collective-permute-start.8) | collective-permute-done | bytes 479264 | tf_op jit(solution)/shard_map/ppermute | solution.py:341
  61.6 3.5 %collective-permute-start.9 = (bf16[208,1152]{1,0:T(8,128)(2,1)S(1)}, bf16[208,1152]{1,0:T(8,128)(2,1)S(1)}, u32[]{:S(2)}, u32[]{:S(2)}) collective-permute-start(bf16[208,1152]{1,0:T(8,128)(2,1)S(1)} %collective-permute-done.8.refs_3_), channel_id=1, source_target_pairs={{0,512},{1,513},{2,514},{3,515},{4,516},{5,517},{6,518},{7,519},{8... | collective-permute-start | bytes 1437704 | tf_op jit(solution)/shard_map/ppermute | solution.py:341
  66.4 0.1 pad_maximum_fusion.scalars_ref
  66.5 0.0 collective-permute-done.6.refs_1_
  66.5 0.0 copy-start.2
  66.5 0.7 copy-done.2
  67.2 0.0 copy-start.4
  67.2 0.7 copy-done.4
  67.9 1.0 copy-done.6
  68.9 1.0 copy-done.7
  70.0 3.0 %first_tile.1 = (f32[192,1152]{1,0:T(8,128)S(1)}, f32[192,1152]{1,0:T(8,128)S(1)}, f32[384,1152]{1,0:T(8,128)S(1)}, f32[2,192]{1,0:T(2,128)S(1)}, f32[2,1152]{1,0:T(2,128)S(1)}) custom-call(f32[2]{0:T(128)S(1)} %pad_maximum_fusion.scalars_ref, f32[2,1152]{1,0:T(2,128)S(1)} %copy-done.4, f32[2,1152]{1,0:T(2,128)S(1)} %copy-done.2, ...), custom_call_target="tpu_custom_call" | custom-call | flops 1019215872 | bytes 5308416 | tf_op jit(solution)/shard_map/first_tile/pallas_call | solution.py:209
  73.0 0.0 copy-start.1
  73.0 0.9 copy-done.1
  73.9 0.0 collective-permute-done.7.refs_2_
  73.9 0.0 collective-permute-done.9.refs_3_
  73.9 3.6 %last_tile.1 = (bf16[192,1152]{1,0:T(8,128)(2,1)S(1)}, bf16[192,1152]{1,0:T(8,128)(2,1)S(1)}, f32[192,1152]{1,0:T(8,128)S(1)}, bf16[208,1152]{1,0:T(8,128)(2,1)S...) custom-call(f32[2]{0:T(128)S(1)} %pad_maximum_fusion.scalars_ref, f32[2,1152]{1,0:T(2,128)S(1)} %copy-done.4, ...), custom_call_target="tpu_custom_call" | custom-call | flops 1019215872 | bytes 5308416 | tf_op jit(solution)/shard_map/last_tile/pallas_call | solution.py:209
  77.5 0.0 copy-start
  77.5 0.9 copy-done
  78.5 2.0 %collective-permute-start.11 = (bf16[208,1152]{1,0:T(8,128)(2,1)S(1)}, bf16[208,1152]{1,0:T(8,128)(2,1)S(1)}, u32[]{:S(2)}, u32[]{:S(2)}) collective-permute-start(bf16[208,1152]{1,0:T(8,128)(2,1)S(1)} %get-tuple-element.71), channel_id=1, source_target_pairs={{0,128},{1,385},{2,130},{3,387},{4,132},{5,389},{6,134},{7,391},{8... | collective-permute-start | bytes 1437704 | tf_op jit(solution)/shard_map/ppermute | solution.py:341
  80.5 2.3 %collective-permute-start.10 = (bf16[192,1152]{1,0:T(8,128)(2,1)S(1)}, bf16[192,1152]{1,0:T(8,128)(2,1)S(1)}, u32[]{:S(2)}, u32[]{:S(2)}) collective-permute-start(bf16[192,1152]{1,0:T(8,128)(2,1)S(1)} %get-tuple-element.67), channel_id=1, source_target_pairs={{0,512},{1,513},{2,514},{3,515},{4,516},{5,517},{6,518},{7,519},{8... | collective-permute-start | bytes 1327112 | tf_op jit(solution)/shard_map/ppermute | solution.py:341
  82.8 11.7 %while.20 = (s32[]{:T(128)}, f32[4,1152]{1,0:T(4,128)S(1)}, s32[]{:T(128)}, s32[]{:T(128)}) while((s32[]{:T(128)}, f32[4,1152]{1,0:T(4,128)S(1)}, s32[]{:T(128)}, s32[]{:T(128)}) %tuple.44), condition=%wide.region_1.2_spmd, body=%wide.region_0.1_spmd.sunk | while | flops 9218 | bytes 258181 | solution.py:351
  82.9 5.2 %collective-permute-start = (f32[4,1152]{1,0:T(4,128)S(1)}, f32[4,1152]{1,0:T(4,128)S(1)}, u32[]{:S(2)}, u32[]{:S(2)}) collective-permute-start(f32[4,1152]{1,0:T(4,128)S(1)} %get-tuple-element.144), channel_id=1, source_target_pairs={{0,1},{1,0},{2,3},{3,2},{4,5},{5,4},{6,7},{7,6},{8,9},{9,8},{10,11... | collective-permute-start | bytes 55304 | tf_op jit(solution)/shard_map/while/body/ppermute | solution.py:341
  88.1 0.8 collective-permute-done
  88.9 3.4 %collective-permute-start.1 = (f32[4,1152]{1,0:T(4,128)S(1)}, f32[4,1152]{1,0:T(4,128)S(1)}, u32[]{:S(2)}, u32[]{:S(2)}) collective-permute-start(f32[4,1152]{1,0:T(4,128)S(1)} %add.69), channel_id=1, source_target_pairs={{0,8},{1,9},{2,10},{3,11},{4,12},{5,13},{6,14},{7,15},{8,0},{9,1},... | collective-permute-start | bytes 55304 | tf_op jit(solution)/shard_map/while/body/ppermute | solution.py:341
  92.3 2.3 %collective-permute-done.1 = f32[4,1152]{1,0:T(4,128)S(1)} collective-permute-done((f32[4,1152]{1,0:T(4,128)S(1)}, f32[4,1152]{1,0:T(4,128)S(1)}, u32[]{:S(2)}, u32[]{:S(2)}) %collective-permute-start.1) | collective-permute-done | bytes 18464 | tf_op jit(solution)/shard_map/while/body/ppermute | solution.py:341
  94.6 0.0 collective-permute-done.10
  94.6 27.0 %while.21 = (s32[]{:T(128)}, f32[4,1152]{1,0:T(4,128)S(1)}, s32[]{:T(128)}, s32[]{:T(128)}) while((s32[]{:T(128)}, f32[4,1152]{1,0:T(4,128)S(1)}, s32[]{:T(128)}, s32[]{:T(128)}) %tuple.47), condition=%wide.region_3.4_spmd, body=%wide.region_2.3_spmd.sunk | while | flops 18434 | bytes 516309 | solution.py:351
  94.6 4.6 %collective-permute-start.2 = (f32[4,1152]{1,0:T(4,128)S(1)}, f32[4,1152]{1,0:T(4,128)S(1)}, u32[]{:S(2)}, u32[]{:S(2)}) collective-permute-start(f32[4,1152]{1,0:T(4,128)S(1)} %get-tuple-element.156), channel_id=1, source_target_pairs={{0,24},{1,25},{2,26},{3,27},{4,28},{5,29},{6,30},{7,31},{8,16},{9,... | collective-permute-start | bytes 55304 | tf_op jit(solution)/shard_map/while/body/ppermute | solution.py:341
  99.2 2.4 %collective-permute-done.2 = f32[4,1152]{1,0:T(4,128)S(1)} collective-permute-done((f32[4,1152]{1,0:T(4,128)S(1)}, f32[4,1152]{1,0:T(4,128)S(1)}, u32[]{:S(2)}, u32[]{:S(2)}) %collective-permute-start.2) | collective-permute-done | bytes 18464 | tf_op jit(solution)/shard_map/while/body/ppermute | solution.py:341
  101.6 2.3 %collective-permute-start.3 = (f32[4,1152]{1,0:T(4,128)S(1)}, f32[4,1152]{1,0:T(4,128)S(1)}, u32[]{:S(2)}, u32[]{:S(2)}) collective-permute-start(f32[4,1152]{1,0:T(4,128)S(1)} %add.72), channel_id=1, source_target_pairs={{0,512},{1,513},{2,514},{3,515},{4,516},{5,517},{6,518},{7,519},{8... | collective-permute-start | bytes 55304 | tf_op jit(solution)/shard_map/while/body/ppermute | solution.py:341
  104.0 3.3 %collective-permute-done.3 = f32[4,1152]{1,0:T(4,128)S(1)} collective-permute-done((f32[4,1152]{1,0:T(4,128)S(1)}, f32[4,1152]{1,0:T(4,128)S(1)}, u32[]{:S(2)}, u32[]{:S(2)}) %collective-permute-start.3) | collective-permute-done | bytes 18464 | tf_op jit(solution)/shard_map/while/body/ppermute | solution.py:341
  107.3 5.1 %collective-permute-start.4 = (f32[4,1152]{1,0:T(4,128)S(1)}, f32[4,1152]{1,0:T(4,128)S(1)}, u32[]{:S(2)}, u32[]{:S(2)}) collective-permute-start(f32[4,1152]{1,0:T(4,128)S(1)} %add.73), channel_id=1, source_target_pairs={{0,518},{1,519},{2,512},{3,513},{4,514},{5,515},{6,516},{7,517},{8... | collective-permute-start | bytes 55304 | tf_op jit(solution)/shard_map/while/body/ppermute | solution.py:341
  112.4 1.7 collective-permute-done.4
  114.2 4.3 %collective-permute-start.5 = (f32[4,1152]{1,0:T(4,128)S(1)}, f32[4,1152]{1,0:T(4,128)S(1)}, u32[]{:S(2)}, u32[]{:S(2)}) collective-permute-start(f32[4,1152]{1,0:T(4,128)S(1)} %add.74), channel_id=1, source_target_pairs={{0,514},{1,515},{2,516},{3,517},{4,518},{5,519},{6,512},{7,513},{8... | collective-permute-start | bytes 55304 | tf_op jit(solution)/shard_map/while/body/ppermute | solution.py:341
  118.5 3.1 %collective-permute-done.5 = f32[4,1152]{1,0:T(4,128)S(1)} collective-permute-done((f32[4,1152]{1,0:T(4,128)S(1)}, f32[4,1152]{1,0:T(4,128)S(1)}, u32[]{:S(2)}, u32[]{:S(2)}) %collective-permute-start.5) | collective-permute-done | bytes 18464 | tf_op jit(solution)/shard_map/while/body/ppermute | solution.py:341
  121.6 0.0 collective-permute-done.11.refs_1_
  121.6 0.0 copy-start.8
  121.6 6.6 %collective-permute-start.14 = (f32[4,1152]{1,0:T(4,128)S(1)}, f32[4,1152]{1,0:T(4,128)S(1)}, u32[]{:S(2)}, u32[]{:S(2)}) collective-permute-start(f32[4,1152]{1,0:T(4,128)S(1)} %get-tuple-element.77), channel_id=1, source_target_pairs={{0,32},{1,33},{2,34},{3,35},{4,36},{5,37},{6,38},{7,39},{8,40},{9,... | collective-permute-start | bytes 55304 | tf_op jit(solution)/shard_map/ppermute | solution.py:341
  128.2 1.7 collective-permute-done.14
  129.9 4.1 %collective-permute-start.15 = (f32[4,1152]{1,0:T(4,128)S(1)}, f32[4,1152]{1,0:T(4,128)S(1)}, u32[]{:S(2)}, u32[]{:S(2)}) collective-permute-start(f32[4,1152]{1,0:T(4,128)S(1)} %add.49), channel_id=1, source_target_pairs={{0,480},{1,481},{2,482},{3,483},{4,484},{5,485},{6,486},{7,487},{8... | collective-permute-start | bytes 55304 | tf_op jit(solution)/shard_map/ppermute | solution.py:341
  134.1 0.0 copy-done.3
  134.1 0.0 copy-done.5
  134.1 0.6 fusion.1
  134.7 1.1 collective-permute-done.15
  135.8 7.3 %collective-permute-start.16 = (f32[4,1152]{1,0:T(4,128)S(1)}, f32[4,1152]{1,0:T(4,128)S(1)}, u32[]{:S(2)}, u32[]{:S(2)}) collective-permute-start(f32[4,1152]{1,0:T(4,128)S(1)} %add.50), channel_id=1, source_target_pairs={{0,96},{1,97},{2,98},{3,99},{4,100},{5,101},{6,102},{7,103},{8,104... | collective-permute-start | bytes 55304 | tf_op jit(solution)/shard_map/ppermute | solution.py:341
  143.1 0.1 add_convert_fusion
  143.2 1.9 %collective-permute-start.13 = (bf16[192,1152]{1,0:T(8,128)(2,1)S(1)}, bf16[192,1152]{1,0:T(8,128)(2,1)S(1)}, u32[]{:S(2)}, u32[]{:S(2)}) collective-permute-start(bf16[192,1152]{1,0:T(8,128)(2,1)S(1)} %add_convert_fusion), channel_id=1, source_target_pairs={{0,384},{1,129},{2,386},{3,131},{4,388},{5,133},{6,390},{7,135},{8... | collective-permute-start | bytes 1327112 | tf_op jit(solution)/shard_map/ppermute | solution.py:341
  145.2 3.2 %collective-permute-start.12 = (bf16[192,1152]{1,0:T(8,128)(2,1)S(1)}, bf16[192,1152]{1,0:T(8,128)(2,1)S(1)}, u32[]{:S(2)}, u32[]{:S(2)}) collective-permute-start(bf16[192,1152]{1,0:T(8,128)(2,1)S(1)} %get-tuple-element.74), channel_id=1, source_target_pairs={{0,512},{1,513},{2,514},{3,515},{4,516},{5,517},{6,518},{7,519},{8... | collective-permute-start | bytes 1327112 | tf_op jit(solution)/shard_map/ppermute | solution.py:341
  148.4 0.0 collective-permute-done.16
  148.4 7.3 %collective-permute-start.17 = (f32[4,1152]{1,0:T(4,128)S(1)}, f32[4,1152]{1,0:T(4,128)S(1)}, u32[]{:S(2)}, u32[]{:S(2)}) collective-permute-start(f32[4,1152]{1,0:T(4,128)S(1)} %add.51), channel_id=1, source_target_pairs={{0,352},{1,353},{2,354},{3,355},{4,356},{5,357},{6,358},{7,359},{8... | collective-permute-start | bytes 55304 | tf_op jit(solution)/shard_map/ppermute | solution.py:341
  155.7 0.6 add_multiply_fusion
  156.2 0.0 copy-done.8
  156.3 4.0 %backward_norm.2 = bf16[192,1152]{1,0:T(8,128)(2,1)} custom-call(bf16[192,1152]{1,0:T(8,128)(2,1)} %bitcast.6, f32[1,1152]{1,0:T(1,128)} %get-tuple-element.97.gain_ref, f32[1,1152]{1,0:T(1,128)} %get-tuple-element.94.shift_ref, f32[1]{0:T(128)S(6)} %exp.3.scale_ref, f32[192,1152]{1,0:T(8,128)} %copy-done, bf16[208,1152]{1,0:T(8,128)(2,1)} %copy-done.8), custom_call_target="tpu_custom_call" | custom-call | flops 8847360 | bytes 2654208 | tf_op jit(solution)/shard_map/backward_norm/pallas_call | solution.py:253
  160.3 3.8 %collective-permute-done.17 = f32[4,1152]{1,0:T(4,128)S(1)} collective-permute-done((f32[4,1152]{1,0:T(4,128)S(1)}, f32[4,1152]{1,0:T(4,128)S(1)}, u32[]{:S(2)}, u32[]{:S(2)}) %collective-permute-start.17) | collective-permute-done | bytes 18464 | tf_op jit(solution)/shard_map/ppermute | solution.py:341
  164.1 0.6 fusion
  164.7 7.4 %collective-permute-done.13.refs_2_ = bf16[192,1152]{1,0:T(8,128)(2,1)S(1)} collective-permute-done((bf16[192,1152]{1,0:T(8,128)(2,1)S(1)}, bf16[192,1152]{1,0:T(8,128)(2,1)S(1)}, u32[]{:S(2)}, u32[]{:S(2)}) %collective-permute-start.13) | collective-permute-done | bytes 442400 | tf_op jit(solution)/shard_map/ppermute | solution.py:341
  172.1 0.0 collective-permute-done.12.refs_1_
  172.1 0.8 copy-done.9
  172.9 0.1 copy-done.10
  173.0 4.1 %backward_norm.3 = bf16[192,1152]{1,0:T(8,128)(2,1)} custom-call(bf16[192,1152]{1,0:T(8,128)(2,1)} %bitcast.8, f32[1,1152]{1,0:T(1,128)} %get-tuple-element.98.gain_ref, f32[1,1152]{1,0:T(1,128)} %get-tuple-element.93.shift_ref, f32[1]{0:T(128)S(6)} %exp.3.scale_ref, f32[192,1152]{1,0:T(8,128)} %copy-done.1, bf16[192,1152]{1,0:T(8,128)(2,1)} %copy-done.10, ...), custom_call_target="tpu_custom_call" | custom-call | flops 8847360 | bytes 2654208 | tf_op jit(solution)/shard_map/backward_norm/pallas_call | solution.py:253
  (16 shorter events, 0.1 us)
Async XLA Ops:
  4.8 56.9 %collective-permute-start.8 = (bf16[208,1152]{1,0:T(8,128)(2,1)}, bf16[208,1152]{1,0:T(8,128)(2,1)S(1)}, u32[]{:S(2)}, u32[]{:S(2)}) collective-permute-start(bf16[208,1152]{1,0:T(8,128)(2,1)} %get-tuple-element.60.refs_2_), channel_id=1, source_target_pairs={{0,384},{1,129},{2,386},{3,131},{4,388},{5,133},{6,390},{7,135},{8... | collective-permute-start | bytes 1437704 | tf_op jit(solution)/shard_map/ppermute | solution.py:341
  22.0 44.5 %collective-permute-start.6 = (bf16[208,1152]{1,0:T(8,128)(2,1)}, bf16[208,1152]{1,0:T(8,128)(2,1)S(1)}, u32[]{:S(2)}, u32[]{:S(2)}) collective-permute-start(bf16[208,1152]{1,0:T(8,128)(2,1)} %get-tuple-element.59.refs_0_), channel_id=1, source_target_pairs={{0,128},{1,385},{2,130},{3,387},{4,132},{5,389},{6,134},{7,391},{8... | collective-permute-start | bytes 1437704 | tf_op jit(solution)/shard_map/ppermute | solution.py:341
  25.7 48.2 %collective-permute-start.7 = (bf16[208,1152]{1,0:T(8,128)(2,1)}, bf16[208,1152]{1,0:T(8,128)(2,1)S(1)}, u32[]{:S(2)}, u32[]{:S(2)}) collective-permute-start(bf16[208,1152]{1,0:T(8,128)(2,1)} %get-tuple-element.60.refs_2_), channel_id=1, source_target_pairs={{0,512},{1,513},{2,514},{3,515},{4,516},{5,517},{6,518},{7,519},{8... | collective-permute-start | bytes 1437704 | tf_op jit(solution)/shard_map/ppermute | solution.py:341
  61.6 12.3 %collective-permute-start.9 = (bf16[208,1152]{1,0:T(8,128)(2,1)S(1)}, bf16[208,1152]{1,0:T(8,128)(2,1)S(1)}, u32[]{:S(2)}, u32[]{:S(2)}) collective-permute-start(bf16[208,1152]{1,0:T(8,128)(2,1)S(1)} %collective-permute-done.8.refs_3_), channel_id=1, source_target_pairs={{0,512},{1,513},{2,514},{3,515},{4,516},{5,517},{6,518},{7,519},{8... | collective-permute-start | bytes 1437704 | tf_op jit(solution)/shard_map/ppermute | solution.py:341
  66.5 0.7 copy-start.2
  67.2 0.7 copy-start.4
  67.9 1.0 copy-start.6
  68.9 1.0 copy-start.7
  73.0 0.9 copy-start.1
  77.5 0.9 copy-start
  78.4 55.6 %copy-start.3 = (f32[2,1152]{1,0:T(2,128)S(1)}, f32[2,1152]{1,0:T(2,128)}, u32[]{:S(2)}) copy-start(f32[2,1152]{1,0:T(2,128)} %shifts_ref.5) | copy-start | bytes 27652
  78.4 55.6 %copy-start.5 = (f32[2,1152]{1,0:T(2,128)S(1)}, f32[2,1152]{1,0:T(2,128)}, u32[]{:S(2)}) copy-start(f32[2,1152]{1,0:T(2,128)} %gains_ref.5) | copy-start | bytes 27652
  78.5 43.2 %collective-permute-start.11 = (bf16[208,1152]{1,0:T(8,128)(2,1)S(1)}, bf16[208,1152]{1,0:T(8,128)(2,1)S(1)}, u32[]{:S(2)}, u32[]{:S(2)}) collective-permute-start(bf16[208,1152]{1,0:T(8,128)(2,1)S(1)} %get-tuple-element.71), channel_id=1, source_target_pairs={{0,128},{1,385},{2,130},{3,387},{4,132},{5,389},{6,134},{7,391},{8... | collective-permute-start | bytes 1437704 | tf_op jit(solution)/shard_map/ppermute | solution.py:341
  80.5 14.1 %collective-permute-start.10 = (bf16[192,1152]{1,0:T(8,128)(2,1)S(1)}, bf16[192,1152]{1,0:T(8,128)(2,1)S(1)}, u32[]{:S(2)}, u32[]{:S(2)}) collective-permute-start(bf16[192,1152]{1,0:T(8,128)(2,1)S(1)} %get-tuple-element.67), channel_id=1, source_target_pairs={{0,512},{1,513},{2,514},{3,515},{4,516},{5,517},{6,518},{7,519},{8... | collective-permute-start | bytes 1327112 | tf_op jit(solution)/shard_map/ppermute | solution.py:341
  82.9 6.0 %collective-permute-start = (f32[4,1152]{1,0:T(4,128)S(1)}, f32[4,1152]{1,0:T(4,128)S(1)}, u32[]{:S(2)}, u32[]{:S(2)}) collective-permute-start(f32[4,1152]{1,0:T(4,128)S(1)} %get-tuple-element.144), channel_id=1, source_target_pairs={{0,1},{1,0},{2,3},{3,2},{4,5},{5,4},{6,7},{7,6},{8,9},{9,8},{10,11... | collective-permute-start | bytes 55304 | tf_op jit(solution)/shard_map/while/body/ppermute | solution.py:341
  88.9 5.6 %collective-permute-start.1 = (f32[4,1152]{1,0:T(4,128)S(1)}, f32[4,1152]{1,0:T(4,128)S(1)}, u32[]{:S(2)}, u32[]{:S(2)}) collective-permute-start(f32[4,1152]{1,0:T(4,128)S(1)} %add.69), channel_id=1, source_target_pairs={{0,8},{1,9},{2,10},{3,11},{4,12},{5,13},{6,14},{7,15},{8,0},{9,1},... | collective-permute-start | bytes 55304 | tf_op jit(solution)/shard_map/while/body/ppermute | solution.py:341
  94.6 7.0 %collective-permute-start.2 = (f32[4,1152]{1,0:T(4,128)S(1)}, f32[4,1152]{1,0:T(4,128)S(1)}, u32[]{:S(2)}, u32[]{:S(2)}) collective-permute-start(f32[4,1152]{1,0:T(4,128)S(1)} %get-tuple-element.156), channel_id=1, source_target_pairs={{0,24},{1,25},{2,26},{3,27},{4,28},{5,29},{6,30},{7,31},{8,16},{9,... | collective-permute-start | bytes 55304 | tf_op jit(solution)/shard_map/while/body/ppermute | solution.py:341
  101.6 5.6 %collective-permute-start.3 = (f32[4,1152]{1,0:T(4,128)S(1)}, f32[4,1152]{1,0:T(4,128)S(1)}, u32[]{:S(2)}, u32[]{:S(2)}) collective-permute-start(f32[4,1152]{1,0:T(4,128)S(1)} %add.72), channel_id=1, source_target_pairs={{0,512},{1,513},{2,514},{3,515},{4,516},{5,517},{6,518},{7,519},{8... | collective-permute-start | bytes 55304 | tf_op jit(solution)/shard_map/while/body/ppermute | solution.py:341
  107.3 6.9 %collective-permute-start.4 = (f32[4,1152]{1,0:T(4,128)S(1)}, f32[4,1152]{1,0:T(4,128)S(1)}, u32[]{:S(2)}, u32[]{:S(2)}) collective-permute-start(f32[4,1152]{1,0:T(4,128)S(1)} %add.73), channel_id=1, source_target_pairs={{0,518},{1,519},{2,512},{3,513},{4,514},{5,515},{6,516},{7,517},{8... | collective-permute-start | bytes 55304 | tf_op jit(solution)/shard_map/while/body/ppermute | solution.py:341
  114.2 7.4 %collective-permute-start.5 = (f32[4,1152]{1,0:T(4,128)S(1)}, f32[4,1152]{1,0:T(4,128)S(1)}, u32[]{:S(2)}, u32[]{:S(2)}) collective-permute-start(f32[4,1152]{1,0:T(4,128)S(1)} %add.74), channel_id=1, source_target_pairs={{0,514},{1,515},{2,516},{3,517},{4,518},{5,519},{6,512},{7,513},{8... | collective-permute-start | bytes 55304 | tf_op jit(solution)/shard_map/while/body/ppermute | solution.py:341
  121.6 34.6 %copy-start.8 = (bf16[208,1152]{1,0:T(8,128)(2,1)}, bf16[208,1152]{1,0:T(8,128)(2,1)S(1)}, u32[]{:S(2)}) copy-start(bf16[208,1152]{1,0:T(8,128)(2,1)S(1)} %collective-permute-done.11.refs_1_) | copy-start | bytes 1437700
  121.6 8.3 %collective-permute-start.14 = (f32[4,1152]{1,0:T(4,128)S(1)}, f32[4,1152]{1,0:T(4,128)S(1)}, u32[]{:S(2)}, u32[]{:S(2)}) collective-permute-start(f32[4,1152]{1,0:T(4,128)S(1)} %get-tuple-element.77), channel_id=1, source_target_pairs={{0,32},{1,33},{2,34},{3,35},{4,36},{5,37},{6,38},{7,39},{8,40},{9,... | collective-permute-start | bytes 55304 | tf_op jit(solution)/shard_map/ppermute | solution.py:341
  129.9 5.9 %collective-permute-start.15 = (f32[4,1152]{1,0:T(4,128)S(1)}, f32[4,1152]{1,0:T(4,128)S(1)}, u32[]{:S(2)}, u32[]{:S(2)}) collective-permute-start(f32[4,1152]{1,0:T(4,128)S(1)} %add.49), channel_id=1, source_target_pairs={{0,480},{1,481},{2,482},{3,483},{4,484},{5,485},{6,486},{7,487},{8... | collective-permute-start | bytes 55304 | tf_op jit(solution)/shard_map/ppermute | solution.py:341
  135.8 12.6 %collective-permute-start.16 = (f32[4,1152]{1,0:T(4,128)S(1)}, f32[4,1152]{1,0:T(4,128)S(1)}, u32[]{:S(2)}, u32[]{:S(2)}) collective-permute-start(f32[4,1152]{1,0:T(4,128)S(1)} %add.50), channel_id=1, source_target_pairs={{0,96},{1,97},{2,98},{3,99},{4,100},{5,101},{6,102},{7,103},{8,104... | collective-permute-start | bytes 55304 | tf_op jit(solution)/shard_map/ppermute | solution.py:341
  143.2 28.9 %collective-permute-start.13 = (bf16[192,1152]{1,0:T(8,128)(2,1)S(1)}, bf16[192,1152]{1,0:T(8,128)(2,1)S(1)}, u32[]{:S(2)}, u32[]{:S(2)}) collective-permute-start(bf16[192,1152]{1,0:T(8,128)(2,1)S(1)} %add_convert_fusion), channel_id=1, source_target_pairs={{0,384},{1,129},{2,386},{3,131},{4,388},{5,133},{6,390},{7,135},{8... | collective-permute-start | bytes 1327112 | tf_op jit(solution)/shard_map/ppermute | solution.py:341
  145.2 26.9 %collective-permute-start.12 = (bf16[192,1152]{1,0:T(8,128)(2,1)S(1)}, bf16[192,1152]{1,0:T(8,128)(2,1)S(1)}, u32[]{:S(2)}, u32[]{:S(2)}) collective-permute-start(bf16[192,1152]{1,0:T(8,128)(2,1)S(1)} %get-tuple-element.74), channel_id=1, source_target_pairs={{0,512},{1,513},{2,514},{3,515},{4,516},{5,517},{6,518},{7,519},{8... | collective-permute-start | bytes 1327112 | tf_op jit(solution)/shard_map/ppermute | solution.py:341
  148.4 15.7 %collective-permute-start.17 = (f32[4,1152]{1,0:T(4,128)S(1)}, f32[4,1152]{1,0:T(4,128)S(1)}, u32[]{:S(2)}, u32[]{:S(2)}) collective-permute-start(f32[4,1152]{1,0:T(4,128)S(1)} %add.51), channel_id=1, source_target_pairs={{0,352},{1,353},{2,354},{3,355},{4,356},{5,357},{6,358},{7,359},{8... | collective-permute-start | bytes 55304 | tf_op jit(solution)/shard_map/ppermute | solution.py:341
  172.1 0.8 copy-start.9
  172.1 0.9 copy-start.10

commit v3 on v2

--- a/solution.py
+++ b/solution.py
@@ -114,9 +114,10 @@
     blocks = refs[:4]
     if final:
         image_before, loss_before, sums_before = refs[4:7]
-        text_a_ref, text_b_ref, image_ref, back_ref, loss_ref, sums_ref = refs[7:13]
+        texts_ref, image_ref, back_ref, loss_ref, sums_ref = refs[7:12]
     else:
         text_a_ref, text_b_ref, image_ref, loss_ref, sums_ref = refs[4:9]
+        texts_ref = None
     images, texts, coeff = refs[-3:]
     rows = loss_ref.shape[1]
     for at in range(2):
@@ -162,12 +163,15 @@
     unit_sum, shift_sum = 0.0, 0.0
     if final:
         unit_sum, shift_sum = sums_before[:1, :], sums_before[1:2, :]
-    for at, part_ref in ((1, text_b_ref), (0, text_a_ref)):
+    for at in (1, 0):
         own = slice(at * rows, (at + 1) * rows)
         part = lax.dot_general(
             coeff[:, own], images[...], TN, preferred_element_type=jnp.float32
         )
-        part_ref[...] = part.astype(part_ref.dtype)
+        if final:
+            texts_ref[(1 - at) * rows : (2 - at) * rows, :] = part.astype(jnp.bfloat16)
+        else:
+            (text_a_ref, text_b_ref)[at][...] = part
         unit_add, shift_add = add_sums(texts[own, :].astype(jnp.float32), part, inverses(2 + at))
         unit_sum, shift_sum = unit_sum + unit_add, shift_sum + shift_add
     if not final:
@@ -200,7 +204,7 @@
         return jax.ShapeDtypeStruct((count, width), kind)
 
     if final:
-        outs = [wide(rows, jnp.bfloat16)] * 2
+        outs = [wide(2 * rows, jnp.bfloat16)]
         outs += [wide(rows, jnp.float32), wide(rows + EXTRA, jnp.bfloat16)]
         outs += [jax.ShapeDtypeStruct((1, rows), jnp.float32), wide(4, jnp.float32)]
     else:
@@ -226,7 +230,7 @@
     )(scalars, gains, shifts, *images, *texts, *before)
 
 
-def backward_kernel(feats_ref, gain_ref, shift_ref, scale_ref, *refs):
+def backward_kernel(firsts, feats_ref, gain_ref, shift_ref, scale_ref, *refs):
     *part_refs, grad_ref = refs
 
     @pl.loop(0, feats_ref.shape[0] // ROW_BLOCK, unroll=UNROLL)
@@ -236,9 +240,10 @@
         gain = gain_ref[...]
         normed, rstd, unnormed, inverse = norm_rows(feats, gain, shift_ref[...])
         unit = unnormed * inverse
-        pulled = part_refs[0][rows, :].astype(jnp.float32)
-        for part_ref in part_refs[1:]:
-            pulled = pulled + part_ref[rows, :].astype(jnp.float32)
+        pulled = 0.0
+        for first, part_ref in zip(firsts, part_refs):
+            at = pl.ds(pl.multiple_of(first + step * ROW_BLOCK, ROW_BLOCK), ROW_BLOCK)
+            pulled = pulled + part_ref[at, :].astype(jnp.float32)
         pulled = pulled * scale_ref[0]
         along = jnp.sum(unit * pulled, axis=-1, keepdims=True)
         pulled = inverse * (pulled - unit * along) * gain
@@ -249,9 +254,11 @@
 
 def backward_norm(feats, gain, shift, scale, parts):
     rows, width = feats.shape
+    firsts = [first for first, _ in parts]
+    parts = [part for _, part in parts]
     whole = pl.BlockSpec(memory_space=pltpu.VMEM)
     return pl.pallas_call(
-        backward_kernel,
+        functools.partial(backward_kernel, firsts),
         out_shape=jax.ShapeDtypeStruct((rows, width), jnp.bfloat16),
         in_specs=[whole] * 3 + [pl.BlockSpec(memory_space=pltpu.SMEM)] + [whole] * len(parts),
         out_specs=whole,
@@ -356,7 +363,8 @@
     y_pairs = routes.across_y()
     z_steps = routes.ring(1, 2)
     flat_steps = [routes.along(5, near), *routes.ring(None, 3), *routes.ring(4, 0)]
-    early_steps, middle_steps = flat_steps[:2], flat_steps[2:]
+    early_steps, middle_steps = flat_steps[:3], flat_steps[3:] + z_steps[:-2]
+    late_steps = z_steps[-2:]
     group_rows = 2 * RING
 
     def body(image_feats, text_feats, gains, shifts, log_scale, logit_bias):
@@ -372,32 +380,31 @@
         text_zy = send(text_z, y_pairs)
         images = [image, image_z]
         text_part, text_z_part, *before = tile(scalars, gains, shifts, images, [text, text_z])
-        text_y_part, text_zy_part, image_part, image_z_part, loss_own, sums = tile(
+        y_parts, image_part, image_z_part, loss_own, sums = tile(
             scalars, gains, shifts, images, [text_y, text_zy], before
         )
 
-        text_zy_back = send(text_zy_part, y_pairs)
         image_back = send(image_z_part, image_pairs)
+        y_back = send(y_parts, y_pairs)
         sums = sum_over(sums, early_steps, turns)
-        sums, text_zy_back, text_y_part = lax.optimization_barrier(
-            (sums, text_zy_back, text_y_part)
-        )
-        text_z_sum = text_z_part + text_zy_back.astype(jnp.float32)
+        sums, y_back = lax.optimization_barrier((sums, y_back))
+        text_z_sum = text_z_part + y_back[:rows].astype(jnp.float32)
         text_z_back = send(text_z_sum.astype(jnp.bfloat16), text_pairs)
-        text_y_back = send(text_y_part, y_pairs)
         sums = sum_over(sums, middle_steps, turns)
-        sums, image_back = lax.optimization_barrier((sums, image_back))
+        sums, image_back, text_z_back = lax.optimization_barrier((sums, image_back, text_z_back))
         image_grad = backward_norm(
-            image_feats[0], gains[:1], shifts[:1], scale, [image_part, image_back]
-        )
-        for pairs in z_steps:
+            image_feats[0], gains[:1], shifts[:1], scale, [(0, image_part), (0, image_back)]
+        )
+        sums = sums + send(sums, late_steps[0])
+        sums, image_grad = lax.optimization_barrier((sums, image_grad))
+        for pairs in late_steps[1:]:
             sums = sums + send(sums, pairs)
         text_grad = backward_norm(
             text_feats[0],
             gains[1:],
             shifts[1:],
             scale,
-            [text_part, text_y_back, text_z_back],
+            [(0, text_part), (rows, y_back), (0, text_z_back)],
         )
 
         row_mean = (loss_own + get_line(image_back[rows:], rows)) / (group_rows * rows)

time: 178 us -> 184 us (1.034)
  the two profiles are of different devices: /device:TPU:64 before, /device:TPU:28 now
where the time goes in v3:
time: 184 us; the launch traced here: 183 us
  starting transfers between devices  110 us (60%)
  waiting for transfers between devices  44 us (24%)
  Pallas kernels  19 us (10%)
  local copies, waits for them, and re-layouts  6.53 us (4%)
  between operations  2.16 us (1%)
    ppermute x17, starting transfers between devices, send(): return lax.ppermute(value, AXES, pairs)  110 us
    ppermute x17, waiting for transfers between devices, send(): return lax.ppermute(value, AXES, pairs)  44 us
    pallas_call x2, Pallas kernels, backward_norm(): pl.pallas_call(functools.partial(backward_kernel, firsts), out_shape=jax....  8.3 us
    pallas_call x2, Pallas kernels, tile(): pl.pallas_call(functools.partial(tile_kernel, final), out_shape=tuple(out...  6.58 us
    unnamed x20, local copies, waits for them, and re-layouts  5.3 us
    pallas_call x1, Pallas kernels, forward_norms(): pl.pallas_call(forward_kernel, out_shape=(emb, emb), scratch_shapes=[pltp...  4.13 us
  transfers between devices with their start and end apart: 17, of which 10 were waited for; matrix products, arithmetic and copies ran while one was open for 1% of the time, Pallas kernels for 6%

profile of v3, /device:TPU:28, one launch (start us, length us, event | category | flops | bytes accessed | tf_op | source)
XLA Modules:
  0.0 182.9 jit_solution(7044323802261518121)
XLA Ops:
  0.6 4.1 %forward_norms.1 = (bf16[208,1152]{1,0:T(8,128)(2,1)}, bf16[208,1152]{1,0:T(8,128)(2,1)}) custom-call(bf16[192,1152]{1,0:T(8,128)(2,1)} %bitcast.5, bf16[192,1152]{1,0:T(8,128)(2,1)} %bitcast.7, f32[2,1152]{1,0:T(2,128)} %gains_ref.5, f32[2,1152]{1,0:T(2,128)} %shifts_ref.5), custom_call_target="tpu_custom_call" | custom-call | flops 8847360 | bytes 1769472 | tf_op jit(solution)/shard_map/forward_norms/pallas_call | solution.py:92
  4.8 18.2 %collective-permute-start.10 = (bf16[208,1152]{1,0:T(8,128)(2,1)}, bf16[208,1152]{1,0:T(8,128)(2,1)S(1)}, u32[]{:S(2)}, u32[]{:S(2)}) collective-permute-start(bf16[208,1152]{1,0:T(8,128)(2,1)} %get-tuple-element.61.refs_2_), channel_id=1, source_target_pairs={{0,384},{1,129},{2,386},{3,131},{4,388},{5,133},{6,390},{7,135},{8... | collective-permute-start | bytes 1437704 | tf_op jit(solution)/shard_map/ppermute | solution.py:348
  22.9 3.6 %collective-permute-start.8 = (bf16[208,1152]{1,0:T(8,128)(2,1)}, bf16[208,1152]{1,0:T(8,128)(2,1)S(1)}, u32[]{:S(2)}, u32[]{:S(2)}) collective-permute-start(bf16[208,1152]{1,0:T(8,128)(2,1)} %get-tuple-element.60.refs_0_), channel_id=1, source_target_pairs={{0,128},{1,385},{2,130},{3,387},{4,132},{5,389},{6,134},{7,391},{8... | collective-permute-start | bytes 1437704 | tf_op jit(solution)/shard_map/ppermute | solution.py:348
  26.6 2.4 %collective-permute-start.9 = (bf16[208,1152]{1,0:T(8,128)(2,1)}, bf16[208,1152]{1,0:T(8,128)(2,1)S(1)}, u32[]{:S(2)}, u32[]{:S(2)}) collective-permute-start(bf16[208,1152]{1,0:T(8,128)(2,1)} %get-tuple-element.61.refs_2_), channel_id=1, source_target_pairs={{0,512},{1,513},{2,514},{3,515},{4,516},{5,517},{6,518},{7,519},{8... | collective-permute-start | bytes 1437704 | tf_op jit(solution)/shard_map/ppermute | solution.py:348
  29.0 22.1 %collective-permute-done.10.refs_3_ = bf16[208,1152]{1,0:T(8,128)(2,1)S(1)} collective-permute-done((bf16[208,1152]{1,0:T(8,128)(2,1)}, bf16[208,1152]{1,0:T(8,128)(2,1)S(1)}, u32[]{:S(2)}, u32[]{:S(2)}) %collective-permute-start.10) | collective-permute-done | bytes 479264 | tf_op jit(solution)/shard_map/ppermute | solution.py:348
  51.1 2.3 %collective-permute-start.11 = (bf16[208,1152]{1,0:T(8,128)(2,1)S(1)}, bf16[208,1152]{1,0:T(8,128)(2,1)S(1)}, u32[]{:S(2)}, u32[]{:S(2)}) collective-permute-start(bf16[208,1152]{1,0:T(8,128)(2,1)S(1)} %collective-permute-done.10.refs_3_), channel_id=1, source_target_pairs={{0,512},{1,513},{2,514},{3,515},{4,516},{5,517},{6,518},{7,519},{8... | collective-permute-start | bytes 1437704 | tf_op jit(solution)/shard_map/ppermute | solution.py:348
  54.8 0.1 pad_maximum_fusion.scalars_ref
  54.8 0.5 collective-permute-done.8.refs_1_
  55.4 0.0 copy-start.2
  55.4 0.7 copy-done.2
  56.1 0.0 copy-start.4
  56.1 0.7 copy-done.4
  56.8 0.0 copy-start.6
  56.8 1.0 copy-done.6
  57.8 1.0 copy-done.7
  58.8 3.0 %first_tile.1 = (f32[192,1152]{1,0:T(8,128)S(1)}, f32[192,1152]{1,0:T(8,128)S(1)}, f32[384,1152]{1,0:T(8,128)S(1)}, f32[2,192]{1,0:T(2,128)S(1)}, f32[2,1152]{1,0:T(2,128)S(1)}) custom-call(f32[2]{0:T(128)S(1)} %pad_maximum_fusion.scalars_ref, f32[2,1152]{1,0:T(2,128)S(1)} %copy-done.4, f32[2,1152]{1,0:T(2,128)S(1)} %copy-done.2, ...), custom_call_target="tpu_custom_call" | custom-call | flops 1019215872 | bytes 5308416 | tf_op jit(solution)/shard_map/first_tile/pallas_call | solution.py:213
  61.8 0.0 copy-start
  61.8 0.9 copy-done
  62.7 0.0 collective-permute-done.9.refs_2_
  62.7 0.0 collective-permute-done.11.refs_3_
  62.7 3.6 %last_tile.1 = (bf16[384,1152]{1,0:T(8,128)(2,1)S(1)}, f32[192,1152]{1,0:T(8,128)S(1)}, bf16[208,1152]{1,0:T(8,128)(2,1)S(1)}, f32[1,192]{1,0:T(1,128)S(1)}, f32[4,1152]{1,0:T(4,128)S(1)}) custom-call(f32[2]{0:T(128)S(1)} %pad_maximum_fusion.scalars_ref, f32[2,1152]{1,0:T(2,128)S(1)} %copy-done.4, f32[2,1152]{1,0:T(2,128)S(1)} %copy-done.2, ...), custom_call_target="tpu_custom_call" | custom-call | flops 1019215872 | bytes 5308416 | tf_op jit(solution)/shard_map/last_tile/pallas_call | solution.py:213
  66.3 0.0 copy-start.1
  66.3 0.9 copy-done.1
  67.3 3.0 %collective-permute-start.12 = (bf16[384,1152]{1,0:T(8,128)(2,1)S(1)}, bf16[384,1152]{1,0:T(8,128)(2,1)S(1)}, u32[]{:S(2)}, u32[]{:S(2)}) collective-permute-start(bf16[384,1152]{1,0:T(8,128)(2,1)S(1)} %get-tuple-element.67), channel_id=1, source_target_pairs={{0,512},{1,513},{2,514},{3,515},{4,516},{5,517},{6,518},{7,519},{8... | collective-permute-start | bytes 2654216 | tf_op jit(solution)/shard_map/ppermute | solution.py:348
  70.3 17.0 %collective-permute-start.13 = (bf16[208,1152]{1,0:T(8,128)(2,1)S(1)}, bf16[208,1152]{1,0:T(8,128)(2,1)}, u32[]{:S(2)}, u32[]{:S(2)}) collective-permute-start(bf16[208,1152]{1,0:T(8,128)(2,1)S(1)} %get-tuple-element.70), channel_id=1, source_target_pairs={{0,128},{1,385},{2,130},{3,387},{4,132},{5,389},{6,134},{7,391},{8... | collective-permute-start | bytes 1437704 | tf_op jit(solution)/shard_map/ppermute | solution.py:348
  87.3 14.4 %while.20 = (s32[]{:T(128)}, f32[4,1152]{1,0:T(4,128)S(1)}, s32[]{:T(128)}, s32[]{:T(128)}) while((s32[]{:T(128)}, f32[4,1152]{1,0:T(4,128)S(1)}, s32[]{:T(128)}, s32[]{:T(128)}) %tuple.46), condition=%wide.region_1.2_spmd, body=%wide.region_0.1_spmd.sunk | while | flops 13826 | bytes 387245 | solution.py:358
  87.3 2.0 %collective-permute-start = (f32[4,1152]{1,0:T(4,128)S(1)}, f32[4,1152]{1,0:T(4,128)S(1)}, u32[]{:S(2)}, u32[]{:S(2)}) collective-permute-start(f32[4,1152]{1,0:T(4,128)S(1)} %get-tuple-element.146), channel_id=1, source_target_pairs={{0,1},{1,0},{2,3},{3,2},{4,5},{5,4},{6,7},{7,6},{8,9},{9,8},{10,11... | collective-permute-start | bytes 55304 | tf_op jit(solution)/shard_map/while/body/ppermute | solution.py:348
  89.4 1.0 collective-permute-done
  90.4 3.1 %collective-permute-start.1 = (f32[4,1152]{1,0:T(4,128)S(1)}, f32[4,1152]{1,0:T(4,128)S(1)}, u32[]{:S(2)}, u32[]{:S(2)}) collective-permute-start(f32[4,1152]{1,0:T(4,128)S(1)} %add.69), channel_id=1, source_target_pairs={{0,8},{1,9},{2,10},{3,11},{4,12},{5,13},{6,14},{7,15},{8,0},{9,1},... | collective-permute-start | bytes 55304 | tf_op jit(solution)/shard_map/while/body/ppermute | solution.py:348
  93.5 2.5 %collective-permute-done.1 = f32[4,1152]{1,0:T(4,128)S(1)} collective-permute-done((f32[4,1152]{1,0:T(4,128)S(1)}, f32[4,1152]{1,0:T(4,128)S(1)}, u32[]{:S(2)}, u32[]{:S(2)}) %collective-permute-start.1) | collective-permute-done | bytes 18464 | tf_op jit(solution)/shard_map/while/body/ppermute | solution.py:348
  96.1 2.4 %collective-permute-start.2 = (f32[4,1152]{1,0:T(4,128)S(1)}, f32[4,1152]{1,0:T(4,128)S(1)}, u32[]{:S(2)}, u32[]{:S(2)}) collective-permute-start(f32[4,1152]{1,0:T(4,128)S(1)} %add.70), channel_id=1, source_target_pairs={{0,24},{1,25},{2,26},{3,27},{4,28},{5,29},{6,30},{7,31},{8,16},{9,... | collective-permute-start | bytes 55304 | tf_op jit(solution)/shard_map/while/body/ppermute | solution.py:348
  98.5 3.2 %collective-permute-done.2 = f32[4,1152]{1,0:T(4,128)S(1)} collective-permute-done((f32[4,1152]{1,0:T(4,128)S(1)}, f32[4,1152]{1,0:T(4,128)S(1)}, u32[]{:S(2)}, u32[]{:S(2)}) %collective-permute-start.2) | collective-permute-done | bytes 18464 | tf_op jit(solution)/shard_map/while/body/ppermute | solution.py:348
  101.7 0.0 copy-start.5
  101.7 0.0 collective-permute-done.12.refs_1_
  101.8 0.0 copy-start.8
  101.8 0.1 add_convert_fusion
  101.9 8.4 %collective-permute-start.14 = (bf16[192,1152]{1,0:T(8,128)(2,1)S(1)}, bf16[192,1152]{1,0:T(8,128)(2,1)S(1)}, u32[]{:S(2)}, u32[]{:S(2)}) collective-permute-start(bf16[192,1152]{1,0:T(8,128)(2,1)S(1)} %add_convert_fusion), channel_id=1, source_target_pairs={{0,384},{1,129},{2,386},{3,131},{4,388},{5,133},{6,390},{7,135},{8... | collective-permute-start | bytes 1327112 | tf_op jit(solution)/shard_map/ppermute | solution.py:348
  110.3 0.0 collective-permute-done.13.refs_1_
  110.3 47.8 %while.21 = (s32[]{:T(128)}, f32[4,1152]{1,0:T(4,128)S(1)}, s32[]{:T(128)}, s32[]{:T(128)}) while((s32[]{:T(128)}, f32[4,1152]{1,0:T(4,128)S(1)}, s32[]{:T(128)}, s32[]{:T(128)}) %tuple.49), condition=%wide.region_3.4_spmd, body=%wide.region_2.3_spmd.sunk | while | flops 23042 | bytes 645373 | solution.py:358
  110.3 2.3 %collective-permute-start.3 = (f32[4,1152]{1,0:T(4,128)S(1)}, f32[4,1152]{1,0:T(4,128)S(1)}, u32[]{:S(2)}, u32[]{:S(2)}) collective-permute-start(f32[4,1152]{1,0:T(4,128)S(1)} %get-tuple-element.158), channel_id=1, source_target_pairs={{0,512},{1,513},{2,514},{3,515},{4,516},{5,517},{6,518},{7,519},{8... | collective-permute-start | bytes 55304 | tf_op jit(solution)/shard_map/while/body/ppermute | solution.py:348
  112.6 3.3 %collective-permute-done.3 = f32[4,1152]{1,0:T(4,128)S(1)} collective-permute-done((f32[4,1152]{1,0:T(4,128)S(1)}, f32[4,1152]{1,0:T(4,128)S(1)}, u32[]{:S(2)}, u32[]{:S(2)}) %collective-permute-start.3) | collective-permute-done | bytes 18464 | tf_op jit(solution)/shard_map/while/body/ppermute | solution.py:348
  116.0 4.7 %collective-permute-start.4 = (f32[4,1152]{1,0:T(4,128)S(1)}, f32[4,1152]{1,0:T(4,128)S(1)}, u32[]{:S(2)}, u32[]{:S(2)}) collective-permute-start(f32[4,1152]{1,0:T(4,128)S(1)} %add.73), channel_id=1, source_target_pairs={{0,518},{1,519},{2,512},{3,513},{4,514},{5,515},{6,516},{7,517},{8... | collective-permute-start | bytes 55304 | tf_op jit(solution)/shard_map/while/body/ppermute | solution.py:348
  120.6 2.2 %collective-permute-done.4 = f32[4,1152]{1,0:T(4,128)S(1)} collective-permute-done((f32[4,1152]{1,0:T(4,128)S(1)}, f32[4,1152]{1,0:T(4,128)S(1)}, u32[]{:S(2)}, u32[]{:S(2)}) %collective-permute-start.4) | collective-permute-done | bytes 18464 | tf_op jit(solution)/shard_map/while/body/ppermute | solution.py:348
  122.8 2.4 %collective-permute-start.5 = (f32[4,1152]{1,0:T(4,128)S(1)}, f32[4,1152]{1,0:T(4,128)S(1)}, u32[]{:S(2)}, u32[]{:S(2)}) collective-permute-start(f32[4,1152]{1,0:T(4,128)S(1)} %add.74), channel_id=1, source_target_pairs={{0,514},{1,515},{2,516},{3,517},{4,518},{5,519},{6,512},{7,513},{8... | collective-permute-start | bytes 55304 | tf_op jit(solution)/shard_map/while/body/ppermute | solution.py:348
  125.2 5.1 %collective-permute-done.5 = f32[4,1152]{1,0:T(4,128)S(1)} collective-permute-done((f32[4,1152]{1,0:T(4,128)S(1)}, f32[4,1152]{1,0:T(4,128)S(1)}, u32[]{:S(2)}, u32[]{:S(2)}) %collective-permute-start.5) | collective-permute-done | bytes 18464 | tf_op jit(solution)/shard_map/while/body/ppermute | solution.py:348
  130.3 3.4 %collective-permute-start.6 = (f32[4,1152]{1,0:T(4,128)S(1)}, f32[4,1152]{1,0:T(4,128)S(1)}, u32[]{:S(2)}, u32[]{:S(2)}) collective-permute-start(f32[4,1152]{1,0:T(4,128)S(1)} %add.75), channel_id=1, source_target_pairs={{0,32},{1,33},{2,34},{3,35},{4,36},{5,37},{6,38},{7,39},{8,40},{9,... | collective-permute-start | bytes 55304 | tf_op jit(solution)/shard_map/while/body/ppermute | solution.py:348
  133.7 2.2 %collective-permute-done.6 = f32[4,1152]{1,0:T(4,128)S(1)} collective-permute-done((f32[4,1152]{1,0:T(4,128)S(1)}, f32[4,1152]{1,0:T(4,128)S(1)}, u32[]{:S(2)}, u32[]{:S(2)}) %collective-permute-start.6) | collective-permute-done | bytes 18464 | tf_op jit(solution)/shard_map/while/body/ppermute | solution.py:348
  135.9 20.4 %collective-permute-start.7 = (f32[4,1152]{1,0:T(4,128)S(1)}, f32[4,1152]{1,0:T(4,128)S(1)}, u32[]{:S(2)}, u32[]{:S(2)}) collective-permute-start(f32[4,1152]{1,0:T(4,128)S(1)} %add.76), channel_id=1, source_target_pairs={{0,480},{1,481},{2,482},{3,483},{4,484},{5,485},{6,486},{7,487},{8... | collective-permute-start | bytes 55304 | tf_op jit(solution)/shard_map/while/body/ppermute | solution.py:348
  156.4 1.8 collective-permute-done.7
  158.1 0.0 collective-permute-done.14.refs_2_
  158.1 0.0 copy-start.9
  158.1 5.4 %collective-permute-start.15 = (f32[4,1152]{1,0:T(4,128)S(1)}, f32[4,1152]{1,0:T(4,128)S(1)}, u32[]{:S(2)}, u32[]{:S(2)}) collective-permute-start(f32[4,1152]{1,0:T(4,128)S(1)} %get-tuple-element.73), channel_id=1, source_target_pairs={{0,96},{1,97},{2,98},{3,99},{4,100},{5,101},{6,102},{7,103},{8,104... | collective-permute-start | bytes 55304 | tf_op jit(solution)/shard_map/ppermute | solution.py:348
  163.5 0.0 copy-done.3
  163.5 0.0 copy-done.5
  163.6 0.6 fusion.1
  164.2 4.0 %backward_norm.2 = bf16[192,1152]{1,0:T(8,128)(2,1)} custom-call(bf16[192,1152]{1,0:T(8,128)(2,1)} %bitcast.6, f32[1,1152]{1,0:T(1,128)} %get-tuple-element.99.gain_ref, f32[1,1152]{1,0:T(1,128)} %get-tuple-element.96.shift_ref, f32[1]{0:T(128)S(6)} %exp.3.scale_ref, f32[192,1152]{1,0:T(8,128)} %copy-done.1, bf16[208,1152]{1,0:T(8,128)(2,1)} %collective-permute-done.13.refs_1_), custom_call_target="tpu_custom_call" | custom-call | flops 8847360 | bytes 2654208 | tf_op jit(solution)/shard_map/backward_norm/pallas_call | solution.py:260
  168.2 0.0 copy-done.8
  168.2 0.0 collective-permute-done.15
  168.2 8.5 %collective-permute-start.16 = (f32[4,1152]{1,0:T(4,128)S(1)}, f32[4,1152]{1,0:T(4,128)S(1)}, u32[]{:S(2)}, u32[]{:S(2)}) collective-permute-start(f32[4,1152]{1,0:T(4,128)S(1)} %add.49), channel_id=1, source_target_pairs={{0,352},{1,353},{2,354},{3,355},{4,356},{5,357},{6,358},{7,359},{8... | collective-permute-start | bytes 55304 | tf_op jit(solution)/shard_map/ppermute | solution.py:348
  176.7 1.3 add_multiply_fusion
  178.0 0.0 copy-done.9
  178.0 4.3 %backward_norm.3 = bf16[192,1152]{1,0:T(8,128)(2,1)} custom-call(bf16[192,1152]{1,0:T(8,128)(2,1)} %bitcast.8, f32[1,1152]{1,0:T(1,128)} %get-tuple-element.100.gain_ref, f32[1,1152]{1,0:T(1,128)} %get-tuple-element.95.shift_ref, f32[1]{0:T(128)S(6)} %exp.3.scale_ref, f32[192,1152]{1,0:T(8,128)} %copy-done, bf16[384,1152]{1,0:T(8,128)(2,1)} %copy-done.8, ...), custom_call_target="tpu_custom_call" | custom-call | flops 8847360 | bytes 2654208 | tf_op jit(solution)/shard_map/backward_norm/pallas_call | solution.py:260
  182.3 0.0 collective-permute-done.16
  182.3 0.6 fusion
  (12 shorter events, 0.1 us)
Async XLA Ops:
  4.8 46.3 %collective-permute-start.10 = (bf16[208,1152]{1,0:T(8,128)(2,1)}, bf16[208,1152]{1,0:T(8,128)(2,1)S(1)}, u32[]{:S(2)}, u32[]{:S(2)}) collective-permute-start(bf16[208,1152]{1,0:T(8,128)(2,1)} %get-tuple-element.61.refs_2_), channel_id=1, source_target_pairs={{0,384},{1,129},{2,386},{3,131},{4,388},{5,133},{6,390},{7,135},{8... | collective-permute-start | bytes 1437704 | tf_op jit(solution)/shard_map/ppermute | solution.py:348
  22.9 32.4 %collective-permute-start.8 = (bf16[208,1152]{1,0:T(8,128)(2,1)}, bf16[208,1152]{1,0:T(8,128)(2,1)S(1)}, u32[]{:S(2)}, u32[]{:S(2)}) collective-permute-start(bf16[208,1152]{1,0:T(8,128)(2,1)} %get-tuple-element.60.refs_0_), channel_id=1, source_target_pairs={{0,128},{1,385},{2,130},{3,387},{4,132},{5,389},{6,134},{7,391},{8... | collective-permute-start | bytes 1437704 | tf_op jit(solution)/shard_map/ppermute | solution.py:348
  26.6 36.1 %collective-permute-start.9 = (bf16[208,1152]{1,0:T(8,128)(2,1)}, bf16[208,1152]{1,0:T(8,128)(2,1)S(1)}, u32[]{:S(2)}, u32[]{:S(2)}) collective-permute-start(bf16[208,1152]{1,0:T(8,128)(2,1)} %get-tuple-element.61.refs_2_), channel_id=1, source_target_pairs={{0,512},{1,513},{2,514},{3,515},{4,516},{5,517},{6,518},{7,519},{8... | collective-permute-start | bytes 1437704 | tf_op jit(solution)/shard_map/ppermute | solution.py:348
  51.1 11.6 %collective-permute-start.11 = (bf16[208,1152]{1,0:T(8,128)(2,1)S(1)}, bf16[208,1152]{1,0:T(8,128)(2,1)S(1)}, u32[]{:S(2)}, u32[]{:S(2)}) collective-permute-start(bf16[208,1152]{1,0:T(8,128)(2,1)S(1)} %collective-permute-done.10.refs_3_), channel_id=1, source_target_pairs={{0,512},{1,513},{2,514},{3,515},{4,516},{5,517},{6,518},{7,519},{8... | collective-permute-start | bytes 1437704 | tf_op jit(solution)/shard_map/ppermute | solution.py:348
  55.4 0.7 copy-start.2
  56.1 0.7 copy-start.4
  56.8 1.0 copy-start.6
  57.8 1.0 copy-start.7
  61.8 0.9 copy-start
  66.3 0.9 copy-start.1
  67.3 34.5 %collective-permute-start.12 = (bf16[384,1152]{1,0:T(8,128)(2,1)S(1)}, bf16[384,1152]{1,0:T(8,128)(2,1)S(1)}, u32[]{:S(2)}, u32[]{:S(2)}) collective-permute-start(bf16[384,1152]{1,0:T(8,128)(2,1)S(1)} %get-tuple-element.67), channel_id=1, source_target_pairs={{0,512},{1,513},{2,514},{3,515},{4,516},{5,517},{6,518},{7,519},{8... | collective-permute-start | bytes 2654216 | tf_op jit(solution)/shard_map/ppermute | solution.py:348
  70.3 40.0 %collective-permute-start.13 = (bf16[208,1152]{1,0:T(8,128)(2,1)S(1)}, bf16[208,1152]{1,0:T(8,128)(2,1)}, u32[]{:S(2)}, u32[]{:S(2)}) collective-permute-start(bf16[208,1152]{1,0:T(8,128)(2,1)S(1)} %get-tuple-element.70), channel_id=1, source_target_pairs={{0,128},{1,385},{2,130},{3,387},{4,132},{5,389},{6,134},{7,391},{8... | collective-permute-start | bytes 1437704 | tf_op jit(solution)/shard_map/ppermute | solution.py:348
  87.3 3.1 %collective-permute-start = (f32[4,1152]{1,0:T(4,128)S(1)}, f32[4,1152]{1,0:T(4,128)S(1)}, u32[]{:S(2)}, u32[]{:S(2)}) collective-permute-start(f32[4,1152]{1,0:T(4,128)S(1)} %get-tuple-element.146), channel_id=1, source_target_pairs={{0,1},{1,0},{2,3},{3,2},{4,5},{5,4},{6,7},{7,6},{8,9},{9,8},{10,11... | collective-permute-start | bytes 55304 | tf_op jit(solution)/shard_map/while/body/ppermute | solution.py:348
  90.4 5.6 %collective-permute-start.1 = (f32[4,1152]{1,0:T(4,128)S(1)}, f32[4,1152]{1,0:T(4,128)S(1)}, u32[]{:S(2)}, u32[]{:S(2)}) collective-permute-start(f32[4,1152]{1,0:T(4,128)S(1)} %add.69), channel_id=1, source_target_pairs={{0,8},{1,9},{2,10},{3,11},{4,12},{5,13},{6,14},{7,15},{8,0},{9,1},... | collective-permute-start | bytes 55304 | tf_op jit(solution)/shard_map/while/body/ppermute | solution.py:348
  96.1 5.6 %collective-permute-start.2 = (f32[4,1152]{1,0:T(4,128)S(1)}, f32[4,1152]{1,0:T(4,128)S(1)}, u32[]{:S(2)}, u32[]{:S(2)}) collective-permute-start(f32[4,1152]{1,0:T(4,128)S(1)} %add.70), channel_id=1, source_target_pairs={{0,24},{1,25},{2,26},{3,27},{4,28},{5,29},{6,30},{7,31},{8,16},{9,... | collective-permute-start | bytes 55304 | tf_op jit(solution)/shard_map/while/body/ppermute | solution.py:348
  101.7 61.8 %copy-start.3 = (f32[2,1152]{1,0:T(2,128)S(1)}, f32[2,1152]{1,0:T(2,128)}, u32[]{:S(2)}) copy-start(f32[2,1152]{1,0:T(2,128)} %shifts_ref.5) | copy-start | bytes 27652
  101.7 61.8 %copy-start.5 = (f32[2,1152]{1,0:T(2,128)S(1)}, f32[2,1152]{1,0:T(2,128)}, u32[]{:S(2)}) copy-start(f32[2,1152]{1,0:T(2,128)} %gains_ref.5) | copy-start | bytes 27652
  101.8 66.4 %copy-start.8 = (bf16[384,1152]{1,0:T(8,128)(2,1)}, bf16[384,1152]{1,0:T(8,128)(2,1)S(1)}, u32[]{:S(2)}) copy-start(bf16[384,1152]{1,0:T(8,128)(2,1)S(1)} %collective-permute-done.12.refs_1_) | copy-start | bytes 2654212
  101.9 56.3 %collective-permute-start.14 = (bf16[192,1152]{1,0:T(8,128)(2,1)S(1)}, bf16[192,1152]{1,0:T(8,128)(2,1)S(1)}, u32[]{:S(2)}, u32[]{:S(2)}) collective-permute-start(bf16[192,1152]{1,0:T(8,128)(2,1)S(1)} %add_convert_fusion), channel_id=1, source_target_pairs={{0,384},{1,129},{2,386},{3,131},{4,388},{5,133},{6,390},{7,135},{8... | collective-permute-start | bytes 1327112 | tf_op jit(solution)/shard_map/ppermute | solution.py:348
  110.3 5.7 %collective-permute-start.3 = (f32[4,1152]{1,0:T(4,128)S(1)}, f32[4,1152]{1,0:T(4,128)S(1)}, u32[]{:S(2)}, u32[]{:S(2)}) collective-permute-start(f32[4,1152]{1,0:T(4,128)S(1)} %get-tuple-element.158), channel_id=1, source_target_pairs={{0,512},{1,513},{2,514},{3,515},{4,516},{5,517},{6,518},{7,519},{8... | collective-permute-start | bytes 55304 | tf_op jit(solution)/shard_map/while/body/ppermute | solution.py:348
  116.0 6.9 %collective-permute-start.4 = (f32[4,1152]{1,0:T(4,128)S(1)}, f32[4,1152]{1,0:T(4,128)S(1)}, u32[]{:S(2)}, u32[]{:S(2)}) collective-permute-start(f32[4,1152]{1,0:T(4,128)S(1)} %add.73), channel_id=1, source_target_pairs={{0,518},{1,519},{2,512},{3,513},{4,514},{5,515},{6,516},{7,517},{8... | collective-permute-start | bytes 55304 | tf_op jit(solution)/shard_map/while/body/ppermute | solution.py:348
  122.8 7.4 %collective-permute-start.5 = (f32[4,1152]{1,0:T(4,128)S(1)}, f32[4,1152]{1,0:T(4,128)S(1)}, u32[]{:S(2)}, u32[]{:S(2)}) collective-permute-start(f32[4,1152]{1,0:T(4,128)S(1)} %add.74), channel_id=1, source_target_pairs={{0,514},{1,515},{2,516},{3,517},{4,518},{5,519},{6,512},{7,513},{8... | collective-permute-start | bytes 55304 | tf_op jit(solution)/shard_map/while/body/ppermute | solution.py:348
  130.3 5.6 %collective-permute-start.6 = (f32[4,1152]{1,0:T(4,128)S(1)}, f32[4,1152]{1,0:T(4,128)S(1)}, u32[]{:S(2)}, u32[]{:S(2)}) collective-permute-start(f32[4,1152]{1,0:T(4,128)S(1)} %add.75), channel_id=1, source_target_pairs={{0,32},{1,33},{2,34},{3,35},{4,36},{5,37},{6,38},{7,39},{8,40},{9,... | collective-permute-start | bytes 55304 | tf_op jit(solution)/shard_map/while/body/ppermute | solution.py:348
  135.9 22.2 %collective-permute-start.7 = (f32[4,1152]{1,0:T(4,128)S(1)}, f32[4,1152]{1,0:T(4,128)S(1)}, u32[]{:S(2)}, u32[]{:S(2)}) collective-permute-start(f32[4,1152]{1,0:T(4,128)S(1)} %add.76), channel_id=1, source_target_pairs={{0,480},{1,481},{2,482},{3,483},{4,484},{5,485},{6,486},{7,487},{8... | collective-permute-start | bytes 55304 | tf_op jit(solution)/shard_map/while/body/ppermute | solution.py:348
  158.1 19.8 %copy-start.9 = (bf16[192,1152]{1,0:T(8,128)(2,1)}, bf16[192,1152]{1,0:T(8,128)(2,1)S(1)}, u32[]{:S(2)}) copy-start(bf16[192,1152]{1,0:T(8,128)(2,1)S(1)} %collective-permute-done.14.refs_2_) | copy-start | bytes 1327108
  158.1 10.0 %collective-permute-start.15 = (f32[4,1152]{1,0:T(4,128)S(1)}, f32[4,1152]{1,0:T(4,128)S(1)}, u32[]{:S(2)}, u32[]{:S(2)}) collective-permute-start(f32[4,1152]{1,0:T(4,128)S(1)} %get-tuple-element.73), channel_id=1, source_target_pairs={{0,96},{1,97},{2,98},{3,99},{4,100},{5,101},{6,102},{7,103},{8,104... | collective-permute-start | bytes 55304 | tf_op jit(solution)/shard_map/ppermute | solution.py:348
  168.2 14.1 %collective-permute-start.16 = (f32[4,1152]{1,0:T(4,128)S(1)}, f32[4,1152]{1,0:T(4,128)S(1)}, u32[]{:S(2)}, u32[]{:S(2)}) collective-permute-start(f32[4,1152]{1,0:T(4,128)S(1)} %add.49), channel_id=1, source_target_pairs={{0,352},{1,353},{2,354},{3,355},{4,356},{5,357},{6,358},{7,359},{8... | collective-permute-start | bytes 55304 | tf_op jit(solution)/shard_map/ppermute | solution.py:348

commit v4 on v3

--- a/solution.py
+++ b/solution.py
@@ -111,92 +111,73 @@
 
 
 def tile_kernel(final, scalars_ref, gains_ref, shifts_ref, *refs):
-    blocks = refs[:4]
+    image_in, text_ins = refs[0], refs[1:5]
     if final:
-        image_before, loss_before, sums_before = refs[4:7]
-        texts_ref, image_ref, back_ref, loss_ref, sums_ref = refs[7:12]
+        parts_before, sums_before = refs[5:7]
+        text_ref, text_z_ref, texts_ref, image_ref, sums_ref = refs[7:12]
     else:
-        text_a_ref, text_b_ref, image_ref, loss_ref, sums_ref = refs[4:9]
-        texts_ref = None
-    images, texts, coeff = refs[-3:]
-    rows = loss_ref.shape[1]
-    for at in range(2):
+        parts_ref, image_ref, loss_ref, sums_ref = refs[5:9]
+    texts, coeff = refs[-2:]
+    rows = coeff.shape[0]
+    image = image_in[:rows, :]
+    for at, ref in enumerate(text_ins):
+        texts[at * rows : (at + 1) * rows, :] = ref[:rows, :]
+    logits = lax.dot_general(image, texts[...], NT, preferred_element_type=jnp.float32)
+    logits = scalars_ref[0] * logits + scalars_ref[1]
+    if not final:
+        row_at = lax.broadcasted_iota(jnp.int32, logits.shape, 0)
+        column_at = lax.broadcasted_iota(jnp.int32, logits.shape, 1)
+        signs = jnp.where(row_at == column_at, -1.0, 1.0)
+        logits = signs * logits
+    small = jnp.exp(-jnp.abs(logits))
+    terms = jnp.maximum(logits, 0.0) + jnp.log1p(small)
+    slopes = jnp.where(logits >= 0.0, 1.0, small) / (1.0 + small)
+    if not final:
+        slopes = signs * slopes
+    coeff[...] = slopes.astype(jnp.bfloat16)
+    losses = to_lanes(jnp.sum(terms, axis=1, keepdims=True))
+    if final:
+        put_line(image_ref, losses)
+    else:
+        loss_ref[...] = losses
+
+    unit_sum, shift_sum = 0.0, 0.0
+    for at in (3, 2, 1, 0):
         own = slice(at * rows, (at + 1) * rows)
-        images[own, :] = blocks[at][:rows, :]
-        texts[own, :] = blocks[2 + at][:rows, :]
-    losses = []
-    for at in range(2):
-        own = slice(at * rows, (at + 1) * rows)
-        logits = lax.dot_general(
-            images[own, :], texts[...], NT, preferred_element_type=jnp.float32
-        )
-        logits = scalars_ref[0] * logits + scalars_ref[1]
-        diagonal = at == 0 and not final
-        if diagonal:
-            row_at = lax.broadcasted_iota(jnp.int32, logits.shape, 0)
-            column_at = lax.broadcasted_iota(jnp.int32, logits.shape, 1)
-            signs = jnp.where(row_at == column_at, -1.0, 1.0)
-            logits = signs * logits
-        small = jnp.exp(-jnp.abs(logits))
-        terms = jnp.maximum(logits, 0.0) + jnp.log1p(small)
-        slopes = jnp.where(logits >= 0.0, 1.0, small) / (1.0 + small)
-        if diagonal:
-            slopes = signs * slopes
-        coeff[own, :] = slopes.astype(jnp.bfloat16)
-        losses.append(to_lanes(jnp.sum(terms, axis=1, keepdims=True)))
+        part = lax.dot_general(coeff[:, own], image, TN, preferred_element_type=jnp.float32)
+        if not final:
+            parts_ref[own, :] = part
+        elif at >= 2:
+            whole = part + parts_before[own, :]
+            texts_ref[(3 - at) * rows : (4 - at) * rows, :] = whole.astype(jnp.bfloat16)
+        else:
+            (text_ref, text_z_ref)[at][...] = part + parts_before[own, :]
+        inverse = to_rows(get_line(text_ins[at][rows:, :], rows))
+        unit_add, shift_add = add_sums(texts[own, :].astype(jnp.float32), part, inverse)
+        unit_sum, shift_sum = unit_sum + unit_add, shift_sum + shift_add
+    part = jnp.dot(coeff[...], texts[...], preferred_element_type=jnp.float32)
     if final:
-        loss_ref[...] = loss_before[:1, :] + losses[0]
-        put_line(back_ref, loss_before[1:2, :] + losses[1])
+        image_ref[:rows, :] = part.astype(jnp.bfloat16)
     else:
-        for at in range(2):
-            loss_ref[at : at + 1, :] = losses[at]
-
-    def inverses(at):
-        return to_rows(get_line(blocks[at][rows:, :], rows))
-
-    def finish(tower, unit_sum, shift_sum):
-        gain = gains_ref[tower : tower + 1, :]
+        image_ref[...] = part
+    inverse = to_rows(get_line(image_in[rows:, :], rows))
+    image_unit_sum, image_shift_sum = add_sums(image.astype(jnp.float32), part, inverse)
+    sums = (image_unit_sum, unit_sum, image_shift_sum, shift_sum)
+    if not final:
+        for at in range(4):
+            sums_ref[at : at + 1, :] = sums[at]
+        return
+    for tower in range(2):
         shift = shifts_ref[tower : tower + 1, :]
-        sums_ref[tower : tower + 1, :] = scalars_ref[0] * (unit_sum - shift * shift_sum) / gain
+        unit_sum = sums[tower] + sums_before[tower : tower + 1, :]
+        shift_sum = sums[2 + tower] + sums_before[2 + tower : 3 + tower, :]
+        gain_sum = (unit_sum - shift * shift_sum) / gains_ref[tower : tower + 1, :]
+        sums_ref[tower : tower + 1, :] = scalars_ref[0] * gain_sum
         sums_ref[2 + tower : 3 + tower, :] = scalars_ref[0] * shift_sum
 
-    unit_sum, shift_sum = 0.0, 0.0
-    if final:
-        unit_sum, shift_sum = sums_before[:1, :], sums_before[1:2, :]
-    for at in (1, 0):
-        own = slice(at * rows, (at + 1) * rows)
-        part = lax.dot_general(
-            coeff[:, own], images[...], TN, preferred_element_type=jnp.float32
-        )
-        if final:
-            texts_ref[(1 - at) * rows : (2 - at) * rows, :] = part.astype(jnp.bfloat16)
-        else:
-            (text_a_ref, text_b_ref)[at][...] = part
-        unit_add, shift_add = add_sums(texts[own, :].astype(jnp.float32), part, inverses(2 + at))
-        unit_sum, shift_sum = unit_sum + unit_add, shift_sum + shift_add
-    if not final:
-        sums_ref[:1, :] = unit_sum
-        sums_ref[1:2, :] = shift_sum
-        image_ref[...] = jnp.dot(coeff[...], texts[...], preferred_element_type=jnp.float32)
-        return
-    finish(1, unit_sum, shift_sum)
-    unit_sum, shift_sum = 0.0, 0.0
-    for at in range(2):
-        own = slice(at * rows, (at + 1) * rows)
-        part = image_before[own, :] + jnp.dot(
-            coeff[own, :], texts[...], preferred_element_type=jnp.float32
-        )
-        if at == 0:
-            image_ref[...] = part
-        else:
-            back_ref[:rows, :] = part.astype(jnp.bfloat16)
-        unit_add, shift_add = add_sums(images[own, :].astype(jnp.float32), part, inverses(at))
-        unit_sum, shift_sum = unit_sum + unit_add, shift_sum + shift_add
-    finish(0, unit_sum, shift_sum)
-
-
-def tile(scalars, gains, shifts, images, texts, before=()):
-    rows, width = images[0].shape[0] - EXTRA, images[0].shape[1]
+
+def tile(scalars, gains, shifts, image, texts, before=()):
+    rows, width = image.shape[0] - EXTRA, image.shape[1]
     final = len(before) > 0
     whole = pl.BlockSpec(memory_space=pltpu.VMEM)
 
@@ -204,21 +185,20 @@
         return jax.ShapeDtypeStruct((count, width), kind)
 
     if final:
-        outs = [wide(2 * rows, jnp.bfloat16)]
-        outs += [wide(rows, jnp.float32), wide(rows + EXTRA, jnp.bfloat16)]
-        outs += [jax.ShapeDtypeStruct((1, rows), jnp.float32), wide(4, jnp.float32)]
+        outs = [wide(rows, jnp.float32)] * 2
+        outs += [wide(2 * rows, jnp.bfloat16), wide(rows + EXTRA, jnp.bfloat16)]
     else:
-        outs = [wide(rows, jnp.float32)] * 2 + [wide(2 * rows, jnp.float32)]
-        outs += [jax.ShapeDtypeStruct((2, rows), jnp.float32), wide(2, jnp.float32)]
+        outs = [wide(4 * rows, jnp.float32), wide(rows, jnp.float32)]
+        outs += [jax.ShapeDtypeStruct((1, rows), jnp.float32)]
+    outs += [wide(4, jnp.float32)]
     return pl.pallas_call(
         functools.partial(tile_kernel, final),
         out_shape=tuple(outs),
-        in_specs=[pl.BlockSpec(memory_space=pltpu.SMEM)] + [whole] * (6 + len(before)),
+        in_specs=[pl.BlockSpec(memory_space=pltpu.SMEM)] + [whole] * (7 + len(before)),
         out_specs=(whole,) * len(outs),
         scratch_shapes=[
-            pltpu.VMEM((2 * rows, width), jnp.bfloat16),
-            pltpu.VMEM((2 * rows, width), jnp.bfloat16),
-            pltpu.VMEM((2 * rows, 2 * rows), jnp.bfloat16),
+            pltpu.VMEM((4 * rows, width), jnp.bfloat16),
+            pltpu.VMEM((rows, 4 * rows), jnp.bfloat16),
         ],
         compiler_params=pltpu.CompilerParams(vmem_limit_bytes=TILE_VMEM_LIMIT),
         cost_estimate=pl.CostEstimate(
@@ -227,7 +207,7 @@
             transcendentals=12 * rows * rows,
         ),
         name="last_tile" if final else "first_tile",
-    )(scalars, gains, shifts, *images, *texts, *before)
+    )(scalars, gains, shifts, image, *texts, *before)
 
 
 def backward_kernel(firsts, feats_ref, gain_ref, shift_ref, scale_ref, *refs):
@@ -363,7 +343,7 @@
     y_pairs = routes.across_y()
     z_steps = routes.ring(1, 2)
     flat_steps = [routes.along(5, near), *routes.ring(None, 3), *routes.ring(4, 0)]
-    early_steps, middle_steps = flat_steps[:3], flat_steps[3:] + z_steps[:-2]
+    early_steps, middle_steps = flat_steps[:4], flat_steps[4:] + z_steps[:-2]
     late_steps = z_steps[-2:]
     group_rows = 2 * RING
 
@@ -375,13 +355,13 @@
         rows = image_feats.shape[1]
 
         text_z = send(text, text_pairs)
+        text_y = send(text, y_pairs)
         image_z = send(image, image_pairs)
-        text_y = send(text, y_pairs)
         text_zy = send(text_z, y_pairs)
-        images = [image, image_z]
-        text_part, text_z_part, *before = tile(scalars, gains, shifts, images, [text, text_z])
-        y_parts, image_part, image_z_part, loss_own, sums = tile(
-            scalars, gains, shifts, images, [text_y, text_zy], before
+        texts = [text, text_z, text_y, text_zy]
+        text_parts, image_part, loss_own, sums = tile(scalars, gains, shifts, image, texts)
+        text_part, text_z_part, y_parts, image_z_part, sums = tile(
+            scalars, gains, shifts, image_z, texts, [text_parts, sums]
         )
 
         image_back = send(image_z_part, image_pairs)

time: 184 us -> 166 us (0.902)
  the two profiles are of different devices: /device:TPU:28 before, /device:TPU:6 now
where the time goes in v4:
time: 166 us; the launch traced here: 164 us
  starting transfers between devices  85.4 us (51%)
  waiting for transfers between devices  47.8 us (29%)
  Pallas kernels  20.8 us (13%)
  local copies, waits for them, and re-layouts  6.52 us (4%)
  between operations  2.14 us (1%)
    ppermute x17, starting transfers between devices, send(): return lax.ppermute(value, AXES, pairs)  85.4 us
    ppermute x17, waiting for transfers between devices, send(): return lax.ppermute(value, AXES, pairs)  47.8 us
    pallas_call x2, Pallas kernels, tile(): pl.pallas_call(functools.partial(tile_kernel, final), out_shape=tuple(out...  8.31 us
    pallas_call x2, Pallas kernels, backward_norm(): pl.pallas_call(functools.partial(backward_kernel, firsts), out_shape=jax....  8.3 us
    unnamed x22, local copies, waits for them, and re-layouts  5.29 us
    pallas_call x1, Pallas kernels, forward_norms(): pl.pallas_call(forward_kernel, out_shape=(emb, emb), scratch_shapes=[pltp...  4.16 us
  transfers between devices with their start and end apart: 17, of which 13 were waited for; matrix products, arithmetic and copies ran while one was open for 1% of the time, Pallas kernels for 8%

profile of v4, /device:TPU:6, one launch (start us, length us, event | category | flops | bytes accessed | tf_op | source)
XLA Modules:
  0.0 164.2 jit_solution(12512295810778066483)
XLA Ops:
  0.6 4.2 %forward_norms.1 = (bf16[208,1152]{1,0:T(8,128)(2,1)}, bf16[208,1152]{1,0:T(8,128)(2,1)}) custom-call(bf16[192,1152]{1,0:T(8,128)(2,1)} %bitcast.5, bf16[192,1152]{1,0:T(8,128)(2,1)} %bitcast.7, f32[2,1152]{1,0:T(2,128)} %gains_ref.5, f32[2,1152]{1,0:T(2,128)} %shifts_ref.5), custom_call_target="tpu_custom_call" | custom-call | flops 8847360 | bytes 1769472 | tf_op jit(solution)/shard_map/forward_norms/pallas_call | solution.py:92
  4.8 18.2 %collective-permute-start.9 = (bf16[208,1152]{1,0:T(8,128)(2,1)}, bf16[208,1152]{1,0:T(8,128)(2,1)S(1)}, u32[]{:S(2)}, u32[]{:S(2)}) collective-permute-start(bf16[208,1152]{1,0:T(8,128)(2,1)} %get-tuple-element.60.refs_1_), channel_id=1, source_target_pairs={{0,384},{1,129},{2,386},{3,131},{4,388},{5,133},{6,390},{7,135},{8... | collective-permute-start | bytes 1437704 | tf_op jit(solution)/shard_map/ppermute | solution.py:328
  23.0 3.5 %collective-permute-start.10 = (bf16[208,1152]{1,0:T(8,128)(2,1)}, bf16[208,1152]{1,0:T(8,128)(2,1)S(1)}, u32[]{:S(2)}, u32[]{:S(2)}) collective-permute-start(bf16[208,1152]{1,0:T(8,128)(2,1)} %get-tuple-element.60.refs_1_), channel_id=1, source_target_pairs={{0,512},{1,513},{2,514},{3,515},{4,516},{5,517},{6,518},{7,519},{8... | collective-permute-start | bytes 1437704 | tf_op jit(solution)/shard_map/ppermute | solution.py:328
  26.5 18.6 %collective-permute-done.9.refs_2_ = bf16[208,1152]{1,0:T(8,128)(2,1)S(1)} collective-permute-done((bf16[208,1152]{1,0:T(8,128)(2,1)}, bf16[208,1152]{1,0:T(8,128)(2,1)S(1)}, u32[]{:S(2)}, u32[]{:S(2)}) %collective-permute-start.9) | collective-permute-done | bytes 479264 | tf_op jit(solution)/shard_map/ppermute | solution.py:328
  45.1 3.5 %collective-permute-start.11 = (bf16[208,1152]{1,0:T(8,128)(2,1)S(1)}, bf16[208,1152]{1,0:T(8,128)(2,1)S(1)}, u32[]{:S(2)}, u32[]{:S(2)}) collective-permute-start(bf16[208,1152]{1,0:T(8,128)(2,1)S(1)} %collective-permute-done.9.refs_2_), channel_id=1, source_target_pairs={{0,512},{1,513},{2,514},{3,515},{4,516},{5,517},{6,518},{7,519},{8... | collective-permute-start | bytes 1437704 | tf_op jit(solution)/shard_map/ppermute | solution.py:328
  48.6 3.4 %collective-permute-start.8 = (bf16[208,1152]{1,0:T(8,128)(2,1)}, bf16[208,1152]{1,0:T(8,128)(2,1)S(1)}, u32[]{:S(2)}, u32[]{:S(2)}) collective-permute-start(bf16[208,1152]{1,0:T(8,128)(2,1)} %get-tuple-element.59.refs_0_), channel_id=1, source_target_pairs={{0,128},{1,385},{2,130},{3,387},{4,132},{5,389},{6,134},{7,391},{8... | collective-permute-start | bytes 1437704 | tf_op jit(solution)/shard_map/ppermute | solution.py:328
  53.3 0.1 pad_maximum_fusion.scalars_ref
  53.4 0.0 collective-permute-done.10.refs_3_
  53.4 2.3 %collective-permute-done.11.refs_4_ = bf16[208,1152]{1,0:T(8,128)(2,1)S(1)} collective-permute-done((bf16[208,1152]{1,0:T(8,128)(2,1)S(1)}, bf16[208,1152]{1,0:T(8,128)(2,1)S(1)}, u32[]{:S(2)}, u32[]{:S(2)}) %collective-permute-start.11) | collective-permute-done | bytes 479264 | tf_op jit(solution)/shard_map/ppermute | solution.py:328
  55.7 0.0 copy-start.2
  55.7 1.0 copy-done.2
  56.7 0.0 copy-start.4
  56.7 0.7 copy-done.4
  57.4 0.0 copy-start.6
  57.4 0.7 copy-done.6
  58.1 1.0 copy-done.8
  59.1 4.0 %first_tile.1 = (f32[768,1152]{1,0:T(8,128)S(1)}, f32[192,1152]{1,0:T(8,128)S(1)}, f32[1,192]{1,0:T(1,128)S(1)}, f32[4,1152]{1,0:T(4,128)S(1)}) custom-call(f32[2]{0:T(128)S(1)} %pad_maximum_fusion.scalars_ref, f32[2,1152]{1,0:T(2,128)S(1)} %copy-done.6, f32[2,1152]{1,0:T(2,128)S(1)} %copy-done.4, bf16[208,1152]{1,0:T(8,128)(2,1)S(1)} %copy-done.8, ...), custom_call_target="tpu_custom_call" | custom-call | flops 1019215872 | bytes 5308416 | tf_op jit(solution)/shard_map/first_tile/pallas_call | solution.py:194
  63.2 0.0 copy-start.1
  63.2 0.9 copy-done.1
  64.1 7.8 %collective-permute-done.8.refs_0_ = bf16[208,1152]{1,0:T(8,128)(2,1)S(1)} collective-permute-done((bf16[208,1152]{1,0:T(8,128)(2,1)}, bf16[208,1152]{1,0:T(8,128)(2,1)S(1)}, u32[]{:S(2)}, u32[]{:S(2)}) %collective-permute-start.8) | collective-permute-done | bytes 479264 | tf_op jit(solution)/shard_map/ppermute | solution.py:328
  71.9 0.0 copy-done.3
  71.9 4.3 %last_tile.1 = (f32[192,1152]{1,0:T(8,128)S(1)}, f32[192,1152]{1,0:T(8,128)S(1)}, bf16[384,1152]{1,0:T(8,128)(2,1)S(1)}, bf16[208,1152]{1,0:T(8,128)(2,1)S(1)}, f32[4,1152]{1,0:T(4,128)S(1)}) custom-call(f32[2]{0:T(128)S(1)} %pad_maximum_fusion.scalars_ref, f32[2,1152]{1,0:T(2,128)S(1)} %copy-done.6, f32[2,1152]{1,0:T(2,128)S(1)} %copy-done.4, ...), custom_call_target="tpu_custom_call" | custom-call | flops 1019215872 | bytes 5308416 | tf_op jit(solution)/shard_map/last_tile/pallas_call | solution.py:194
  76.2 0.0 copy-start
  76.2 0.9 copy-done
  77.1 2.5 %collective-permute-start.12 = (bf16[384,1152]{1,0:T(8,128)(2,1)S(1)}, bf16[384,1152]{1,0:T(8,128)(2,1)S(1)}, u32[]{:S(2)}, u32[]{:S(2)}) collective-permute-start(bf16[384,1152]{1,0:T(8,128)(2,1)S(1)} %get-tuple-element.65), channel_id=1, source_target_pairs={{0,512},{1,513},{2,514},{3,515},{4,516},{5,517},{6,518},{7,519},{8... | collective-permute-start | bytes 2654216 | tf_op jit(solution)/shard_map/ppermute | solution.py:328
  79.6 3.9 %collective-permute-start.13 = (bf16[208,1152]{1,0:T(8,128)(2,1)S(1)}, bf16[208,1152]{1,0:T(8,128)(2,1)}, u32[]{:S(2)}, u32[]{:S(2)}) collective-permute-start(bf16[208,1152]{1,0:T(8,128)(2,1)S(1)} %get-tuple-element.68), channel_id=1, source_target_pairs={{0,128},{1,385},{2,130},{3,387},{4,132},{5,389},{6,134},{7,391},{8... | collective-permute-start | bytes 1437704 | tf_op jit(solution)/shard_map/ppermute | solution.py:328
  83.5 21.3 %while.20 = (s32[]{:T(128)}, f32[4,1152]{1,0:T(4,128)S(1)}, s32[]{:T(128)}, s32[]{:T(128)}) while((s32[]{:T(128)}, f32[4,1152]{1,0:T(4,128)S(1)}, s32[]{:T(128)}, s32[]{:T(128)}) %tuple.46), condition=%wide.region_1.2_spmd, body=%wide.region_0.1_spmd.sunk | while | flops 18434 | bytes 516309 | solution.py:338
  83.5 1.9 %collective-permute-start = (f32[4,1152]{1,0:T(4,128)S(1)}, f32[4,1152]{1,0:T(4,128)S(1)}, u32[]{:S(2)}, u32[]{:S(2)}) collective-permute-start(f32[4,1152]{1,0:T(4,128)S(1)} %get-tuple-element.144), channel_id=1, source_target_pairs={{0,1},{1,0},{2,3},{3,2},{4,5},{5,4},{6,7},{7,6},{8,9},{9,8},{10,11... | collective-permute-start | bytes 55304 | tf_op jit(solution)/shard_map/while/body/ppermute | solution.py:328
  85.5 1.2 collective-permute-done
  86.6 2.7 %collective-permute-start.1 = (f32[4,1152]{1,0:T(4,128)S(1)}, f32[4,1152]{1,0:T(4,128)S(1)}, u32[]{:S(2)}, u32[]{:S(2)}) collective-permute-start(f32[4,1152]{1,0:T(4,128)S(1)} %add.69), channel_id=1, source_target_pairs={{0,8},{1,9},{2,10},{3,11},{4,12},{5,13},{6,14},{7,15},{8,0},{9,1},... | collective-permute-start | bytes 55304 | tf_op jit(solution)/shard_map/while/body/ppermute | solution.py:328
  89.3 2.9 %collective-permute-done.1 = f32[4,1152]{1,0:T(4,128)S(1)} collective-permute-done((f32[4,1152]{1,0:T(4,128)S(1)}, f32[4,1152]{1,0:T(4,128)S(1)}, u32[]{:S(2)}, u32[]{:S(2)}) %collective-permute-start.1) | collective-permute-done | bytes 18464 | tf_op jit(solution)/shard_map/while/body/ppermute | solution.py:328
  92.3 2.3 %collective-permute-start.2 = (f32[4,1152]{1,0:T(4,128)S(1)}, f32[4,1152]{1,0:T(4,128)S(1)}, u32[]{:S(2)}, u32[]{:S(2)}) collective-permute-start(f32[4,1152]{1,0:T(4,128)S(1)} %add.70), channel_id=1, source_target_pairs={{0,24},{1,25},{2,26},{3,27},{4,28},{5,29},{6,30},{7,31},{8,16},{9,... | collective-permute-start | bytes 55304 | tf_op jit(solution)/shard_map/while/body/ppermute | solution.py:328
  94.6 4.5 %collective-permute-done.2 = f32[4,1152]{1,0:T(4,128)S(1)} collective-permute-done((f32[4,1152]{1,0:T(4,128)S(1)}, f32[4,1152]{1,0:T(4,128)S(1)}, u32[]{:S(2)}, u32[]{:S(2)}) %collective-permute-start.2) | collective-permute-done | bytes 18464 | tf_op jit(solution)/shard_map/while/body/ppermute | solution.py:328
  99.1 3.5 %collective-permute-start.3 = (f32[4,1152]{1,0:T(4,128)S(1)}, f32[4,1152]{1,0:T(4,128)S(1)}, u32[]{:S(2)}, u32[]{:S(2)}) collective-permute-start(f32[4,1152]{1,0:T(4,128)S(1)} %add.71), channel_id=1, source_target_pairs={{0,512},{1,513},{2,514},{3,515},{4,516},{5,517},{6,518},{7,519},{8... | collective-permute-start | bytes 55304 | tf_op jit(solution)/shard_map/while/body/ppermute | solution.py:328
  102.6 2.2 %collective-permute-done.3 = f32[4,1152]{1,0:T(4,128)S(1)} collective-permute-done((f32[4,1152]{1,0:T(4,128)S(1)}, f32[4,1152]{1,0:T(4,128)S(1)}, u32[]{:S(2)}, u32[]{:S(2)}) %collective-permute-start.3) | collective-permute-done | bytes 18464 | tf_op jit(solution)/shard_map/while/body/ppermute | solution.py:328
  104.8 0.0 collective-permute-done.12.refs_1_
  104.8 0.0 copy-start.9
  104.8 0.1 add_convert_fusion
  104.9 7.1 %collective-permute-start.14 = (bf16[192,1152]{1,0:T(8,128)(2,1)S(1)}, bf16[192,1152]{1,0:T(8,128)(2,1)S(1)}, u32[]{:S(2)}, u32[]{:S(2)}) collective-permute-start(bf16[192,1152]{1,0:T(8,128)(2,1)S(1)} %add_convert_fusion), channel_id=1, source_target_pairs={{0,384},{1,129},{2,386},{3,131},{4,388},{5,133},{6,390},{7,135},{8... | collective-permute-start | bytes 1327112 | tf_op jit(solution)/shard_map/ppermute | solution.py:328
  112.0 0.0 collective-permute-done.13.refs_1_
  112.0 32.5 %while.21 = (s32[]{:T(128)}, f32[4,1152]{1,0:T(4,128)S(1)}, s32[]{:T(128)}, s32[]{:T(128)}) while((s32[]{:T(128)}, f32[4,1152]{1,0:T(4,128)S(1)}, s32[]{:T(128)}, s32[]{:T(128)}) %tuple.49), condition=%wide.region_3.4_spmd, body=%wide.region_2.3_spmd.sunk | while | flops 18434 | bytes 516309 | solution.py:338
  112.0 5.4 %collective-permute-start.4 = (f32[4,1152]{1,0:T(4,128)S(1)}, f32[4,1152]{1,0:T(4,128)S(1)}, u32[]{:S(2)}, u32[]{:S(2)}) collective-permute-start(f32[4,1152]{1,0:T(4,128)S(1)} %get-tuple-element.156), channel_id=1, source_target_pairs={{0,518},{1,519},{2,512},{3,513},{4,514},{5,515},{6,516},{7,517},{8... | collective-permute-start | bytes 55304 | tf_op jit(solution)/shard_map/while/body/ppermute | solution.py:328
  117.4 1.7 %collective-permute-done.4 = f32[4,1152]{1,0:T(4,128)S(1)} collective-permute-done((f32[4,1152]{1,0:T(4,128)S(1)}, f32[4,1152]{1,0:T(4,128)S(1)}, u32[]{:S(2)}, u32[]{:S(2)}) %collective-permute-start.4) | collective-permute-done | bytes 18464 | tf_op jit(solution)/shard_map/while/body/ppermute | solution.py:328
  119.1 5.3 %collective-permute-start.5 = (f32[4,1152]{1,0:T(4,128)S(1)}, f32[4,1152]{1,0:T(4,128)S(1)}, u32[]{:S(2)}, u32[]{:S(2)}) collective-permute-start(f32[4,1152]{1,0:T(4,128)S(1)} %add.74), channel_id=1, source_target_pairs={{0,514},{1,515},{2,516},{3,517},{4,518},{5,519},{6,512},{7,513},{8... | collective-permute-start | bytes 55304 | tf_op jit(solution)/shard_map/while/body/ppermute | solution.py:328
  124.4 2.2 %collective-permute-done.5 = f32[4,1152]{1,0:T(4,128)S(1)} collective-permute-done((f32[4,1152]{1,0:T(4,128)S(1)}, f32[4,1152]{1,0:T(4,128)S(1)}, u32[]{:S(2)}, u32[]{:S(2)}) %collective-permute-start.5) | collective-permute-done | bytes 18464 | tf_op jit(solution)/shard_map/while/body/ppermute | solution.py:328
  126.6 4.7 %collective-permute-start.6 = (f32[4,1152]{1,0:T(4,128)S(1)}, f32[4,1152]{1,0:T(4,128)S(1)}, u32[]{:S(2)}, u32[]{:S(2)}) collective-permute-start(f32[4,1152]{1,0:T(4,128)S(1)} %add.75), channel_id=1, source_target_pairs={{0,32},{1,33},{2,34},{3,35},{4,36},{5,37},{6,38},{7,39},{8,40},{9,... | collective-permute-start | bytes 55304 | tf_op jit(solution)/shard_map/while/body/ppermute | solution.py:328
  131.3 1.7 %collective-permute-done.6 = f32[4,1152]{1,0:T(4,128)S(1)} collective-permute-done((f32[4,1152]{1,0:T(4,128)S(1)}, f32[4,1152]{1,0:T(4,128)S(1)}, u32[]{:S(2)}, u32[]{:S(2)}) %collective-permute-start.6) | collective-permute-done | bytes 18464 | tf_op jit(solution)/shard_map/while/body/ppermute | solution.py:328
  133.0 9.7 %collective-permute-start.7 = (f32[4,1152]{1,0:T(4,128)S(1)}, f32[4,1152]{1,0:T(4,128)S(1)}, u32[]{:S(2)}, u32[]{:S(2)}) collective-permute-start(f32[4,1152]{1,0:T(4,128)S(1)} %add.76), channel_id=1, source_target_pairs={{0,480},{1,481},{2,482},{3,483},{4,484},{5,485},{6,486},{7,487},{8... | collective-permute-start | bytes 55304 | tf_op jit(solution)/shard_map/while/body/ppermute | solution.py:328
  142.8 1.7 %collective-permute-done.7 = f32[4,1152]{1,0:T(4,128)S(1)} collective-permute-done((f32[4,1152]{1,0:T(4,128)S(1)}, f32[4,1152]{1,0:T(4,128)S(1)}, u32[]{:S(2)}, u32[]{:S(2)}) %collective-permute-start.7) | collective-permute-done | bytes 18464 | tf_op jit(solution)/shard_map/while/body/ppermute | solution.py:328
  144.5 0.0 collective-permute-done.14.refs_2_
  144.5 0.0 copy-start.10
  144.5 1.9 %collective-permute-start.15 = (f32[4,1152]{1,0:T(4,128)S(1)}, f32[4,1152]{1,0:T(4,128)S(1)}, u32[]{:S(2)}, u32[]{:S(2)}) collective-permute-start(f32[4,1152]{1,0:T(4,128)S(1)} %get-tuple-element.71), channel_id=1, source_target_pairs={{0,96},{1,97},{2,98},{3,99},{4,100},{5,101},{6,102},{7,103},{8,104... | collective-permute-start | bytes 55304 | tf_op jit(solution)/shard_map/ppermute | solution.py:328
  146.4 0.0 copy-done.5
  146.4 0.0 copy-done.7
  146.5 0.6 fusion.1
  147.1 4.0 %backward_norm.2 = bf16[192,1152]{1,0:T(8,128)(2,1)} custom-call(bf16[192,1152]{1,0:T(8,128)(2,1)} %bitcast.6, f32[1,1152]{1,0:T(1,128)} %get-tuple-element.97.gain_ref, f32[1,1152]{1,0:T(1,128)} %get-tuple-element.94.shift_ref, f32[1]{0:T(128)S(6)} %exp.3.scale_ref, f32[192,1152]{1,0:T(8,128)} %copy-done.1, bf16[208,1152]{1,0:T(8,128)(2,1)} %collective-permute-done.13.refs_1_), custom_call_target="tpu_custom_call" | custom-call | flops 8847360 | bytes 2654208 | tf_op jit(solution)/shard_map/backward_norm/pallas_call | solution.py:240
  151.1 0.9 collective-permute-done.15
  152.0 6.0 %collective-permute-start.16 = (f32[4,1152]{1,0:T(4,128)S(1)}, f32[4,1152]{1,0:T(4,128)S(1)}, u32[]{:S(2)}, u32[]{:S(2)}) collective-permute-start(f32[4,1152]{1,0:T(4,128)S(1)} %add.49), channel_id=1, source_target_pairs={{0,352},{1,353},{2,354},{3,355},{4,356},{5,357},{6,358},{7,359},{8... | collective-permute-start | bytes 55304 | tf_op jit(solution)/shard_map/ppermute | solution.py:328
  158.0 1.3 add_multiply_fusion
  159.2 0.0 copy-done.9
  159.2 0.0 copy-done.10
  159.2 4.3 %backward_norm.3 = bf16[192,1152]{1,0:T(8,128)(2,1)} custom-call(bf16[192,1152]{1,0:T(8,128)(2,1)} %bitcast.8, f32[1,1152]{1,0:T(1,128)} %get-tuple-element.98.gain_ref, f32[1,1152]{1,0:T(1,128)} %get-tuple-element.93.shift_ref, f32[1]{0:T(128)S(6)} %exp.3.scale_ref, f32[192,1152]{1,0:T(8,128)} %copy-done, bf16[384,1152]{1,0:T(8,128)(2,1)} %copy-done.9, ...), custom_call_target="tpu_custom_call" | custom-call | flops 8847360 | bytes 2654208 | tf_op jit(solution)/shard_map/backward_norm/pallas_call | solution.py:240
  163.5 0.1 collective-permute-done.16
  163.6 0.6 fusion
  (14 shorter events, 0.1 us)
Async XLA Ops:
  4.8 40.3 %collective-permute-start.9 = (bf16[208,1152]{1,0:T(8,128)(2,1)}, bf16[208,1152]{1,0:T(8,128)(2,1)S(1)}, u32[]{:S(2)}, u32[]{:S(2)}) collective-permute-start(bf16[208,1152]{1,0:T(8,128)(2,1)} %get-tuple-element.60.refs_1_), channel_id=1, source_target_pairs={{0,384},{1,129},{2,386},{3,131},{4,388},{5,133},{6,390},{7,135},{8... | collective-permute-start | bytes 1437704 | tf_op jit(solution)/shard_map/ppermute | solution.py:328
  23.0 30.4 %collective-permute-start.10 = (bf16[208,1152]{1,0:T(8,128)(2,1)}, bf16[208,1152]{1,0:T(8,128)(2,1)S(1)}, u32[]{:S(2)}, u32[]{:S(2)}) collective-permute-start(bf16[208,1152]{1,0:T(8,128)(2,1)} %get-tuple-element.60.refs_1_), channel_id=1, source_target_pairs={{0,512},{1,513},{2,514},{3,515},{4,516},{5,517},{6,518},{7,519},{8... | collective-permute-start | bytes 1437704 | tf_op jit(solution)/shard_map/ppermute | solution.py:328
  45.1 10.6 %collective-permute-start.11 = (bf16[208,1152]{1,0:T(8,128)(2,1)S(1)}, bf16[208,1152]{1,0:T(8,128)(2,1)S(1)}, u32[]{:S(2)}, u32[]{:S(2)}) collective-permute-start(bf16[208,1152]{1,0:T(8,128)(2,1)S(1)} %collective-permute-done.9.refs_2_), channel_id=1, source_target_pairs={{0,512},{1,513},{2,514},{3,515},{4,516},{5,517},{6,518},{7,519},{8... | collective-permute-start | bytes 1437704 | tf_op jit(solution)/shard_map/ppermute | solution.py:328
  48.6 23.3 %collective-permute-start.8 = (bf16[208,1152]{1,0:T(8,128)(2,1)}, bf16[208,1152]{1,0:T(8,128)(2,1)S(1)}, u32[]{:S(2)}, u32[]{:S(2)}) collective-permute-start(bf16[208,1152]{1,0:T(8,128)(2,1)} %get-tuple-element.59.refs_0_), channel_id=1, source_target_pairs={{0,128},{1,385},{2,130},{3,387},{4,132},{5,389},{6,134},{7,391},{8... | collective-permute-start | bytes 1437704 | tf_op jit(solution)/shard_map/ppermute | solution.py:328
  55.7 1.0 copy-start.2
  56.7 0.7 copy-start.4
  57.4 0.7 copy-start.6
  58.1 1.0 copy-start.8
  59.1 12.8 %copy-start.3 = (bf16[208,1152]{1,0:T(8,128)(2,1)S(1)}, bf16[208,1152]{1,0:T(8,128)(2,1)}, u32[]{:S(2)}) copy-start(bf16[208,1152]{1,0:T(8,128)(2,1)} %get-tuple-element.60.refs_1_) | copy-start | bytes 1437700
  63.2 0.9 copy-start.1
  76.2 0.9 copy-start
  77.1 69.3 %copy-start.5 = (f32[2,1152]{1,0:T(2,128)S(1)}, f32[2,1152]{1,0:T(2,128)}, u32[]{:S(2)}) copy-start(f32[2,1152]{1,0:T(2,128)} %shifts_ref.5) | copy-start | bytes 27652
  77.1 69.3 %copy-start.7 = (f32[2,1152]{1,0:T(2,128)S(1)}, f32[2,1152]{1,0:T(2,128)}, u32[]{:S(2)}) copy-start(f32[2,1152]{1,0:T(2,128)} %gains_ref.5) | copy-start | bytes 27652
  77.1 27.7 %collective-permute-start.12 = (bf16[384,1152]{1,0:T(8,128)(2,1)S(1)}, bf16[384,1152]{1,0:T(8,128)(2,1)S(1)}, u32[]{:S(2)}, u32[]{:S(2)}) collective-permute-start(bf16[384,1152]{1,0:T(8,128)(2,1)S(1)} %get-tuple-element.65), channel_id=1, source_target_pairs={{0,512},{1,513},{2,514},{3,515},{4,516},{5,517},{6,518},{7,519},{8... | collective-permute-start | bytes 2654216 | tf_op jit(solution)/shard_map/ppermute | solution.py:328
  79.6 32.4 %collective-permute-start.13 = (bf16[208,1152]{1,0:T(8,128)(2,1)S(1)}, bf16[208,1152]{1,0:T(8,128)(2,1)}, u32[]{:S(2)}, u32[]{:S(2)}) collective-permute-start(bf16[208,1152]{1,0:T(8,128)(2,1)S(1)} %get-tuple-element.68), channel_id=1, source_target_pairs={{0,128},{1,385},{2,130},{3,387},{4,132},{5,389},{6,134},{7,391},{8... | collective-permute-start | bytes 1437704 | tf_op jit(solution)/shard_map/ppermute | solution.py:328
  83.5 3.1 %collective-permute-start = (f32[4,1152]{1,0:T(4,128)S(1)}, f32[4,1152]{1,0:T(4,128)S(1)}, u32[]{:S(2)}, u32[]{:S(2)}) collective-permute-start(f32[4,1152]{1,0:T(4,128)S(1)} %get-tuple-element.144), channel_id=1, source_target_pairs={{0,1},{1,0},{2,3},{3,2},{4,5},{5,4},{6,7},{7,6},{8,9},{9,8},{10,11... | collective-permute-start | bytes 55304 | tf_op jit(solution)/shard_map/while/body/ppermute | solution.py:328
  86.6 5.6 %collective-permute-start.1 = (f32[4,1152]{1,0:T(4,128)S(1)}, f32[4,1152]{1,0:T(4,128)S(1)}, u32[]{:S(2)}, u32[]{:S(2)}) collective-permute-start(f32[4,1152]{1,0:T(4,128)S(1)} %add.69), channel_id=1, source_target_pairs={{0,8},{1,9},{2,10},{3,11},{4,12},{5,13},{6,14},{7,15},{8,0},{9,1},... | collective-permute-start | bytes 55304 | tf_op jit(solution)/shard_map/while/body/ppermute | solution.py:328
  92.3 6.9 %collective-permute-start.2 = (f32[4,1152]{1,0:T(4,128)S(1)}, f32[4,1152]{1,0:T(4,128)S(1)}, u32[]{:S(2)}, u32[]{:S(2)}) collective-permute-start(f32[4,1152]{1,0:T(4,128)S(1)} %add.70), channel_id=1, source_target_pairs={{0,24},{1,25},{2,26},{3,27},{4,28},{5,29},{6,30},{7,31},{8,16},{9,... | collective-permute-start | bytes 55304 | tf_op jit(solution)/shard_map/while/body/ppermute | solution.py:328
  99.1 5.6 %collective-permute-start.3 = (f32[4,1152]{1,0:T(4,128)S(1)}, f32[4,1152]{1,0:T(4,128)S(1)}, u32[]{:S(2)}, u32[]{:S(2)}) collective-permute-start(f32[4,1152]{1,0:T(4,128)S(1)} %add.71), channel_id=1, source_target_pairs={{0,512},{1,513},{2,514},{3,515},{4,516},{5,517},{6,518},{7,519},{8... | collective-permute-start | bytes 55304 | tf_op jit(solution)/shard_map/while/body/ppermute | solution.py:328
  104.8 54.5 %copy-start.9 = (bf16[384,1152]{1,0:T(8,128)(2,1)}, bf16[384,1152]{1,0:T(8,128)(2,1)S(1)}, u32[]{:S(2)}) copy-start(bf16[384,1152]{1,0:T(8,128)(2,1)S(1)} %collective-permute-done.12.refs_1_) | copy-start | bytes 2654212
  104.9 39.6 %collective-permute-start.14 = (bf16[192,1152]{1,0:T(8,128)(2,1)S(1)}, bf16[192,1152]{1,0:T(8,128)(2,1)S(1)}, u32[]{:S(2)}, u32[]{:S(2)}) collective-permute-start(bf16[192,1152]{1,0:T(8,128)(2,1)S(1)} %add_convert_fusion), channel_id=1, source_target_pairs={{0,384},{1,129},{2,386},{3,131},{4,388},{5,133},{6,390},{7,135},{8... | collective-permute-start | bytes 1327112 | tf_op jit(solution)/shard_map/ppermute | solution.py:328
  112.0 7.1 %collective-permute-start.4 = (f32[4,1152]{1,0:T(4,128)S(1)}, f32[4,1152]{1,0:T(4,128)S(1)}, u32[]{:S(2)}, u32[]{:S(2)}) collective-permute-start(f32[4,1152]{1,0:T(4,128)S(1)} %get-tuple-element.156), channel_id=1, source_target_pairs={{0,518},{1,519},{2,512},{3,513},{4,514},{5,515},{6,516},{7,517},{8... | collective-permute-start | bytes 55304 | tf_op jit(solution)/shard_map/while/body/ppermute | solution.py:328
  119.1 7.4 %collective-permute-start.5 = (f32[4,1152]{1,0:T(4,128)S(1)}, f32[4,1152]{1,0:T(4,128)S(1)}, u32[]{:S(2)}, u32[]{:S(2)}) collective-permute-start(f32[4,1152]{1,0:T(4,128)S(1)} %add.74), channel_id=1, source_target_pairs={{0,514},{1,515},{2,516},{3,517},{4,518},{5,519},{6,512},{7,513},{8... | collective-permute-start | bytes 55304 | tf_op jit(solution)/shard_map/while/body/ppermute | solution.py:328
  126.6 6.4 %collective-permute-start.6 = (f32[4,1152]{1,0:T(4,128)S(1)}, f32[4,1152]{1,0:T(4,128)S(1)}, u32[]{:S(2)}, u32[]{:S(2)}) collective-permute-start(f32[4,1152]{1,0:T(4,128)S(1)} %add.75), channel_id=1, source_target_pairs={{0,32},{1,33},{2,34},{3,35},{4,36},{5,37},{6,38},{7,39},{8,40},{9,... | collective-permute-start | bytes 55304 | tf_op jit(solution)/shard_map/while/body/ppermute | solution.py:328
  133.0 11.5 %collective-permute-start.7 = (f32[4,1152]{1,0:T(4,128)S(1)}, f32[4,1152]{1,0:T(4,128)S(1)}, u32[]{:S(2)}, u32[]{:S(2)}) collective-permute-start(f32[4,1152]{1,0:T(4,128)S(1)} %add.76), channel_id=1, source_target_pairs={{0,480},{1,481},{2,482},{3,483},{4,484},{5,485},{6,486},{7,487},{8... | collective-permute-start | bytes 55304 | tf_op jit(solution)/shard_map/while/body/ppermute | solution.py:328
  144.5 14.7 %copy-start.10 = (bf16[192,1152]{1,0:T(8,128)(2,1)}, bf16[192,1152]{1,0:T(8,128)(2,1)S(1)}, u32[]{:S(2)}) copy-start(bf16[192,1152]{1,0:T(8,128)(2,1)S(1)} %collective-permute-done.14.refs_2_) | copy-start | bytes 1327108
  144.5 7.5 %collective-permute-start.15 = (f32[4,1152]{1,0:T(4,128)S(1)}, f32[4,1152]{1,0:T(4,128)S(1)}, u32[]{:S(2)}, u32[]{:S(2)}) collective-permute-start(f32[4,1152]{1,0:T(4,128)S(1)} %get-tuple-element.71), channel_id=1, source_target_pairs={{0,96},{1,97},{2,98},{3,99},{4,100},{5,101},{6,102},{7,103},{8,104... | collective-permute-start | bytes 55304 | tf_op jit(solution)/shard_map/ppermute | solution.py:328
  152.0 11.7 %collective-permute-start.16 = (f32[4,1152]{1,0:T(4,128)S(1)}, f32[4,1152]{1,0:T(4,128)S(1)}, u32[]{:S(2)}, u32[]{:S(2)}) collective-permute-start(f32[4,1152]{1,0:T(4,128)S(1)} %add.49), channel_id=1, source_target_pairs={{0,352},{1,353},{2,354},{3,355},{4,356},{5,357},{6,358},{7,359},{8... | collective-permute-start | bytes 55304 | tf_op jit(solution)/shard_map/ppermute | solution.py:328

commit v5 on v4

--- a/solution.py
+++ b/solution.py
@@ -211,7 +211,15 @@
 
 
 def backward_kernel(firsts, feats_ref, gain_ref, shift_ref, scale_ref, *refs):
-    *part_refs, grad_ref = refs
+    count = len(firsts)
+    part_refs = refs[:count]
+    if len(refs) > count + 1:
+        loss_ref, grad_ref, mean_ref = refs[count:]
+        rows = loss_ref.shape[1]
+        losses = loss_ref[...] + get_line(part_refs[-1][rows:, :], rows)
+        mean_ref[...] = losses / (2 * RING * rows)
+    else:
+        grad_ref = refs[count]
 
     @pl.loop(0, feats_ref.shape[0] // ROW_BLOCK, unroll=UNROLL)
     def _(step):
@@ -232,22 +240,26 @@
         grad_ref[rows, :] = pulled.astype(jnp.bfloat16)
 
 
-def backward_norm(feats, gain, shift, scale, parts):
+def backward_norm(feats, gain, shift, scale, parts, loss=None):
     rows, width = feats.shape
     firsts = [first for first, _ in parts]
-    parts = [part for _, part in parts]
+    values = [part for _, part in parts]
     whole = pl.BlockSpec(memory_space=pltpu.VMEM)
+    out_shape = (jax.ShapeDtypeStruct((rows, width), jnp.bfloat16),)
+    if loss is not None:
+        values.append(loss)
+        out_shape += (jax.ShapeDtypeStruct((1, rows), jnp.float32),)
     return pl.pallas_call(
         functools.partial(backward_kernel, firsts),
-        out_shape=jax.ShapeDtypeStruct((rows, width), jnp.bfloat16),
-        in_specs=[whole] * 3 + [pl.BlockSpec(memory_space=pltpu.SMEM)] + [whole] * len(parts),
-        out_specs=whole,
+        out_shape=out_shape,
+        in_specs=[whole] * 3 + [pl.BlockSpec(memory_space=pltpu.SMEM)] + [whole] * len(values),
+        out_specs=(whole,) * len(out_shape),
         compiler_params=pltpu.CompilerParams(vmem_limit_bytes=VMEM_LIMIT),
         cost_estimate=pl.CostEstimate(
             flops=40 * rows * width, bytes_accessed=12 * rows * width, transcendentals=0
         ),
         name="backward_norm",
-    )(feats, gain, shift, scale, *parts)
+    )(feats, gain, shift, scale, *values)
 
 
 def near(place):
@@ -328,14 +340,18 @@
     return lax.ppermute(value, AXES, pairs)
 
 
-def sum_over(value, steps, turns):
-    def one(carry):
-        turn, value = carry
-        for pairs in steps:
-            value = value + send(value, pairs)
-        return turn + 1, value
-
-    return lax.while_loop(lambda carry: carry[0] < turns, one, (jnp.int32(0), value))[1]
+def once(step, value, turns):
+    return lax.while_loop(
+        lambda carry: carry[0] < turns,
+        lambda carry: (carry[0] + 1, step(carry[1])),
+        (jnp.int32(0), value),
+    )[1]
+
+
+def sum_over(value, steps):
+    for pairs in steps:
+        value = value + send(value, pairs)
+    return value
 
 
 def make_body(routes):
@@ -345,7 +361,6 @@
     flat_steps = [routes.along(5, near), *routes.ring(None, 3), *routes.ring(4, 0)]
     early_steps, middle_steps = flat_steps[:4], flat_steps[4:] + z_steps[:-2]
     late_steps = z_steps[-2:]
-    group_rows = 2 * RING
 
     def body(image_feats, text_feats, gains, shifts, log_scale, logit_bias):
         scale = jnp.exp(log_scale)
@@ -356,8 +371,9 @@
 
         text_z = send(text, text_pairs)
         text_y = send(text, y_pairs)
-        image_z = send(image, image_pairs)
-        text_zy = send(text_z, y_pairs)
+        image_late, text_z = lax.optimization_barrier((image, text_z))
+        image_z = send(image_late, image_pairs)
+        text_zy = once(lambda block: send(block, y_pairs), text_z, turns)
         texts = [text, text_z, text_y, text_zy]
         text_parts, image_part, loss_own, sums = tile(scalars, gains, shifts, image, texts)
         text_part, text_z_part, y_parts, image_z_part, sums = tile(
@@ -366,28 +382,31 @@
 
         image_back = send(image_z_part, image_pairs)
         y_back = send(y_parts, y_pairs)
-        sums = sum_over(sums, early_steps, turns)
+        sums = once(lambda value: sum_over(value, early_steps), sums, turns)
         sums, y_back = lax.optimization_barrier((sums, y_back))
         text_z_sum = text_z_part + y_back[:rows].astype(jnp.float32)
         text_z_back = send(text_z_sum.astype(jnp.bfloat16), text_pairs)
-        sums = sum_over(sums, middle_steps, turns)
+        sums = once(lambda value: sum_over(value, middle_steps), sums, turns)
         sums, image_back, text_z_back = lax.optimization_barrier((sums, image_back, text_z_back))
-        image_grad = backward_norm(
-            image_feats[0], gains[:1], shifts[:1], scale, [(0, image_part), (0, image_back)]
+        image_grad, row_mean = backward_norm(
+            image_feats[0],
+            gains[:1],
+            shifts[:1],
+            scale,
+            [(0, image_part), (0, image_back)],
+            loss_own,
         )
         sums = sums + send(sums, late_steps[0])
         sums, image_grad = lax.optimization_barrier((sums, image_grad))
         for pairs in late_steps[1:]:
             sums = sums + send(sums, pairs)
-        text_grad = backward_norm(
+        (text_grad,) = backward_norm(
             text_feats[0],
             gains[1:],
             shifts[1:],
             scale,
             [(0, text_part), (rows, y_back), (0, text_z_back)],
         )
-
-        row_mean = (loss_own + get_line(image_back[rows:], rows)) / (group_rows * rows)
         return (image_grad[None], text_grad[None], sums[:2], sums[2:], row_mean)
 
     return body

time: 166 us -> 162 us (0.976)
  starting transfers between devices: 85.4 us -> 80.4 us
  waiting for transfers between devices: 47.8 us -> 51.5 us
  local copies, waits for them, and re-layouts: 6.52 us -> 4.73 us
    ppermute x17, starting transfers between devices: 85.4 us -> 80.4 us  [send(): return lax.ppermute(value, AXES, pairs)]
    ppermute x17, waiting for transfers between devices: 47.8 us -> 51.5 us  [send(): return lax.ppermute(value, AXES, pairs)]
    unnamed x22 -> x23, local copies, waits for them, and re-layouts: 5.29 us -> 2.7 us
  transfers between devices with their start and end apart: 17 -> 17, of which waited for: 13 -> 11; matrix products, arithmetic and copies ran while one was open for 1% -> 2% of each run, Pallas kernels for 8% -> 8%
where the time goes in v5:
time: 162 us; the launch traced here: 161 us
  starting transfers between devices  80.4 us (50%)
  waiting for transfers between devices  51.5 us (32%)
  Pallas kernels  21.9 us (14%)
  local copies, waits for them, and re-layouts  4.73 us (3%)
  between operations  2.17 us (1%)
    ppermute x17, starting transfers between devices, send(): return lax.ppermute(value, AXES, pairs)  80.4 us
    ppermute x17, waiting for transfers between devices, send(): return lax.ppermute(value, AXES, pairs)  51.5 us
    pallas_call x2, Pallas kernels, tile(): pl.pallas_call(functools.partial(tile_kernel, final), out_shape=tuple(out...  9.47 us
    pallas_call x2, Pallas kernels, backward_norm(): pl.pallas_call(functools.partial(backward_kernel, firsts), out_shape=out_...  8.32 us
    pallas_call x1, Pallas kernels, forward_norms(): pl.pallas_call(forward_kernel, out_shape=(emb, emb), scratch_shapes=[pltp...  4.12 us
  transfers between devices with their start and end apart: 17, of which 11 were waited for; matrix products, arithmetic and copies ran while one was open for 2% of the time, Pallas kernels for 8%

profile of v5, /device:TPU:6, one launch (start us, length us, event | category | flops | bytes accessed | tf_op | source)
XLA Modules:
  0.0 161.0 jit_solution(1896347434901537965)
XLA Ops:
  0.6 0.0 copy-start.4
  0.6 0.0 copy-start.3
  0.7 4.1 %forward_norms.1 = (bf16[208,1152]{1,0:T(8,128)(2,1)}, bf16[208,1152]{1,0:T(8,128)(2,1)}) custom-call(bf16[192,1152]{1,0:T(8,128)(2,1)} %bitcast.5, bf16[192,1152]{1,0:T(8,128)(2,1)} %bitcast.7, f32[2,1152]{1,0:T(2,128)} %gains_ref.5, f32[2,1152]{1,0:T(2,128)} %shifts_ref.5), custom_call_target="tpu_custom_call" | custom-call | flops 8847360 | bytes 1769472 | tf_op jit(solution)/shard_map/forward_norms/pallas_call | solution.py:92
  4.8 18.3 %collective-permute-start.9 = (bf16[208,1152]{1,0:T(8,128)(2,1)}, bf16[208,1152]{1,0:T(8,128)(2,1)S(1)}, u32[]{:S(2)}, u32[]{:S(2)}) collective-permute-start(bf16[208,1152]{1,0:T(8,128)(2,1)} %get-tuple-element.82.refs_1_), channel_id=1, source_target_pairs={{0,384},{1,129},{2,386},{3,131},{4,388},{5,133},{6,390},{7,135},{8... | collective-permute-start | bytes 1437704 | tf_op jit(solution)/shard_map/ppermute | solution.py:340
  23.1 3.5 %collective-permute-start.11 = (bf16[208,1152]{1,0:T(8,128)(2,1)}, bf16[208,1152]{1,0:T(8,128)(2,1)S(1)}, u32[]{:S(2)}, u32[]{:S(2)}) collective-permute-start(bf16[208,1152]{1,0:T(8,128)(2,1)} %get-tuple-element.82.refs_1_), channel_id=1, source_target_pairs={{0,512},{1,513},{2,514},{3,515},{4,516},{5,517},{6,518},{7,519},{8... | collective-permute-start | bytes 1437704 | tf_op jit(solution)/shard_map/ppermute | solution.py:340
  26.6 18.6 %collective-permute-done.9.refs_2_ = bf16[208,1152]{1,0:T(8,128)(2,1)S(1)} collective-permute-done((bf16[208,1152]{1,0:T(8,128)(2,1)}, bf16[208,1152]{1,0:T(8,128)(2,1)S(1)}, u32[]{:S(2)}, u32[]{:S(2)}) %collective-permute-start.9) | collective-permute-done | bytes 479264 | tf_op jit(solution)/shard_map/ppermute | solution.py:340
  45.2 3.4 %collective-permute-start.10 = (bf16[208,1152]{1,0:T(8,128)(2,1)}, bf16[208,1152]{1,0:T(8,128)(2,1)S(1)}, u32[]{:S(2)}, u32[]{:S(2)}) collective-permute-start(bf16[208,1152]{1,0:T(8,128)(2,1)} %get-tuple-element.83.refs_0_), channel_id=1, source_target_pairs={{0,128},{1,385},{2,130},{3,387},{4,132},{5,389},{6,134},{7,391},{8... | collective-permute-start | bytes 1437704 | tf_op jit(solution)/shard_map/ppermute | solution.py:340
  49.9 0.1 pad_maximum_fusion.scalars_ref
  50.0 0.8 copy.12
  50.8 14.4 %while.30 = (s32[]{:T(128)}, bf16[208,1152]{1,0:T(8,128)(2,1)}, s32[]{:T(128)}, s32[]{:T(128)}) while((s32[]{:T(128)}, bf16[208,1152]{1,0:T(8,128)(2,1)}, s32[]{:T(128)}, s32[]{:T(128)}) %tuple.61), condition=%wide.region_1.2_spmd, body=%wide.region_0.1_spmd.sunk | while | flops 2 | bytes 2875485 | solution.py:344
  50.8 3.5 %collective-permute-start = (bf16[208,1152]{1,0:T(8,128)(2,1)}, bf16[208,1152]{1,0:T(8,128)(2,1)S(1)}, u32[]{:S(2)}, u32[]{:S(2)}) collective-permute-start(bf16[208,1152]{1,0:T(8,128)(2,1)} %get-tuple-element.197), channel_id=1, source_target_pairs={{0,512},{1,513},{2,514},{3,515},{4,516},{5,517},{6,518},{7,519},{8... | collective-permute-start | bytes 1437704 | tf_op jit(solution)/shard_map/while/body/ppermute | solution.py:340
  54.3 10.2 %collective-permute-done = bf16[208,1152]{1,0:T(8,128)(2,1)S(1)} collective-permute-done((bf16[208,1152]{1,0:T(8,128)(2,1)}, bf16[208,1152]{1,0:T(8,128)(2,1)S(1)}, u32[]{:S(2)}, u32[]{:S(2)}) %collective-permute-start) | collective-permute-done | bytes 479264 | tf_op jit(solution)/shard_map/while/body/ppermute | solution.py:340
  64.5 0.8 copy.16
  65.3 0.0 collective-permute-done.11.refs_3_
  65.3 0.0 copy-done.4
  65.3 0.0 copy-done.3
  65.3 0.0 copy-done.2
  65.3 0.0 copy-done.6
  65.3 4.5 %first_tile.1 = (f32[768,1152]{1,0:T(8,128)S(1)}, f32[192,1152]{1,0:T(8,128)S(1)}, f32[1,192]{1,0:T(1,128)S(1)}, f32[4,1152]{1,0:T(4,128)S(1)}) custom-call(f32[2]{0:T(128)S(1)} %pad_maximum_fusion.scalars_ref, f32[2,1152]{1,0:T(2,128)S(1)} %copy-done.4, f32[2,1152]{1,0:T(2,128)S(1)} %copy-done.3, bf16[208,1152]{1,0:T(8,128)(2,1)S(1)} %copy-done.6, ...), custom_call_target="tpu_custom_call" | custom-call | flops 1019215872 | bytes 5308416 | tf_op jit(solution)/shard_map/first_tile/pallas_call | solution.py:194
  69.9 0.0 copy-start.1
  69.9 0.9 copy-done.1
  70.8 0.0 collective-permute-done.10.refs_0_
  70.8 0.0 copy-done.8
  70.8 4.9 %last_tile.1 = (f32[192,1152]{1,0:T(8,128)S(1)}, f32[192,1152]{1,0:T(8,128)S(1)}, bf16[384,1152]{1,0:T(8,128)(2,1)}, bf16[208,1152]{1,0:T(8,128)(2,1)S(1)}, f32[4,1152]{1,0:T(4,128)S(1)}) custom-call(f32[2]{0:T(128)S(1)} %pad_maximum_fusion.scalars_ref, f32[2,1152]{1,0:T(2,128)S(1)} %copy-done.4, f32[2,1152]{1,0:T(2,128)S(1)} %copy-done.3, ...), custom_call_target="tpu_custom_call" | custom-call | flops 1019215872 | bytes 5308416 | tf_op jit(solution)/shard_map/last_tile/pallas_call | solution.py:194
  75.7 0.0 copy-done.5
  75.7 0.9 copy-done
  76.7 3.5 %collective-permute-start.12 = (bf16[384,1152]{1,0:T(8,128)(2,1)}, bf16[384,1152]{1,0:T(8,128)(2,1)S(1)}, u32[]{:S(2)}, u32[]{:S(2)}) collective-permute-start(bf16[384,1152]{1,0:T(8,128)(2,1)} %get-tuple-element.90), channel_id=1, source_target_pairs={{0,512},{1,513},{2,514},{3,515},{4,516},{5,517},{6,518},{7,519},{8... | collective-permute-start | bytes 2654216 | tf_op jit(solution)/shard_map/ppermute | solution.py:340
  80.2 6.1 %collective-permute-start.13 = (bf16[208,1152]{1,0:T(8,128)(2,1)S(1)}, bf16[208,1152]{1,0:T(8,128)(2,1)S(1)}, u32[]{:S(2)}, u32[]{:S(2)}) collective-permute-start(bf16[208,1152]{1,0:T(8,128)(2,1)S(1)} %get-tuple-element.93), channel_id=1, source_target_pairs={{0,128},{1,385},{2,130},{3,387},{4,132},{5,389},{6,134},{7,391},{8... | collective-permute-start | bytes 1437704 | tf_op jit(solution)/shard_map/ppermute | solution.py:340
  86.2 21.3 %while.31 = (s32[]{:T(128)}, f32[4,1152]{1,0:T(4,128)S(1)}, s32[]{:T(128)}, s32[]{:T(128)}) while((s32[]{:T(128)}, f32[4,1152]{1,0:T(4,128)S(1)}, s32[]{:T(128)}, s32[]{:T(128)}) %tuple.64), condition=%wide.region_3.4_spmd, body=%wide.region_2.3_spmd.sunk | while | flops 18434 | bytes 516309 | solution.py:344
  86.2 1.9 %collective-permute-start.1 = (f32[4,1152]{1,0:T(4,128)S(1)}, f32[4,1152]{1,0:T(4,128)S(1)}, u32[]{:S(2)}, u32[]{:S(2)}) collective-permute-start(f32[4,1152]{1,0:T(4,128)S(1)} %get-tuple-element.209), channel_id=1, source_target_pairs={{0,1},{1,0},{2,3},{3,2},{4,5},{5,4},{6,7},{7,6},{8,9},{9,8},{10,11... | collective-permute-start | bytes 55304 | tf_op jit(solution)/shard_map/while/body/ppermute | solution.py:340
  88.2 1.2 collective-permute-done.1
  89.3 2.7 %collective-permute-start.2 = (f32[4,1152]{1,0:T(4,128)S(1)}, f32[4,1152]{1,0:T(4,128)S(1)}, u32[]{:S(2)}, u32[]{:S(2)}) collective-permute-start(f32[4,1152]{1,0:T(4,128)S(1)} %add.59), channel_id=1, source_target_pairs={{0,8},{1,9},{2,10},{3,11},{4,12},{5,13},{6,14},{7,15},{8,0},{9,1},... | collective-permute-start | bytes 55304 | tf_op jit(solution)/shard_map/while/body/ppermute | solution.py:340
  92.1 2.9 %collective-permute-done.2 = f32[4,1152]{1,0:T(4,128)S(1)} collective-permute-done((f32[4,1152]{1,0:T(4,128)S(1)}, f32[4,1152]{1,0:T(4,128)S(1)}, u32[]{:S(2)}, u32[]{:S(2)}) %collective-permute-start.2) | collective-permute-done | bytes 18464 | tf_op jit(solution)/shard_map/while/body/ppermute | solution.py:340
  95.0 2.4 %collective-permute-start.3 = (f32[4,1152]{1,0:T(4,128)S(1)}, f32[4,1152]{1,0:T(4,128)S(1)}, u32[]{:S(2)}, u32[]{:S(2)}) collective-permute-start(f32[4,1152]{1,0:T(4,128)S(1)} %add.60), channel_id=1, source_target_pairs={{0,24},{1,25},{2,26},{3,27},{4,28},{5,29},{6,30},{7,31},{8,16},{9,... | collective-permute-start | bytes 55304 | tf_op jit(solution)/shard_map/while/body/ppermute | solution.py:340
  97.4 4.4 %collective-permute-done.3 = f32[4,1152]{1,0:T(4,128)S(1)} collective-permute-done((f32[4,1152]{1,0:T(4,128)S(1)}, f32[4,1152]{1,0:T(4,128)S(1)}, u32[]{:S(2)}, u32[]{:S(2)}) %collective-permute-start.3) | collective-permute-done | bytes 18464 | tf_op jit(solution)/shard_map/while/body/ppermute | solution.py:340
  101.8 2.4 %collective-permute-start.4 = (f32[4,1152]{1,0:T(4,128)S(1)}, f32[4,1152]{1,0:T(4,128)S(1)}, u32[]{:S(2)}, u32[]{:S(2)}) collective-permute-start(f32[4,1152]{1,0:T(4,128)S(1)} %add.61), channel_id=1, source_target_pairs={{0,512},{1,513},{2,514},{3,515},{4,516},{5,517},{6,518},{7,519},{8... | collective-permute-start | bytes 55304 | tf_op jit(solution)/shard_map/while/body/ppermute | solution.py:340
  104.2 3.3 %collective-permute-done.4 = f32[4,1152]{1,0:T(4,128)S(1)} collective-permute-done((f32[4,1152]{1,0:T(4,128)S(1)}, f32[4,1152]{1,0:T(4,128)S(1)}, u32[]{:S(2)}, u32[]{:S(2)}) %collective-permute-start.4) | collective-permute-done | bytes 18464 | tf_op jit(solution)/shard_map/while/body/ppermute | solution.py:340
  107.5 0.0 collective-permute-done.12.refs_1_
  107.5 0.0 copy-start.7
  107.5 0.1 add_convert_fusion
  107.6 5.6 %collective-permute-start.14 = (bf16[192,1152]{1,0:T(8,128)(2,1)S(1)}, bf16[192,1152]{1,0:T(8,128)(2,1)S(1)}, u32[]{:S(2)}, u32[]{:S(2)}) collective-permute-start(bf16[192,1152]{1,0:T(8,128)(2,1)S(1)} %add_convert_fusion), channel_id=1, source_target_pairs={{0,384},{1,129},{2,386},{3,131},{4,388},{5,133},{6,390},{7,135},{8... | collective-permute-start | bytes 1327112 | tf_op jit(solution)/shard_map/ppermute | solution.py:340
  113.2 0.0 collective-permute-done.13.refs_1_
  113.2 0.0 copy-start.9
  113.2 26.9 %while.32 = (s32[]{:T(128)}, f32[4,1152]{1,0:T(4,128)S(1)}, s32[]{:T(128)}, s32[]{:T(128)}) while((s32[]{:T(128)}, f32[4,1152]{1,0:T(4,128)S(1)}, s32[]{:T(128)}, s32[]{:T(128)}) %tuple.67), condition=%wide.region_5.6_spmd, body=%wide.region_4.5_spmd.sunk | while | flops 18434 | bytes 516309 | solution.py:344
  113.3 5.2 %collective-permute-start.5 = (f32[4,1152]{1,0:T(4,128)S(1)}, f32[4,1152]{1,0:T(4,128)S(1)}, u32[]{:S(2)}, u32[]{:S(2)}) collective-permute-start(f32[4,1152]{1,0:T(4,128)S(1)} %get-tuple-element.221), channel_id=1, source_target_pairs={{0,518},{1,519},{2,512},{3,513},{4,514},{5,515},{6,516},{7,517},{8... | collective-permute-start | bytes 55304 | tf_op jit(solution)/shard_map/while/body/ppermute | solution.py:340
  118.4 1.7 %collective-permute-done.5 = f32[4,1152]{1,0:T(4,128)S(1)} collective-permute-done((f32[4,1152]{1,0:T(4,128)S(1)}, f32[4,1152]{1,0:T(4,128)S(1)}, u32[]{:S(2)}, u32[]{:S(2)}) %collective-permute-start.5) | collective-permute-done | bytes 18464 | tf_op jit(solution)/shard_map/while/body/ppermute | solution.py:340
  120.1 4.4 %collective-permute-start.6 = (f32[4,1152]{1,0:T(4,128)S(1)}, f32[4,1152]{1,0:T(4,128)S(1)}, u32[]{:S(2)}, u32[]{:S(2)}) collective-permute-start(f32[4,1152]{1,0:T(4,128)S(1)} %add.64), channel_id=1, source_target_pairs={{0,514},{1,515},{2,516},{3,517},{4,518},{5,519},{6,512},{7,513},{8... | collective-permute-start | bytes 55304 | tf_op jit(solution)/shard_map/while/body/ppermute | solution.py:340
  124.5 3.1 %collective-permute-done.6 = f32[4,1152]{1,0:T(4,128)S(1)} collective-permute-done((f32[4,1152]{1,0:T(4,128)S(1)}, f32[4,1152]{1,0:T(4,128)S(1)}, u32[]{:S(2)}, u32[]{:S(2)}) %collective-permute-start.6) | collective-permute-done | bytes 18464 | tf_op jit(solution)/shard_map/while/body/ppermute | solution.py:340
  127.6 1.9 %collective-permute-start.7 = (f32[4,1152]{1,0:T(4,128)S(1)}, f32[4,1152]{1,0:T(4,128)S(1)}, u32[]{:S(2)}, u32[]{:S(2)}) collective-permute-start(f32[4,1152]{1,0:T(4,128)S(1)} %add.65), channel_id=1, source_target_pairs={{0,32},{1,33},{2,34},{3,35},{4,36},{5,37},{6,38},{7,39},{8,40},{9,... | collective-permute-start | bytes 55304 | tf_op jit(solution)/shard_map/while/body/ppermute | solution.py:340
  129.5 3.7 %collective-permute-done.7 = f32[4,1152]{1,0:T(4,128)S(1)} collective-permute-done((f32[4,1152]{1,0:T(4,128)S(1)}, f32[4,1152]{1,0:T(4,128)S(1)}, u32[]{:S(2)}, u32[]{:S(2)}) %collective-permute-start.7) | collective-permute-done | bytes 18464 | tf_op jit(solution)/shard_map/while/body/ppermute | solution.py:340
  133.2 4.6 %collective-permute-start.8 = (f32[4,1152]{1,0:T(4,128)S(1)}, f32[4,1152]{1,0:T(4,128)S(1)}, u32[]{:S(2)}, u32[]{:S(2)}) collective-permute-start(f32[4,1152]{1,0:T(4,128)S(1)} %add.66), channel_id=1, source_target_pairs={{0,480},{1,481},{2,482},{3,483},{4,484},{5,485},{6,486},{7,487},{8... | collective-permute-start | bytes 55304 | tf_op jit(solution)/shard_map/while/body/ppermute | solution.py:340
  137.9 2.2 %collective-permute-done.8 = f32[4,1152]{1,0:T(4,128)S(1)} collective-permute-done((f32[4,1152]{1,0:T(4,128)S(1)}, f32[4,1152]{1,0:T(4,128)S(1)}, u32[]{:S(2)}, u32[]{:S(2)}) %collective-permute-start.8) | collective-permute-done | bytes 18464 | tf_op jit(solution)/shard_map/while/body/ppermute | solution.py:340
  140.1 0.0 collective-permute-done.14.refs_2_
  140.1 0.0 copy-start.10
  140.1 3.9 %collective-permute-start.15 = (f32[4,1152]{1,0:T(4,128)S(1)}, f32[4,1152]{1,0:T(4,128)S(1)}, u32[]{:S(2)}, u32[]{:S(2)}) collective-permute-start(f32[4,1152]{1,0:T(4,128)S(1)} %get-tuple-element.96), channel_id=1, source_target_pairs={{0,96},{1,97},{2,98},{3,99},{4,100},{5,101},{6,102},{7,103},{8,104... | collective-permute-start | bytes 55304 | tf_op jit(solution)/shard_map/ppermute | solution.py:340
  144.0 0.6 fusion.1
  144.6 0.0 copy-done.9
  144.6 4.0 %backward_norm.2 = (bf16[192,1152]{1,0:T(8,128)(2,1)}, f32[1,192]{1,0:T(1,128)}) custom-call(bf16[192,1152]{1,0:T(8,128)(2,1)} %bitcast.6, f32[1,1152]{1,0:T(1,128)} %get-tuple-element.130.gain_ref, f32[1,1152]{1,0:T(1,128)} %get-tuple-element.127.shift_ref, f32[1]{0:T(128)S(6)} %exp.3.scale_ref, f32[192,1152]{1,0:T(8,128)} %copy-done.1, ...), custom_call_target="tpu_custom_call" | custom-call | flops 8847360 | bytes 2654208 | tf_op jit(solution)/shard_map/backward_norm/pallas_call | solution.py:252
  148.7 0.0 collective-permute-done.15
  148.7 7.3 %collective-permute-start.16 = (f32[4,1152]{1,0:T(4,128)S(1)}, f32[4,1152]{1,0:T(4,128)S(1)}, u32[]{:S(2)}, u32[]{:S(2)}) collective-permute-start(f32[4,1152]{1,0:T(4,128)S(1)} %add.43), channel_id=1, source_target_pairs={{0,352},{1,353},{2,354},{3,355},{4,356},{5,357},{6,358},{7,359},{8... | collective-permute-start | bytes 55304 | tf_op jit(solution)/shard_map/ppermute | solution.py:340
  156.0 0.0 copy-done.7
  156.0 4.3 %backward_norm.3 = bf16[192,1152]{1,0:T(8,128)(2,1)} custom-call(bf16[192,1152]{1,0:T(8,128)(2,1)} %bitcast.8, f32[1,1152]{1,0:T(1,128)} %get-tuple-element.131.gain_ref, f32[1,1152]{1,0:T(1,128)} %get-tuple-element.126.shift_ref, f32[1]{0:T(128)S(6)} %exp.3.scale_ref, f32[192,1152]{1,0:T(8,128)} %copy-done, bf16[384,1152]{1,0:T(8,128)(2,1)} %copy-done.7, ...), custom_call_target="tpu_custom_call" | custom-call | flops 8847360 | bytes 2654208 | tf_op jit(solution)/shard_map/backward_norm/pallas_call | solution.py:252
  160.3 0.1 collective-permute-done.16
  160.4 0.6 fusion
  (16 shorter events, 0.1 us)
Async XLA Ops:
  0.6 64.7 %copy-start.4 = (f32[2,1152]{1,0:T(2,128)S(1)}, f32[2,1152]{1,0:T(2,128)}, u32[]{:S(2)}) copy-start(f32[2,1152]{1,0:T(2,128)} %gains_ref.5) | copy-start | bytes 27652
  0.6 64.6 %copy-start.3 = (f32[2,1152]{1,0:T(2,128)S(1)}, f32[2,1152]{1,0:T(2,128)}, u32[]{:S(2)}) copy-start(f32[2,1152]{1,0:T(2,128)} %shifts_ref.5) | copy-start | bytes 27652
  4.8 60.5 %copy-start.2 = (bf16[208,1152]{1,0:T(8,128)(2,1)S(1)}, bf16[208,1152]{1,0:T(8,128)(2,1)}, u32[]{:S(2)}) copy-start(bf16[208,1152]{1,0:T(8,128)(2,1)} %get-tuple-element.82.refs_1_) | copy-start | bytes 1437700
  4.8 60.5 %copy-start.6 = (bf16[208,1152]{1,0:T(8,128)(2,1)S(1)}, bf16[208,1152]{1,0:T(8,128)(2,1)}, u32[]{:S(2)}) copy-start(bf16[208,1152]{1,0:T(8,128)(2,1)} %get-tuple-element.83.refs_0_) | copy-start | bytes 1437700
  4.8 40.5 %collective-permute-start.9 = (bf16[208,1152]{1,0:T(8,128)(2,1)}, bf16[208,1152]{1,0:T(8,128)(2,1)S(1)}, u32[]{:S(2)}, u32[]{:S(2)}) collective-permute-start(bf16[208,1152]{1,0:T(8,128)(2,1)} %get-tuple-element.82.refs_1_), channel_id=1, source_target_pairs={{0,384},{1,129},{2,386},{3,131},{4,388},{5,133},{6,390},{7,135},{8... | collective-permute-start | bytes 1437704 | tf_op jit(solution)/shard_map/ppermute | solution.py:340
  23.1 42.2 %collective-permute-start.11 = (bf16[208,1152]{1,0:T(8,128)(2,1)}, bf16[208,1152]{1,0:T(8,128)(2,1)S(1)}, u32[]{:S(2)}, u32[]{:S(2)}) collective-permute-start(bf16[208,1152]{1,0:T(8,128)(2,1)} %get-tuple-element.82.refs_1_), channel_id=1, source_target_pairs={{0,512},{1,513},{2,514},{3,515},{4,516},{5,517},{6,518},{7,519},{8... | collective-permute-start | bytes 1437704 | tf_op jit(solution)/shard_map/ppermute | solution.py:340
  45.2 25.6 %collective-permute-start.10 = (bf16[208,1152]{1,0:T(8,128)(2,1)}, bf16[208,1152]{1,0:T(8,128)(2,1)S(1)}, u32[]{:S(2)}, u32[]{:S(2)}) collective-permute-start(bf16[208,1152]{1,0:T(8,128)(2,1)} %get-tuple-element.83.refs_0_), channel_id=1, source_target_pairs={{0,128},{1,385},{2,130},{3,387},{4,132},{5,389},{6,134},{7,391},{8... | collective-permute-start | bytes 1437704 | tf_op jit(solution)/shard_map/ppermute | solution.py:340
  50.8 13.6 %collective-permute-start = (bf16[208,1152]{1,0:T(8,128)(2,1)}, bf16[208,1152]{1,0:T(8,128)(2,1)S(1)}, u32[]{:S(2)}, u32[]{:S(2)}) collective-permute-start(bf16[208,1152]{1,0:T(8,128)(2,1)} %get-tuple-element.197), channel_id=1, source_target_pairs={{0,512},{1,513},{2,514},{3,515},{4,516},{5,517},{6,518},{7,519},{8... | collective-permute-start | bytes 1437704 | tf_op jit(solution)/shard_map/while/body/ppermute | solution.py:340
  65.3 5.5 %copy-start.8 = (bf16[208,1152]{1,0:T(8,128)(2,1)S(1)}, bf16[208,1152]{1,0:T(8,128)(2,1)}, u32[]{:S(2)}) copy-start(bf16[208,1152]{1,0:T(8,128)(2,1)} %get-tuple-element.85.refs_4_) | copy-start | bytes 1437700
  69.9 0.9 copy-start.1
  70.8 4.9 %copy-start.5 = (f32[1,192]{1,0:T(1,128)}, f32[1,192]{1,0:T(1,128)S(1)}, u32[]{:S(2)}) copy-start(f32[1,192]{1,0:T(1,128)S(1)} %get-tuple-element.99.refs_2_) | copy-start | bytes 2308
  75.7 0.9 copy-start
  76.7 30.8 %collective-permute-start.12 = (bf16[384,1152]{1,0:T(8,128)(2,1)}, bf16[384,1152]{1,0:T(8,128)(2,1)S(1)}, u32[]{:S(2)}, u32[]{:S(2)}) collective-permute-start(bf16[384,1152]{1,0:T(8,128)(2,1)} %get-tuple-element.90), channel_id=1, source_target_pairs={{0,512},{1,513},{2,514},{3,515},{4,516},{5,517},{6,518},{7,519},{8... | collective-permute-start | bytes 2654216 | tf_op jit(solution)/shard_map/ppermute | solution.py:340
  80.2 33.1 %collective-permute-start.13 = (bf16[208,1152]{1,0:T(8,128)(2,1)S(1)}, bf16[208,1152]{1,0:T(8,128)(2,1)S(1)}, u32[]{:S(2)}, u32[]{:S(2)}) collective-permute-start(bf16[208,1152]{1,0:T(8,128)(2,1)S(1)} %get-tuple-element.93), channel_id=1, source_target_pairs={{0,128},{1,385},{2,130},{3,387},{4,132},{5,389},{6,134},{7,391},{8... | collective-permute-start | bytes 1437704 | tf_op jit(solution)/shard_map/ppermute | solution.py:340
  86.2 3.1 %collective-permute-start.1 = (f32[4,1152]{1,0:T(4,128)S(1)}, f32[4,1152]{1,0:T(4,128)S(1)}, u32[]{:S(2)}, u32[]{:S(2)}) collective-permute-start(f32[4,1152]{1,0:T(4,128)S(1)} %get-tuple-element.209), channel_id=1, source_target_pairs={{0,1},{1,0},{2,3},{3,2},{4,5},{5,4},{6,7},{7,6},{8,9},{9,8},{10,11... | collective-permute-start | bytes 55304 | tf_op jit(solution)/shard_map/while/body/ppermute | solution.py:340
  89.3 5.6 %collective-permute-start.2 = (f32[4,1152]{1,0:T(4,128)S(1)}, f32[4,1152]{1,0:T(4,128)S(1)}, u32[]{:S(2)}, u32[]{:S(2)}) collective-permute-start(f32[4,1152]{1,0:T(4,128)S(1)} %add.59), channel_id=1, source_target_pairs={{0,8},{1,9},{2,10},{3,11},{4,12},{5,13},{6,14},{7,15},{8,0},{9,1},... | collective-permute-start | bytes 55304 | tf_op jit(solution)/shard_map/while/body/ppermute | solution.py:340
  95.0 6.9 %collective-permute-start.3 = (f32[4,1152]{1,0:T(4,128)S(1)}, f32[4,1152]{1,0:T(4,128)S(1)}, u32[]{:S(2)}, u32[]{:S(2)}) collective-permute-start(f32[4,1152]{1,0:T(4,128)S(1)} %add.60), channel_id=1, source_target_pairs={{0,24},{1,25},{2,26},{3,27},{4,28},{5,29},{6,30},{7,31},{8,16},{9,... | collective-permute-start | bytes 55304 | tf_op jit(solution)/shard_map/while/body/ppermute | solution.py:340
  101.8 5.6 %collective-permute-start.4 = (f32[4,1152]{1,0:T(4,128)S(1)}, f32[4,1152]{1,0:T(4,128)S(1)}, u32[]{:S(2)}, u32[]{:S(2)}) collective-permute-start(f32[4,1152]{1,0:T(4,128)S(1)} %add.61), channel_id=1, source_target_pairs={{0,512},{1,513},{2,514},{3,515},{4,516},{5,517},{6,518},{7,519},{8... | collective-permute-start | bytes 55304 | tf_op jit(solution)/shard_map/while/body/ppermute | solution.py:340
  107.5 48.5 %copy-start.7 = (bf16[384,1152]{1,0:T(8,128)(2,1)}, bf16[384,1152]{1,0:T(8,128)(2,1)S(1)}, u32[]{:S(2)}) copy-start(bf16[384,1152]{1,0:T(8,128)(2,1)S(1)} %collective-permute-done.12.refs_1_) | copy-start | bytes 2654212
  107.6 32.5 %collective-permute-start.14 = (bf16[192,1152]{1,0:T(8,128)(2,1)S(1)}, bf16[192,1152]{1,0:T(8,128)(2,1)S(1)}, u32[]{:S(2)}, u32[]{:S(2)}) collective-permute-start(bf16[192,1152]{1,0:T(8,128)(2,1)S(1)} %add_convert_fusion), channel_id=1, source_target_pairs={{0,384},{1,129},{2,386},{3,131},{4,388},{5,133},{6,390},{7,135},{8... | collective-permute-start | bytes 1327112 | tf_op jit(solution)/shard_map/ppermute | solution.py:340
  113.2 31.4 %copy-start.9 = (bf16[208,1152]{1,0:T(8,128)(2,1)}, bf16[208,1152]{1,0:T(8,128)(2,1)S(1)}, u32[]{:S(2)}) copy-start(bf16[208,1152]{1,0:T(8,128)(2,1)S(1)} %collective-permute-done.13.refs_1_) | copy-start | bytes 1437700
  113.3 6.9 %collective-permute-start.5 = (f32[4,1152]{1,0:T(4,128)S(1)}, f32[4,1152]{1,0:T(4,128)S(1)}, u32[]{:S(2)}, u32[]{:S(2)}) collective-permute-start(f32[4,1152]{1,0:T(4,128)S(1)} %get-tuple-element.221), channel_id=1, source_target_pairs={{0,518},{1,519},{2,512},{3,513},{4,514},{5,515},{6,516},{7,517},{8... | collective-permute-start | bytes 55304 | tf_op jit(solution)/shard_map/while/body/ppermute | solution.py:340
  120.1 7.4 %collective-permute-start.6 = (f32[4,1152]{1,0:T(4,128)S(1)}, f32[4,1152]{1,0:T(4,128)S(1)}, u32[]{:S(2)}, u32[]{:S(2)}) collective-permute-start(f32[4,1152]{1,0:T(4,128)S(1)} %add.64), channel_id=1, source_target_pairs={{0,514},{1,515},{2,516},{3,517},{4,518},{5,519},{6,512},{7,513},{8... | collective-permute-start | bytes 55304 | tf_op jit(solution)/shard_map/while/body/ppermute | solution.py:340
  127.6 5.6 %collective-permute-start.7 = (f32[4,1152]{1,0:T(4,128)S(1)}, f32[4,1152]{1,0:T(4,128)S(1)}, u32[]{:S(2)}, u32[]{:S(2)}) collective-permute-start(f32[4,1152]{1,0:T(4,128)S(1)} %add.65), channel_id=1, source_target_pairs={{0,32},{1,33},{2,34},{3,35},{4,36},{5,37},{6,38},{7,39},{8,40},{9,... | collective-permute-start | bytes 55304 | tf_op jit(solution)/shard_map/while/body/ppermute | solution.py:340
  133.2 6.9 %collective-permute-start.8 = (f32[4,1152]{1,0:T(4,128)S(1)}, f32[4,1152]{1,0:T(4,128)S(1)}, u32[]{:S(2)}, u32[]{:S(2)}) collective-permute-start(f32[4,1152]{1,0:T(4,128)S(1)} %add.66), channel_id=1, source_target_pairs={{0,480},{1,481},{2,482},{3,483},{4,484},{5,485},{6,486},{7,487},{8... | collective-permute-start | bytes 55304 | tf_op jit(solution)/shard_map/while/body/ppermute | solution.py:340
  140.1 15.9 %copy-start.10 = (bf16[192,1152]{1,0:T(8,128)(2,1)}, bf16[192,1152]{1,0:T(8,128)(2,1)S(1)}, u32[]{:S(2)}) copy-start(bf16[192,1152]{1,0:T(8,128)(2,1)S(1)} %collective-permute-done.14.refs_2_) | copy-start | bytes 1327108
  140.1 8.5 %collective-permute-start.15 = (f32[4,1152]{1,0:T(4,128)S(1)}, f32[4,1152]{1,0:T(4,128)S(1)}, u32[]{:S(2)}, u32[]{:S(2)}) collective-permute-start(f32[4,1152]{1,0:T(4,128)S(1)} %get-tuple-element.96), channel_id=1, source_target_pairs={{0,96},{1,97},{2,98},{3,99},{4,100},{5,101},{6,102},{7,103},{8,104... | collective-permute-start | bytes 55304 | tf_op jit(solution)/shard_map/ppermute | solution.py:340
  148.7 11.7 %collective-permute-start.16 = (f32[4,1152]{1,0:T(4,128)S(1)}, f32[4,1152]{1,0:T(4,128)S(1)}, u32[]{:S(2)}, u32[]{:S(2)}) collective-permute-start(f32[4,1152]{1,0:T(4,128)S(1)} %add.43), channel_id=1, source_target_pairs={{0,352},{1,353},{2,354},{3,355},{4,356},{5,357},{6,358},{7,359},{8... | collective-permute-start | bytes 55304 | tf_op jit(solution)/shard_map/ppermute | solution.py:340

commit v6 on v5

--- a/solution.py
+++ b/solution.py
@@ -18,7 +18,7 @@
 ROW_BLOCK = 16
 UNROLL = 4
 EPS = 1e-06
-EXTRA = 16
+EXTRA = 8
 LANES = 256
 NT = (((1,), (1,)), ((), ()))
 TN = (((0,), (0,)), ((), ()))
@@ -210,7 +210,7 @@
     )(scalars, gains, shifts, image, *texts, *before)
 
 
-def backward_kernel(firsts, feats_ref, gain_ref, shift_ref, scale_ref, *refs):
+def backward_kernel(tower, firsts, feats_ref, gains_ref, shifts_ref, scale_ref, *refs):
     count = len(firsts)
     part_refs = refs[:count]
     if len(refs) > count + 1:
@@ -221,12 +221,13 @@
     else:
         grad_ref = refs[count]
 
-    @pl.loop(0, feats_ref.shape[0] // ROW_BLOCK, unroll=UNROLL)
+    @pl.loop(0, feats_ref.shape[0] // ROW_BLOCK, unroll=True)
     def _(step):
         rows = pl.ds(pl.multiple_of(step * ROW_BLOCK, ROW_BLOCK), ROW_BLOCK)
         feats = feats_ref[rows, :].astype(jnp.float32)
-        gain = gain_ref[...]
-        normed, rstd, unnormed, inverse = norm_rows(feats, gain, shift_ref[...])
+        gain = gains_ref[tower : tower + 1, :]
+        shift = shifts_ref[tower : tower + 1, :]
+        normed, rstd, unnormed, inverse = norm_rows(feats, gain, shift)
         unit = unnormed * inverse
         pulled = 0.0
         for first, part_ref in zip(firsts, part_refs):
@@ -240,7 +241,7 @@
         grad_ref[rows, :] = pulled.astype(jnp.bfloat16)
 
 
-def backward_norm(feats, gain, shift, scale, parts, loss=None):
+def backward_norm(tower, feats, gains, shifts, scale, parts, loss=None):
     rows, width = feats.shape
     firsts = [first for first, _ in parts]
     values = [part for _, part in parts]
@@ -250,7 +251,7 @@
         values.append(loss)
         out_shape += (jax.ShapeDtypeStruct((1, rows), jnp.float32),)
     return pl.pallas_call(
-        functools.partial(backward_kernel, firsts),
+        functools.partial(backward_kernel, tower, firsts),
         out_shape=out_shape,
         in_specs=[whole] * 3 + [pl.BlockSpec(memory_space=pltpu.SMEM)] + [whole] * len(values),
         out_specs=(whole,) * len(out_shape),
@@ -259,7 +260,7 @@
             flops=40 * rows * width, bytes_accessed=12 * rows * width, transcendentals=0
         ),
         name="backward_norm",
-    )(feats, gain, shift, scale, *values)
+    )(feats, gains, shifts, scale, *values)
 
 
 def near(place):
@@ -389,9 +390,10 @@
         sums = once(lambda value: sum_over(value, middle_steps), sums, turns)
         sums, image_back, text_z_back = lax.optimization_barrier((sums, image_back, text_z_back))
         image_grad, row_mean = backward_norm(
+            0,
             image_feats[0],
-            gains[:1],
-            shifts[:1],
+            gains,
+            shifts,
             scale,
             [(0, image_part), (0, image_back)],
             loss_own,
@@ -401,9 +403,10 @@
         for pairs in late_steps[1:]:
             sums = sums + send(sums, pairs)
         (text_grad,) = backward_norm(
+            1,
             text_feats[0],
-            gains[1:],
-            shifts[1:],
+            gains,
+            shifts,
             scale,
             [(0, text_part), (rows, y_back), (0, text_z_back)],
         )

time: 162 us -> 160 us (0.988)
  Pallas kernels: 21.9 us -> 20.2 us
    pallas_call x2, Pallas kernels: 8.32 us -> 6.65 us  [backward_norm(): pl.pallas_call(functools.partial(backward_kernel, tower, firsts), out_sha...]
  transfers between devices with their start and end apart: 17 -> 17, of which waited for: 11 -> 12; matrix products, arithmetic and copies ran while one was open for 2% -> 1% of each run, Pallas kernels for 8% -> 7%
where the time goes in v6:
time: 160 us; the launch traced here: 159 us
  starting transfers between devices  80 us (50%)
  waiting for transfers between devices  52.1 us (33%)
  Pallas kernels  20.2 us (13%)
  local copies, waits for them, and re-layouts  4.07 us (3%)
  between operations  2.17 us (1%)
    ppermute x17, starting transfers between devices, send(): return lax.ppermute(value, AXES, pairs)  80 us
    ppermute x17, waiting for transfers between devices, send(): return lax.ppermute(value, AXES, pairs)  52.1 us
    pallas_call x2, Pallas kernels, tile(): pl.pallas_call(functools.partial(tile_kernel, final), out_shape=tuple(out...  9.46 us
    pallas_call x2, Pallas kernels, backward_norm(): pl.pallas_call(functools.partial(backward_kernel, tower, firsts), out_sha...  6.65 us
    pallas_call x1, Pallas kernels, forward_norms(): pl.pallas_call(forward_kernel, out_shape=(emb, emb), scratch_shapes=[pltp...  4.13 us
  transfers between devices with their start and end apart: 17, of which 12 were waited for; matrix products, arithmetic and copies ran while one was open for 1% of the time, Pallas kernels for 7%

profile of v6, /device:TPU:6, one launch (start us, length us, event | category | flops | bytes accessed | tf_op | source)
XLA Modules:
  0.0 158.9 jit_solution(3252375339055637775)
XLA Ops:
  0.6 0.0 copy-start.3
  0.6 0.0 copy-start.4
  0.7 4.1 %forward_norms.1 = (bf16[200,1152]{1,0:T(8,128)(2,1)}, bf16[200,1152]{1,0:T(8,128)(2,1)}) custom-call(bf16[192,1152]{1,0:T(8,128)(2,1)} %bitcast.5, bf16[192,1152]{1,0:T(8,128)(2,1)} %bitcast.7, f32[2,1152]{1,0:T(2,128)} %gains_ref.9, f32[2,1152]{1,0:T(2,128)} %shifts_ref.9), custom_call_target="tpu_custom_call" | custom-call | flops 8847360 | bytes 1769472 | tf_op jit(solution)/shard_map/forward_norms/pallas_call | solution.py:92
  4.8 18.3 %collective-permute-start.9 = (bf16[200,1152]{1,0:T(8,128)(2,1)}, bf16[200,1152]{1,0:T(8,128)(2,1)S(1)}, u32[]{:S(2)}, u32[]{:S(2)}) collective-permute-start(bf16[200,1152]{1,0:T(8,128)(2,1)} %get-tuple-element.82.refs_1_), channel_id=1, source_target_pairs={{0,384},{1,129},{2,386},{3,131},{4,388},{5,133},{6,390},{7,135},{8... | collective-permute-start | bytes 1382408 | tf_op jit(solution)/shard_map/ppermute | solution.py:341
  23.1 3.5 %collective-permute-start.11 = (bf16[200,1152]{1,0:T(8,128)(2,1)}, bf16[200,1152]{1,0:T(8,128)(2,1)S(1)}, u32[]{:S(2)}, u32[]{:S(2)}) collective-permute-start(bf16[200,1152]{1,0:T(8,128)(2,1)} %get-tuple-element.82.refs_1_), channel_id=1, source_target_pairs={{0,512},{1,513},{2,514},{3,515},{4,516},{5,517},{6,518},{7,519},{8... | collective-permute-start | bytes 1382408 | tf_op jit(solution)/shard_map/ppermute | solution.py:341
  26.6 17.8 %collective-permute-done.9.refs_2_ = bf16[200,1152]{1,0:T(8,128)(2,1)S(1)} collective-permute-done((bf16[200,1152]{1,0:T(8,128)(2,1)}, bf16[200,1152]{1,0:T(8,128)(2,1)S(1)}, u32[]{:S(2)}, u32[]{:S(2)}) %collective-permute-start.9) | collective-permute-done | bytes 460832 | tf_op jit(solution)/shard_map/ppermute | solution.py:341
  44.4 3.4 %collective-permute-start.10 = (bf16[200,1152]{1,0:T(8,128)(2,1)}, bf16[200,1152]{1,0:T(8,128)(2,1)S(1)}, u32[]{:S(2)}, u32[]{:S(2)}) collective-permute-start(bf16[200,1152]{1,0:T(8,128)(2,1)} %get-tuple-element.83.refs_0_), channel_id=1, source_target_pairs={{0,128},{1,385},{2,130},{3,387},{4,132},{5,389},{6,134},{7,391},{8... | collective-permute-start | bytes 1382408 | tf_op jit(solution)/shard_map/ppermute | solution.py:341
  49.2 0.1 pad_maximum_fusion.scalars_ref
  49.2 0.8 copy.12
  50.0 14.0 %while.30 = (s32[]{:T(128)}, bf16[200,1152]{1,0:T(8,128)(2,1)}, s32[]{:T(128)}, s32[]{:T(128)}) while((s32[]{:T(128)}, bf16[200,1152]{1,0:T(8,128)(2,1)}, s32[]{:T(128)}, s32[]{:T(128)}) %tuple.57), condition=%wide.region_1.2_spmd, body=%wide.region_0.1_spmd.sunk | while | flops 2 | bytes 2764893 | solution.py:345
  50.0 3.5 %collective-permute-start = (bf16[200,1152]{1,0:T(8,128)(2,1)}, bf16[200,1152]{1,0:T(8,128)(2,1)S(1)}, u32[]{:S(2)}, u32[]{:S(2)}) collective-permute-start(bf16[200,1152]{1,0:T(8,128)(2,1)} %get-tuple-element.191), channel_id=1, source_target_pairs={{0,512},{1,513},{2,514},{3,515},{4,516},{5,517},{6,518},{7,519},{8... | collective-permute-start | bytes 1382408 | tf_op jit(solution)/shard_map/while/body/ppermute | solution.py:341
  53.5 9.8 %collective-permute-done = bf16[200,1152]{1,0:T(8,128)(2,1)S(1)} collective-permute-done((bf16[200,1152]{1,0:T(8,128)(2,1)}, bf16[200,1152]{1,0:T(8,128)(2,1)S(1)}, u32[]{:S(2)}, u32[]{:S(2)}) %collective-permute-start) | collective-permute-done | bytes 460832 | tf_op jit(solution)/shard_map/while/body/ppermute | solution.py:341
  63.3 0.8 copy.16
  64.1 0.0 collective-permute-done.11.refs_3_
  64.1 0.0 copy-done.3
  64.1 0.0 copy-done.4
  64.1 0.0 copy-done.2
  64.1 0.0 copy-done.6
  64.1 4.6 %first_tile.1 = (f32[768,1152]{1,0:T(8,128)S(1)}, f32[192,1152]{1,0:T(8,128)S(1)}, f32[1,192]{1,0:T(1,128)S(1)}, f32[4,1152]{1,0:T(4,128)S(1)}) custom-call(f32[2]{0:T(128)S(1)} %pad_maximum_fusion.scalars_ref, f32[2,1152]{1,0:T(2,128)S(1)} %copy-done.3, f32[2,1152]{1,0:T(2,128)S(1)} %copy-done.4, bf16[200,1152]{1,0:T(8,128)(2,1)S(1)} %copy-done.6, ...), custom_call_target="tpu_custom_call" | custom-call | flops 1019215872 | bytes 5308416 | tf_op jit(solution)/shard_map/first_tile/pallas_call | solution.py:194
  68.7 0.0 copy-start.1
  68.7 0.9 copy-done.1
  69.6 0.0 collective-permute-done.10.refs_0_
  69.6 0.0 copy-done.8
  69.6 4.9 %last_tile.1 = (f32[192,1152]{1,0:T(8,128)S(1)}, f32[192,1152]{1,0:T(8,128)S(1)}, bf16[384,1152]{1,0:T(8,128)(2,1)}, bf16[200,1152]{1,0:T(8,128)(2,1)S(1)}, f32[4,1152]{1,0:T(4,128)S(1)}) custom-call(f32[2]{0:T(128)S(1)} %pad_maximum_fusion.scalars_ref, f32[2,1152]{1,0:T(2,128)S(1)} %copy-done.3, f32[2,1152]{1,0:T(2,128)S(1)} %copy-done.4, ...), custom_call_target="tpu_custom_call" | custom-call | flops 1019215872 | bytes 5308416 | tf_op jit(solution)/shard_map/last_tile/pallas_call | solution.py:194
  74.5 0.0 copy-done.5
  74.5 0.9 copy-done
  75.4 3.5 %collective-permute-start.12 = (bf16[384,1152]{1,0:T(8,128)(2,1)}, bf16[384,1152]{1,0:T(8,128)(2,1)S(1)}, u32[]{:S(2)}, u32[]{:S(2)}) collective-permute-start(bf16[384,1152]{1,0:T(8,128)(2,1)} %get-tuple-element.90), channel_id=1, source_target_pairs={{0,512},{1,513},{2,514},{3,515},{4,516},{5,517},{6,518},{7,519},{8... | collective-permute-start | bytes 2654216 | tf_op jit(solution)/shard_map/ppermute | solution.py:341
  78.9 6.1 %collective-permute-start.13 = (bf16[200,1152]{1,0:T(8,128)(2,1)S(1)}, bf16[200,1152]{1,0:T(8,128)(2,1)S(1)}, u32[]{:S(2)}, u32[]{:S(2)}) collective-permute-start(bf16[200,1152]{1,0:T(8,128)(2,1)S(1)} %get-tuple-element.93), channel_id=1, source_target_pairs={{0,128},{1,385},{2,130},{3,387},{4,132},{5,389},{6,134},{7,391},{8... | collective-permute-start | bytes 1382408 | tf_op jit(solution)/shard_map/ppermute | solution.py:341
  85.0 21.3 %while.31 = (s32[]{:T(128)}, f32[4,1152]{1,0:T(4,128)S(1)}, s32[]{:T(128)}, s32[]{:T(128)}) while((s32[]{:T(128)}, f32[4,1152]{1,0:T(4,128)S(1)}, s32[]{:T(128)}, s32[]{:T(128)}) %tuple.60), condition=%wide.region_3.4_spmd, body=%wide.region_2.3_spmd.sunk | while | flops 18434 | bytes 516309 | solution.py:345
  85.0 1.9 %collective-permute-start.1 = (f32[4,1152]{1,0:T(4,128)S(1)}, f32[4,1152]{1,0:T(4,128)S(1)}, u32[]{:S(2)}, u32[]{:S(2)}) collective-permute-start(f32[4,1152]{1,0:T(4,128)S(1)} %get-tuple-element.203), channel_id=1, source_target_pairs={{0,1},{1,0},{2,3},{3,2},{4,5},{5,4},{6,7},{7,6},{8,9},{9,8},{10,11... | collective-permute-start | bytes 55304 | tf_op jit(solution)/shard_map/while/body/ppermute | solution.py:341
  86.9 1.2 collective-permute-done.1
  88.1 2.7 %collective-permute-start.2 = (f32[4,1152]{1,0:T(4,128)S(1)}, f32[4,1152]{1,0:T(4,128)S(1)}, u32[]{:S(2)}, u32[]{:S(2)}) collective-permute-start(f32[4,1152]{1,0:T(4,128)S(1)} %add.59), channel_id=1, source_target_pairs={{0,8},{1,9},{2,10},{3,11},{4,12},{5,13},{6,14},{7,15},{8,0},{9,1},... | collective-permute-start | bytes 55304 | tf_op jit(solution)/shard_map/while/body/ppermute | solution.py:341
  90.8 2.9 %collective-permute-done.2 = f32[4,1152]{1,0:T(4,128)S(1)} collective-permute-done((f32[4,1152]{1,0:T(4,128)S(1)}, f32[4,1152]{1,0:T(4,128)S(1)}, u32[]{:S(2)}, u32[]{:S(2)}) %collective-permute-start.2) | collective-permute-done | bytes 18464 | tf_op jit(solution)/shard_map/while/body/ppermute | solution.py:341
  93.7 2.4 %collective-permute-start.3 = (f32[4,1152]{1,0:T(4,128)S(1)}, f32[4,1152]{1,0:T(4,128)S(1)}, u32[]{:S(2)}, u32[]{:S(2)}) collective-permute-start(f32[4,1152]{1,0:T(4,128)S(1)} %add.60), channel_id=1, source_target_pairs={{0,24},{1,25},{2,26},{3,27},{4,28},{5,29},{6,30},{7,31},{8,16},{9,... | collective-permute-start | bytes 55304 | tf_op jit(solution)/shard_map/while/body/ppermute | solution.py:341
  96.1 4.5 %collective-permute-done.3 = f32[4,1152]{1,0:T(4,128)S(1)} collective-permute-done((f32[4,1152]{1,0:T(4,128)S(1)}, f32[4,1152]{1,0:T(4,128)S(1)}, u32[]{:S(2)}, u32[]{:S(2)}) %collective-permute-start.3) | collective-permute-done | bytes 18464 | tf_op jit(solution)/shard_map/while/body/ppermute | solution.py:341
  100.6 2.3 %collective-permute-start.4 = (f32[4,1152]{1,0:T(4,128)S(1)}, f32[4,1152]{1,0:T(4,128)S(1)}, u32[]{:S(2)}, u32[]{:S(2)}) collective-permute-start(f32[4,1152]{1,0:T(4,128)S(1)} %add.61), channel_id=1, source_target_pairs={{0,512},{1,513},{2,514},{3,515},{4,516},{5,517},{6,518},{7,519},{8... | collective-permute-start | bytes 55304 | tf_op jit(solution)/shard_map/while/body/ppermute | solution.py:341
  103.0 3.3 %collective-permute-done.4 = f32[4,1152]{1,0:T(4,128)S(1)} collective-permute-done((f32[4,1152]{1,0:T(4,128)S(1)}, f32[4,1152]{1,0:T(4,128)S(1)}, u32[]{:S(2)}, u32[]{:S(2)}) %collective-permute-start.4) | collective-permute-done | bytes 18464 | tf_op jit(solution)/shard_map/while/body/ppermute | solution.py:341
  106.3 0.0 collective-permute-done.12.refs_1_
  106.3 0.0 copy-start.7
  106.3 0.1 add_convert_fusion
  106.4 5.8 %collective-permute-start.14 = (bf16[192,1152]{1,0:T(8,128)(2,1)S(1)}, bf16[192,1152]{1,0:T(8,128)(2,1)S(1)}, u32[]{:S(2)}, u32[]{:S(2)}) collective-permute-start(bf16[192,1152]{1,0:T(8,128)(2,1)S(1)} %add_convert_fusion), channel_id=1, source_target_pairs={{0,384},{1,129},{2,386},{3,131},{4,388},{5,133},{6,390},{7,135},{8... | collective-permute-start | bytes 1327112 | tf_op jit(solution)/shard_map/ppermute | solution.py:341
  112.2 0.0 collective-permute-done.13.refs_1_
  112.2 0.0 copy-start.9
  112.2 26.9 %while.32 = (s32[]{:T(128)}, f32[4,1152]{1,0:T(4,128)S(1)}, s32[]{:T(128)}, s32[]{:T(128)}) while((s32[]{:T(128)}, f32[4,1152]{1,0:T(4,128)S(1)}, s32[]{:T(128)}, s32[]{:T(128)}) %tuple.63), condition=%wide.region_5.6_spmd, body=%wide.region_4.5_spmd.sunk | while | flops 18434 | bytes 516309 | solution.py:345
  112.2 5.2 %collective-permute-start.5 = (f32[4,1152]{1,0:T(4,128)S(1)}, f32[4,1152]{1,0:T(4,128)S(1)}, u32[]{:S(2)}, u32[]{:S(2)}) collective-permute-start(f32[4,1152]{1,0:T(4,128)S(1)} %get-tuple-element.215), channel_id=1, source_target_pairs={{0,518},{1,519},{2,512},{3,513},{4,514},{5,515},{6,516},{7,517},{8... | collective-permute-start | bytes 55304 | tf_op jit(solution)/shard_map/while/body/ppermute | solution.py:341
  117.4 1.7 %collective-permute-done.5 = f32[4,1152]{1,0:T(4,128)S(1)} collective-permute-done((f32[4,1152]{1,0:T(4,128)S(1)}, f32[4,1152]{1,0:T(4,128)S(1)}, u32[]{:S(2)}, u32[]{:S(2)}) %collective-permute-start.5) | collective-permute-done | bytes 18464 | tf_op jit(solution)/shard_map/while/body/ppermute | solution.py:341
  119.1 4.4 %collective-permute-start.6 = (f32[4,1152]{1,0:T(4,128)S(1)}, f32[4,1152]{1,0:T(4,128)S(1)}, u32[]{:S(2)}, u32[]{:S(2)}) collective-permute-start(f32[4,1152]{1,0:T(4,128)S(1)} %add.64), channel_id=1, source_target_pairs={{0,514},{1,515},{2,516},{3,517},{4,518},{5,519},{6,512},{7,513},{8... | collective-permute-start | bytes 55304 | tf_op jit(solution)/shard_map/while/body/ppermute | solution.py:341
  123.5 3.1 %collective-permute-done.6 = f32[4,1152]{1,0:T(4,128)S(1)} collective-permute-done((f32[4,1152]{1,0:T(4,128)S(1)}, f32[4,1152]{1,0:T(4,128)S(1)}, u32[]{:S(2)}, u32[]{:S(2)}) %collective-permute-start.6) | collective-permute-done | bytes 18464 | tf_op jit(solution)/shard_map/while/body/ppermute | solution.py:341
  126.6 1.9 %collective-permute-start.7 = (f32[4,1152]{1,0:T(4,128)S(1)}, f32[4,1152]{1,0:T(4,128)S(1)}, u32[]{:S(2)}, u32[]{:S(2)}) collective-permute-start(f32[4,1152]{1,0:T(4,128)S(1)} %add.65), channel_id=1, source_target_pairs={{0,32},{1,33},{2,34},{3,35},{4,36},{5,37},{6,38},{7,39},{8,40},{9,... | collective-permute-start | bytes 55304 | tf_op jit(solution)/shard_map/while/body/ppermute | solution.py:341
  128.5 3.7 %collective-permute-done.7 = f32[4,1152]{1,0:T(4,128)S(1)} collective-permute-done((f32[4,1152]{1,0:T(4,128)S(1)}, f32[4,1152]{1,0:T(4,128)S(1)}, u32[]{:S(2)}, u32[]{:S(2)}) %collective-permute-start.7) | collective-permute-done | bytes 18464 | tf_op jit(solution)/shard_map/while/body/ppermute | solution.py:341
  132.2 4.3 %collective-permute-start.8 = (f32[4,1152]{1,0:T(4,128)S(1)}, f32[4,1152]{1,0:T(4,128)S(1)}, u32[]{:S(2)}, u32[]{:S(2)}) collective-permute-start(f32[4,1152]{1,0:T(4,128)S(1)} %add.66), channel_id=1, source_target_pairs={{0,480},{1,481},{2,482},{3,483},{4,484},{5,485},{6,486},{7,487},{8... | collective-permute-start | bytes 55304 | tf_op jit(solution)/shard_map/while/body/ppermute | solution.py:341
  136.6 2.5 %collective-permute-done.8 = f32[4,1152]{1,0:T(4,128)S(1)} collective-permute-done((f32[4,1152]{1,0:T(4,128)S(1)}, f32[4,1152]{1,0:T(4,128)S(1)}, u32[]{:S(2)}, u32[]{:S(2)}) %collective-permute-start.8) | collective-permute-done | bytes 18464 | tf_op jit(solution)/shard_map/while/body/ppermute | solution.py:341
  139.1 0.0 collective-permute-done.14.refs_2_
  139.1 0.0 copy-start.10
  139.1 3.5 %collective-permute-start.15 = (f32[4,1152]{1,0:T(4,128)S(1)}, f32[4,1152]{1,0:T(4,128)S(1)}, u32[]{:S(2)}, u32[]{:S(2)}) collective-permute-start(f32[4,1152]{1,0:T(4,128)S(1)} %get-tuple-element.96), channel_id=1, source_target_pairs={{0,96},{1,97},{2,98},{3,99},{4,100},{5,101},{6,102},{7,103},{8,104... | collective-permute-start | bytes 55304 | tf_op jit(solution)/shard_map/ppermute | solution.py:341
  142.6 0.0 copy-done.9
  142.6 3.2 %backward_norm.2 = (bf16[192,1152]{1,0:T(8,128)(2,1)}, f32[1,192]{1,0:T(1,128)}) custom-call(bf16[192,1152]{1,0:T(8,128)(2,1)} %bitcast.6, f32[2,1152]{1,0:T(2,128)} %gains_ref.9, f32[2,1152]{1,0:T(2,128)} %shifts_ref.9, f32[1]{0:T(128)S(6)} %exp.3.scale_ref, f32[192,1152]{1,0:T(8,128)} %copy-done.1, bf16[200,1152]{1,0:T(8,128)(2,1)} %copy-done.9, ...), custom_call_target="tpu_custom_call" | custom-call | flops 8847360 | bytes 2654208 | tf_op jit(solution)/shard_map/backward_norm/pallas_call | solution.py:253
  145.8 0.8 collective-permute-done.15
  146.7 7.4 %collective-permute-start.16 = (f32[4,1152]{1,0:T(4,128)S(1)}, f32[4,1152]{1,0:T(4,128)S(1)}, u32[]{:S(2)}, u32[]{:S(2)}) collective-permute-start(f32[4,1152]{1,0:T(4,128)S(1)} %add.43), channel_id=1, source_target_pairs={{0,352},{1,353},{2,354},{3,355},{4,356},{5,357},{6,358},{7,359},{8... | collective-permute-start | bytes 55304 | tf_op jit(solution)/shard_map/ppermute | solution.py:341
  154.1 0.0 copy-done.7
  154.1 0.0 copy-done.10
  154.1 3.5 %backward_norm.3 = bf16[192,1152]{1,0:T(8,128)(2,1)} custom-call(bf16[192,1152]{1,0:T(8,128)(2,1)} %bitcast.8, f32[2,1152]{1,0:T(2,128)} %gains_ref.9, f32[2,1152]{1,0:T(2,128)} %shifts_ref.9, f32[1]{0:T(128)S(6)} %exp.3.scale_ref, f32[192,1152]{1,0:T(8,128)} %copy-done, bf16[384,1152]{1,0:T(8,128)(2,1)} %copy-done.7, bf16[192,1152]{1,0:T(8,128)(2,1)} %copy-done.10), custom_call_target="tpu_custom_call" | custom-call | flops 8847360 | bytes 2654208 | tf_op jit(solution)/shard_map/backward_norm/pallas_call | solution.py:253
  157.6 0.8 collective-permute-done.16
  158.3 0.6 fusion
  (15 shorter events, 0.1 us)
Async XLA Ops:
  0.6 63.5 %copy-start.3 = (f32[2,1152]{1,0:T(2,128)S(1)}, f32[2,1152]{1,0:T(2,128)}, u32[]{:S(2)}) copy-start(f32[2,1152]{1,0:T(2,128)} %gains_ref.9) | copy-start | bytes 27652
  0.6 63.5 %copy-start.4 = (f32[2,1152]{1,0:T(2,128)S(1)}, f32[2,1152]{1,0:T(2,128)}, u32[]{:S(2)}) copy-start(f32[2,1152]{1,0:T(2,128)} %shifts_ref.9) | copy-start | bytes 27652
  4.8 59.3 %copy-start.2 = (bf16[200,1152]{1,0:T(8,128)(2,1)S(1)}, bf16[200,1152]{1,0:T(8,128)(2,1)}, u32[]{:S(2)}) copy-start(bf16[200,1152]{1,0:T(8,128)(2,1)} %get-tuple-element.82.refs_1_) | copy-start | bytes 1382404
  4.8 59.3 %copy-start.6 = (bf16[200,1152]{1,0:T(8,128)(2,1)S(1)}, bf16[200,1152]{1,0:T(8,128)(2,1)}, u32[]{:S(2)}) copy-start(bf16[200,1152]{1,0:T(8,128)(2,1)} %get-tuple-element.83.refs_0_) | copy-start | bytes 1382404
  4.8 39.7 %collective-permute-start.9 = (bf16[200,1152]{1,0:T(8,128)(2,1)}, bf16[200,1152]{1,0:T(8,128)(2,1)S(1)}, u32[]{:S(2)}, u32[]{:S(2)}) collective-permute-start(bf16[200,1152]{1,0:T(8,128)(2,1)} %get-tuple-element.82.refs_1_), channel_id=1, source_target_pairs={{0,384},{1,129},{2,386},{3,131},{4,388},{5,133},{6,390},{7,135},{8... | collective-permute-start | bytes 1382408 | tf_op jit(solution)/shard_map/ppermute | solution.py:341
  23.1 41.0 %collective-permute-start.11 = (bf16[200,1152]{1,0:T(8,128)(2,1)}, bf16[200,1152]{1,0:T(8,128)(2,1)S(1)}, u32[]{:S(2)}, u32[]{:S(2)}) collective-permute-start(bf16[200,1152]{1,0:T(8,128)(2,1)} %get-tuple-element.82.refs_1_), channel_id=1, source_target_pairs={{0,512},{1,513},{2,514},{3,515},{4,516},{5,517},{6,518},{7,519},{8... | collective-permute-start | bytes 1382408 | tf_op jit(solution)/shard_map/ppermute | solution.py:341
  44.4 25.2 %collective-permute-start.10 = (bf16[200,1152]{1,0:T(8,128)(2,1)}, bf16[200,1152]{1,0:T(8,128)(2,1)S(1)}, u32[]{:S(2)}, u32[]{:S(2)}) collective-permute-start(bf16[200,1152]{1,0:T(8,128)(2,1)} %get-tuple-element.83.refs_0_), channel_id=1, source_target_pairs={{0,128},{1,385},{2,130},{3,387},{4,132},{5,389},{6,134},{7,391},{8... | collective-permute-start | bytes 1382408 | tf_op jit(solution)/shard_map/ppermute | solution.py:341
  50.0 13.2 %collective-permute-start = (bf16[200,1152]{1,0:T(8,128)(2,1)}, bf16[200,1152]{1,0:T(8,128)(2,1)S(1)}, u32[]{:S(2)}, u32[]{:S(2)}) collective-permute-start(bf16[200,1152]{1,0:T(8,128)(2,1)} %get-tuple-element.191), channel_id=1, source_target_pairs={{0,512},{1,513},{2,514},{3,515},{4,516},{5,517},{6,518},{7,519},{8... | collective-permute-start | bytes 1382408 | tf_op jit(solution)/shard_map/while/body/ppermute | solution.py:341
  64.1 5.5 %copy-start.8 = (bf16[200,1152]{1,0:T(8,128)(2,1)S(1)}, bf16[200,1152]{1,0:T(8,128)(2,1)}, u32[]{:S(2)}) copy-start(bf16[200,1152]{1,0:T(8,128)(2,1)} %get-tuple-element.85.refs_4_) | copy-start | bytes 1382404
  68.7 0.9 copy-start.1
  69.6 4.9 %copy-start.5 = (f32[1,192]{1,0:T(1,128)}, f32[1,192]{1,0:T(1,128)S(1)}, u32[]{:S(2)}) copy-start(f32[1,192]{1,0:T(1,128)S(1)} %get-tuple-element.99.refs_2_) | copy-start | bytes 2308
  74.5 0.9 copy-start
  75.4 30.8 %collective-permute-start.12 = (bf16[384,1152]{1,0:T(8,128)(2,1)}, bf16[384,1152]{1,0:T(8,128)(2,1)S(1)}, u32[]{:S(2)}, u32[]{:S(2)}) collective-permute-start(bf16[384,1152]{1,0:T(8,128)(2,1)} %get-tuple-element.90), channel_id=1, source_target_pairs={{0,512},{1,513},{2,514},{3,515},{4,516},{5,517},{6,518},{7,519},{8... | collective-permute-start | bytes 2654216 | tf_op jit(solution)/shard_map/ppermute | solution.py:341
  78.9 33.3 %collective-permute-start.13 = (bf16[200,1152]{1,0:T(8,128)(2,1)S(1)}, bf16[200,1152]{1,0:T(8,128)(2,1)S(1)}, u32[]{:S(2)}, u32[]{:S(2)}) collective-permute-start(bf16[200,1152]{1,0:T(8,128)(2,1)S(1)} %get-tuple-element.93), channel_id=1, source_target_pairs={{0,128},{1,385},{2,130},{3,387},{4,132},{5,389},{6,134},{7,391},{8... | collective-permute-start | bytes 1382408 | tf_op jit(solution)/shard_map/ppermute | solution.py:341
  85.0 3.1 %collective-permute-start.1 = (f32[4,1152]{1,0:T(4,128)S(1)}, f32[4,1152]{1,0:T(4,128)S(1)}, u32[]{:S(2)}, u32[]{:S(2)}) collective-permute-start(f32[4,1152]{1,0:T(4,128)S(1)} %get-tuple-element.203), channel_id=1, source_target_pairs={{0,1},{1,0},{2,3},{3,2},{4,5},{5,4},{6,7},{7,6},{8,9},{9,8},{10,11... | collective-permute-start | bytes 55304 | tf_op jit(solution)/shard_map/while/body/ppermute | solution.py:341
  88.1 5.6 %collective-permute-start.2 = (f32[4,1152]{1,0:T(4,128)S(1)}, f32[4,1152]{1,0:T(4,128)S(1)}, u32[]{:S(2)}, u32[]{:S(2)}) collective-permute-start(f32[4,1152]{1,0:T(4,128)S(1)} %add.59), channel_id=1, source_target_pairs={{0,8},{1,9},{2,10},{3,11},{4,12},{5,13},{6,14},{7,15},{8,0},{9,1},... | collective-permute-start | bytes 55304 | tf_op jit(solution)/shard_map/while/body/ppermute | solution.py:341
  93.7 6.9 %collective-permute-start.3 = (f32[4,1152]{1,0:T(4,128)S(1)}, f32[4,1152]{1,0:T(4,128)S(1)}, u32[]{:S(2)}, u32[]{:S(2)}) collective-permute-start(f32[4,1152]{1,0:T(4,128)S(1)} %add.60), channel_id=1, source_target_pairs={{0,24},{1,25},{2,26},{3,27},{4,28},{5,29},{6,30},{7,31},{8,16},{9,... | collective-permute-start | bytes 55304 | tf_op jit(solution)/shard_map/while/body/ppermute | solution.py:341
  100.6 5.6 %collective-permute-start.4 = (f32[4,1152]{1,0:T(4,128)S(1)}, f32[4,1152]{1,0:T(4,128)S(1)}, u32[]{:S(2)}, u32[]{:S(2)}) collective-permute-start(f32[4,1152]{1,0:T(4,128)S(1)} %add.61), channel_id=1, source_target_pairs={{0,512},{1,513},{2,514},{3,515},{4,516},{5,517},{6,518},{7,519},{8... | collective-permute-start | bytes 55304 | tf_op jit(solution)/shard_map/while/body/ppermute | solution.py:341
  106.3 47.8 %copy-start.7 = (bf16[384,1152]{1,0:T(8,128)(2,1)}, bf16[384,1152]{1,0:T(8,128)(2,1)S(1)}, u32[]{:S(2)}) copy-start(bf16[384,1152]{1,0:T(8,128)(2,1)S(1)} %collective-permute-done.12.refs_1_) | copy-start | bytes 2654212
  106.4 32.7 %collective-permute-start.14 = (bf16[192,1152]{1,0:T(8,128)(2,1)S(1)}, bf16[192,1152]{1,0:T(8,128)(2,1)S(1)}, u32[]{:S(2)}, u32[]{:S(2)}) collective-permute-start(bf16[192,1152]{1,0:T(8,128)(2,1)S(1)} %add_convert_fusion), channel_id=1, source_target_pairs={{0,384},{1,129},{2,386},{3,131},{4,388},{5,133},{6,390},{7,135},{8... | collective-permute-start | bytes 1327112 | tf_op jit(solution)/shard_map/ppermute | solution.py:341
  112.2 30.5 %copy-start.9 = (bf16[200,1152]{1,0:T(8,128)(2,1)}, bf16[200,1152]{1,0:T(8,128)(2,1)S(1)}, u32[]{:S(2)}) copy-start(bf16[200,1152]{1,0:T(8,128)(2,1)S(1)} %collective-permute-done.13.refs_1_) | copy-start | bytes 1382404
  112.2 6.9 %collective-permute-start.5 = (f32[4,1152]{1,0:T(4,128)S(1)}, f32[4,1152]{1,0:T(4,128)S(1)}, u32[]{:S(2)}, u32[]{:S(2)}) collective-permute-start(f32[4,1152]{1,0:T(4,128)S(1)} %get-tuple-element.215), channel_id=1, source_target_pairs={{0,518},{1,519},{2,512},{3,513},{4,514},{5,515},{6,516},{7,517},{8... | collective-permute-start | bytes 55304 | tf_op jit(solution)/shard_map/while/body/ppermute | solution.py:341
  119.1 7.4 %collective-permute-start.6 = (f32[4,1152]{1,0:T(4,128)S(1)}, f32[4,1152]{1,0:T(4,128)S(1)}, u32[]{:S(2)}, u32[]{:S(2)}) collective-permute-start(f32[4,1152]{1,0:T(4,128)S(1)} %add.64), channel_id=1, source_target_pairs={{0,514},{1,515},{2,516},{3,517},{4,518},{5,519},{6,512},{7,513},{8... | collective-permute-start | bytes 55304 | tf_op jit(solution)/shard_map/while/body/ppermute | solution.py:341
  126.6 5.6 %collective-permute-start.7 = (f32[4,1152]{1,0:T(4,128)S(1)}, f32[4,1152]{1,0:T(4,128)S(1)}, u32[]{:S(2)}, u32[]{:S(2)}) collective-permute-start(f32[4,1152]{1,0:T(4,128)S(1)} %add.65), channel_id=1, source_target_pairs={{0,32},{1,33},{2,34},{3,35},{4,36},{5,37},{6,38},{7,39},{8,40},{9,... | collective-permute-start | bytes 55304 | tf_op jit(solution)/shard_map/while/body/ppermute | solution.py:341
  132.2 6.9 %collective-permute-start.8 = (f32[4,1152]{1,0:T(4,128)S(1)}, f32[4,1152]{1,0:T(4,128)S(1)}, u32[]{:S(2)}, u32[]{:S(2)}) collective-permute-start(f32[4,1152]{1,0:T(4,128)S(1)} %add.66), channel_id=1, source_target_pairs={{0,480},{1,481},{2,482},{3,483},{4,484},{5,485},{6,486},{7,487},{8... | collective-permute-start | bytes 55304 | tf_op jit(solution)/shard_map/while/body/ppermute | solution.py:341
  139.1 15.0 %copy-start.10 = (bf16[192,1152]{1,0:T(8,128)(2,1)}, bf16[192,1152]{1,0:T(8,128)(2,1)S(1)}, u32[]{:S(2)}) copy-start(bf16[192,1152]{1,0:T(8,128)(2,1)S(1)} %collective-permute-done.14.refs_2_) | copy-start | bytes 1327108
  139.1 7.6 %collective-permute-start.15 = (f32[4,1152]{1,0:T(4,128)S(1)}, f32[4,1152]{1,0:T(4,128)S(1)}, u32[]{:S(2)}, u32[]{:S(2)}) collective-permute-start(f32[4,1152]{1,0:T(4,128)S(1)} %get-tuple-element.96), channel_id=1, source_target_pairs={{0,96},{1,97},{2,98},{3,99},{4,100},{5,101},{6,102},{7,103},{8,104... | collective-permute-start | bytes 55304 | tf_op jit(solution)/shard_map/ppermute | solution.py:341
  146.7 11.7 %collective-permute-start.16 = (f32[4,1152]{1,0:T(4,128)S(1)}, f32[4,1152]{1,0:T(4,128)S(1)}, u32[]{:S(2)}, u32[]{:S(2)}) collective-permute-start(f32[4,1152]{1,0:T(4,128)S(1)} %add.43), channel_id=1, source_target_pairs={{0,352},{1,353},{2,354},{3,355},{4,356},{5,357},{6,358},{7,359},{8... | collective-permute-start | bytes 55304 | tf_op jit(solution)/shard_map/ppermute | solution.py:341

commit v7 on v6

--- a/solution.py
+++ b/solution.py
@@ -68,37 +68,33 @@
     return normed, rstd, unnormed, inverse
 
 
-def forward_kernel(image_ref, text_ref, gains_ref, shifts_ref, image_emb_ref, text_emb_ref, keep):
-    for tower, (feats_ref, emb_ref) in enumerate(
-        ((image_ref, image_emb_ref), (text_ref, text_emb_ref))
-    ):
-        gain = gains_ref[tower : tower + 1, :]
-        shift = shifts_ref[tower : tower + 1, :]
-
-        @pl.loop(0, feats_ref.shape[0] // ROW_BLOCK, unroll=UNROLL)
-        def _(step):
-            rows = pl.ds(pl.multiple_of(step * ROW_BLOCK, ROW_BLOCK), ROW_BLOCK)
-            feats = feats_ref[rows, :].astype(jnp.float32)
-            _, _, unnormed, inverse = norm_rows(feats, gain, shift)
-            emb_ref[rows, :] = (unnormed * inverse).astype(jnp.bfloat16)
-            keep[rows, :] = jnp.broadcast_to(inverse, (ROW_BLOCK, 128))
-
-        put_line(emb_ref, to_lanes(keep[:, :1]))
-
-
-def forward_norms(image_feats, text_feats, gains, shifts):
-    rows, width = image_feats.shape
-    emb = jax.ShapeDtypeStruct((rows + EXTRA, width), jnp.bfloat16)
+def forward_kernel(tower, feats_ref, gains_ref, shifts_ref, emb_ref, keep):
+    gain = gains_ref[tower : tower + 1, :]
+    shift = shifts_ref[tower : tower + 1, :]
+
+    @pl.loop(0, feats_ref.shape[0] // ROW_BLOCK, unroll=UNROLL)
+    def _(step):
+        rows = pl.ds(pl.multiple_of(step * ROW_BLOCK, ROW_BLOCK), ROW_BLOCK)
+        feats = feats_ref[rows, :].astype(jnp.float32)
+        _, _, unnormed, inverse = norm_rows(feats, gain, shift)
+        emb_ref[rows, :] = (unnormed * inverse).astype(jnp.bfloat16)
+        keep[rows, :] = jnp.broadcast_to(inverse, (ROW_BLOCK, 128))
+
+    put_line(emb_ref, to_lanes(keep[:, :1]))
+
+
+def forward_norm(tower, feats, gains, shifts):
+    rows, width = feats.shape
     return pl.pallas_call(
-        forward_kernel,
-        out_shape=(emb, emb),
+        functools.partial(forward_kernel, tower),
+        out_shape=jax.ShapeDtypeStruct((rows + EXTRA, width), jnp.bfloat16),
         scratch_shapes=[pltpu.VMEM((rows, 128), jnp.float32)],
         compiler_params=pltpu.CompilerParams(vmem_limit_bytes=VMEM_LIMIT),
         cost_estimate=pl.CostEstimate(
-            flops=40 * rows * width, bytes_accessed=8 * rows * width, transcendentals=0
+            flops=20 * rows * width, bytes_accessed=4 * rows * width, transcendentals=0
         ),
-        name="forward_norms",
-    )(image_feats, text_feats, gains, shifts)
+        name="forward_norm",
+    )(feats, gains, shifts)
 
 
 def add_sums(units, parts, inverses):
@@ -367,7 +363,8 @@
         scale = jnp.exp(log_scale)
         scalars = jnp.concatenate([scale, logit_bias])
         turns = jnp.where(log_scale[0] == log_scale[0], 1, 0)
-        image, text = forward_norms(image_feats[0], text_feats[0], gains, shifts)
+        text = forward_norm(1, text_feats[0], gains, shifts)
+        image = forward_norm(0, image_feats[0], gains, shifts)
         rows = image_feats.shape[1]
 
         text_z = send(text, text_pairs)

time: 160 us -> 158 us (0.988)
  waiting for transfers between devices: 52.1 us -> 49.2 us
    ppermute x17, waiting for transfers between devices: 52.1 us -> 49.2 us  [send(): return lax.ppermute(value, AXES, pairs)]
    pallas_call x1 -> x2, Pallas kernels: 4.13 us -> 5.82 us  [forward_norm(): pl.pallas_call(functools.partial(forward_kernel, tower), out_shape=jax.Sh...]
  transfers between devices with their start and end apart: 17 -> 17, of which waited for: 12 -> 12; matrix products, arithmetic and copies ran while one was open for 1% -> 1% of each run, Pallas kernels for 7% -> 9%
where the time goes in v7:
time: 158 us
  starting transfers between devices  80.1 us (51%)
  waiting for transfers between devices  49.2 us (31%)
  Pallas kernels  21.7 us (14%)
  local copies, waits for them, and re-layouts  4.08 us (3%)
  between operations  2.17 us (1%)
    ppermute x17, starting transfers between devices, send(): return lax.ppermute(value, AXES, pairs)  80.1 us
    ppermute x17, waiting for transfers between devices, send(): return lax.ppermute(value, AXES, pairs)  49.2 us
    pallas_call x2, Pallas kernels, tile(): pl.pallas_call(functools.partial(tile_kernel, final), out_shape=tuple(out...  9.2 us
    pallas_call x2, Pallas kernels, backward_norm(): pl.pallas_call(functools.partial(backward_kernel, tower, firsts), out_sha...  6.65 us
    pallas_call x2, Pallas kernels, forward_norm(): pl.pallas_call(functools.partial(forward_kernel, tower), out_shape=jax.Sh...  5.82 us
  transfers between devices with their start and end apart: 17, of which 12 were waited for; matrix products, arithmetic and copies ran while one was open for 1% of the time, Pallas kernels for 9%

profile of v7, /device:TPU:6, one launch (start us, length us, event | category | flops | bytes accessed | tf_op | source)
XLA Modules:
  0.0 157.6 jit_solution(4281391908944483303)
XLA Ops:
  0.6 0.0 copy-start.4
  0.6 0.0 copy-start.5
  0.7 2.9 %forward_norm.3.refs_1_ = bf16[200,1152]{1,0:T(8,128)(2,1)} custom-call(bf16[192,1152]{1,0:T(8,128)(2,1)} %bitcast.7, f32[2,1152]{1,0:T(2,128)} %gains_ref.11, f32[2,1152]{1,0:T(2,128)} %shifts_ref.11), custom_call_target="tpu_custom_call" | custom-call | flops 4423680 | bytes 884736 | tf_op jit(solution)/shard_map/forward_norm/pallas_call | solution.py:88
  3.6 18.3 %collective-permute-start.9 = (bf16[200,1152]{1,0:T(8,128)(2,1)}, bf16[200,1152]{1,0:T(8,128)(2,1)S(1)}, u32[]{:S(2)}, u32[]{:S(2)}) collective-permute-start(bf16[200,1152]{1,0:T(8,128)(2,1)} %forward_norm.3.refs_1_), channel_id=1, source_target_pairs={{0,384},{1,129},{2,386},{3,131},{4,388},{5,133},{6,390},{7,135},{8... | collective-permute-start | bytes 1382408 | tf_op jit(solution)/shard_map/ppermute | solution.py:337
  21.9 3.5 %collective-permute-start.11 = (bf16[200,1152]{1,0:T(8,128)(2,1)}, bf16[200,1152]{1,0:T(8,128)(2,1)S(1)}, u32[]{:S(2)}, u32[]{:S(2)}) collective-permute-start(bf16[200,1152]{1,0:T(8,128)(2,1)} %forward_norm.3.refs_1_), channel_id=1, source_target_pairs={{0,512},{1,513},{2,514},{3,515},{4,516},{5,517},{6,518},{7,519},{8... | collective-permute-start | bytes 1382408 | tf_op jit(solution)/shard_map/ppermute | solution.py:337
  25.4 2.9 %forward_norm.2.refs_0_ = bf16[200,1152]{1,0:T(8,128)(2,1)} custom-call(bf16[192,1152]{1,0:T(8,128)(2,1)} %bitcast.5, f32[2,1152]{1,0:T(2,128)} %gains_ref.11, f32[2,1152]{1,0:T(2,128)} %shifts_ref.11), custom_call_target="tpu_custom_call" | custom-call | flops 4423680 | bytes 884736 | tf_op jit(solution)/shard_map/forward_norm/pallas_call | solution.py:88
  28.3 14.9 %collective-permute-done.9.refs_2_ = bf16[200,1152]{1,0:T(8,128)(2,1)S(1)} collective-permute-done((bf16[200,1152]{1,0:T(8,128)(2,1)}, bf16[200,1152]{1,0:T(8,128)(2,1)S(1)}, u32[]{:S(2)}, u32[]{:S(2)}) %collective-permute-start.9) | collective-permute-done | bytes 460832 | tf_op jit(solution)/shard_map/ppermute | solution.py:337
  43.2 3.4 %collective-permute-start.10 = (bf16[200,1152]{1,0:T(8,128)(2,1)}, bf16[200,1152]{1,0:T(8,128)(2,1)S(1)}, u32[]{:S(2)}, u32[]{:S(2)}) collective-permute-start(bf16[200,1152]{1,0:T(8,128)(2,1)} %forward_norm.2.refs_0_), channel_id=1, source_target_pairs={{0,128},{1,385},{2,130},{3,387},{4,132},{5,389},{6,134},{7,391},{8... | collective-permute-start | bytes 1382408 | tf_op jit(solution)/shard_map/ppermute | solution.py:337
  48.0 0.1 pad_maximum_fusion.scalars_ref
  48.0 0.8 copy.12
  48.8 14.1 %while.30 = (s32[]{:T(128)}, bf16[200,1152]{1,0:T(8,128)(2,1)}, s32[]{:T(128)}, s32[]{:T(128)}) while((s32[]{:T(128)}, bf16[200,1152]{1,0:T(8,128)(2,1)}, s32[]{:T(128)}, s32[]{:T(128)}) %tuple.57), condition=%wide.region_1.2_spmd, body=%wide.region_0.1_spmd.sunk | while | flops 2 | bytes 2764893 | solution.py:341
  48.8 3.5 %collective-permute-start = (bf16[200,1152]{1,0:T(8,128)(2,1)}, bf16[200,1152]{1,0:T(8,128)(2,1)S(1)}, u32[]{:S(2)}, u32[]{:S(2)}) collective-permute-start(bf16[200,1152]{1,0:T(8,128)(2,1)} %get-tuple-element.187), channel_id=1, source_target_pairs={{0,512},{1,513},{2,514},{3,515},{4,516},{5,517},{6,518},{7,519},{8... | collective-permute-start | bytes 1382408 | tf_op jit(solution)/shard_map/while/body/ppermute | solution.py:337
  52.3 9.8 %collective-permute-done = bf16[200,1152]{1,0:T(8,128)(2,1)S(1)} collective-permute-done((bf16[200,1152]{1,0:T(8,128)(2,1)}, bf16[200,1152]{1,0:T(8,128)(2,1)S(1)}, u32[]{:S(2)}, u32[]{:S(2)}) %collective-permute-start) | collective-permute-done | bytes 460832 | tf_op jit(solution)/shard_map/while/body/ppermute | solution.py:337
  62.1 0.8 copy.16
  62.9 0.0 collective-permute-done.11.refs_3_
  62.9 0.0 copy-done.4
  62.9 0.0 copy-done.5
  62.9 0.0 copy-done
  62.9 0.0 copy-done.3
  62.9 4.4 %first_tile.1 = (f32[768,1152]{1,0:T(8,128)S(1)}, f32[192,1152]{1,0:T(8,128)S(1)}, f32[1,192]{1,0:T(1,128)S(1)}, f32[4,1152]{1,0:T(4,128)S(1)}) custom-call(f32[2]{0:T(128)S(1)} %pad_maximum_fusion.scalars_ref, f32[2,1152]{1,0:T(2,128)S(1)} %copy-done.4, f32[2,1152]{1,0:T(2,128)S(1)} %copy-done.5, bf16[200,1152]{1,0:T(8,128)(2,1)S(1)} %copy-done.3, ...), custom_call_target="tpu_custom_call" | custom-call | flops 1019215872 | bytes 5308416 | tf_op jit(solution)/shard_map/first_tile/pallas_call | solution.py:190
  67.3 0.0 copy-start.2
  67.3 0.9 copy-done.2
  68.3 0.0 collective-permute-done.10.refs_0_
  68.3 0.0 copy-done.8
  68.3 4.8 %last_tile.1 = (f32[192,1152]{1,0:T(8,128)S(1)}, f32[192,1152]{1,0:T(8,128)S(1)}, bf16[384,1152]{1,0:T(8,128)(2,1)}, bf16[200,1152]{1,0:T(8,128)(2,1)S(1)}, f32[4,1152]{1,0:T(4,128)S(1)}) custom-call(f32[2]{0:T(128)S(1)} %pad_maximum_fusion.scalars_ref, f32[2,1152]{1,0:T(2,128)S(1)} %copy-done.4, f32[2,1152]{1,0:T(2,128)S(1)} %copy-done.5, ...), custom_call_target="tpu_custom_call" | custom-call | flops 1019215872 | bytes 5308416 | tf_op jit(solution)/shard_map/last_tile/pallas_call | solution.py:190
  73.1 0.0 copy-done.6
  73.1 0.9 copy-done.1
  74.0 3.5 %collective-permute-start.12 = (bf16[384,1152]{1,0:T(8,128)(2,1)}, bf16[384,1152]{1,0:T(8,128)(2,1)S(1)}, u32[]{:S(2)}, u32[]{:S(2)}) collective-permute-start(bf16[384,1152]{1,0:T(8,128)(2,1)} %get-tuple-element.86), channel_id=1, source_target_pairs={{0,512},{1,513},{2,514},{3,515},{4,516},{5,517},{6,518},{7,519},{8... | collective-permute-start | bytes 2654216 | tf_op jit(solution)/shard_map/ppermute | solution.py:337
  77.5 6.1 %collective-permute-start.13 = (bf16[200,1152]{1,0:T(8,128)(2,1)S(1)}, bf16[200,1152]{1,0:T(8,128)(2,1)S(1)}, u32[]{:S(2)}, u32[]{:S(2)}) collective-permute-start(bf16[200,1152]{1,0:T(8,128)(2,1)S(1)} %get-tuple-element.89), channel_id=1, source_target_pairs={{0,128},{1,385},{2,130},{3,387},{4,132},{5,389},{6,134},{7,391},{8... | collective-permute-start | bytes 1382408 | tf_op jit(solution)/shard_map/ppermute | solution.py:337
  83.5 21.3 %while.31 = (s32[]{:T(128)}, f32[4,1152]{1,0:T(4,128)S(1)}, s32[]{:T(128)}, s32[]{:T(128)}) while((s32[]{:T(128)}, f32[4,1152]{1,0:T(4,128)S(1)}, s32[]{:T(128)}, s32[]{:T(128)}) %tuple.60), condition=%wide.region_3.4_spmd, body=%wide.region_2.3_spmd.sunk | while | flops 18434 | bytes 516309 | solution.py:341
  83.5 1.9 %collective-permute-start.1 = (f32[4,1152]{1,0:T(4,128)S(1)}, f32[4,1152]{1,0:T(4,128)S(1)}, u32[]{:S(2)}, u32[]{:S(2)}) collective-permute-start(f32[4,1152]{1,0:T(4,128)S(1)} %get-tuple-element.199), channel_id=1, source_target_pairs={{0,1},{1,0},{2,3},{3,2},{4,5},{5,4},{6,7},{7,6},{8,9},{9,8},{10,11... | collective-permute-start | bytes 55304 | tf_op jit(solution)/shard_map/while/body/ppermute | solution.py:337
  85.5 1.2 collective-permute-done.1
  86.6 2.7 %collective-permute-start.2 = (f32[4,1152]{1,0:T(4,128)S(1)}, f32[4,1152]{1,0:T(4,128)S(1)}, u32[]{:S(2)}, u32[]{:S(2)}) collective-permute-start(f32[4,1152]{1,0:T(4,128)S(1)} %add.59), channel_id=1, source_target_pairs={{0,8},{1,9},{2,10},{3,11},{4,12},{5,13},{6,14},{7,15},{8,0},{9,1},... | collective-permute-start | bytes 55304 | tf_op jit(solution)/shard_map/while/body/ppermute | solution.py:337
  89.4 2.9 %collective-permute-done.2 = f32[4,1152]{1,0:T(4,128)S(1)} collective-permute-done((f32[4,1152]{1,0:T(4,128)S(1)}, f32[4,1152]{1,0:T(4,128)S(1)}, u32[]{:S(2)}, u32[]{:S(2)}) %collective-permute-start.2) | collective-permute-done | bytes 18464 | tf_op jit(solution)/shard_map/while/body/ppermute | solution.py:337
  92.3 2.4 %collective-permute-start.3 = (f32[4,1152]{1,0:T(4,128)S(1)}, f32[4,1152]{1,0:T(4,128)S(1)}, u32[]{:S(2)}, u32[]{:S(2)}) collective-permute-start(f32[4,1152]{1,0:T(4,128)S(1)} %add.60), channel_id=1, source_target_pairs={{0,24},{1,25},{2,26},{3,27},{4,28},{5,29},{6,30},{7,31},{8,16},{9,... | collective-permute-start | bytes 55304 | tf_op jit(solution)/shard_map/while/body/ppermute | solution.py:337
  94.7 4.5 %collective-permute-done.3 = f32[4,1152]{1,0:T(4,128)S(1)} collective-permute-done((f32[4,1152]{1,0:T(4,128)S(1)}, f32[4,1152]{1,0:T(4,128)S(1)}, u32[]{:S(2)}, u32[]{:S(2)}) %collective-permute-start.3) | collective-permute-done | bytes 18464 | tf_op jit(solution)/shard_map/while/body/ppermute | solution.py:337
  99.1 2.3 %collective-permute-start.4 = (f32[4,1152]{1,0:T(4,128)S(1)}, f32[4,1152]{1,0:T(4,128)S(1)}, u32[]{:S(2)}, u32[]{:S(2)}) collective-permute-start(f32[4,1152]{1,0:T(4,128)S(1)} %add.61), channel_id=1, source_target_pairs={{0,512},{1,513},{2,514},{3,515},{4,516},{5,517},{6,518},{7,519},{8... | collective-permute-start | bytes 55304 | tf_op jit(solution)/shard_map/while/body/ppermute | solution.py:337
  101.5 3.3 %collective-permute-done.4 = f32[4,1152]{1,0:T(4,128)S(1)} collective-permute-done((f32[4,1152]{1,0:T(4,128)S(1)}, f32[4,1152]{1,0:T(4,128)S(1)}, u32[]{:S(2)}, u32[]{:S(2)}) %collective-permute-start.4) | collective-permute-done | bytes 18464 | tf_op jit(solution)/shard_map/while/body/ppermute | solution.py:337
  104.8 0.0 collective-permute-done.12.refs_1_
  104.8 0.0 copy-start.7
  104.8 0.1 add_convert_fusion
  104.9 5.8 %collective-permute-start.14 = (bf16[192,1152]{1,0:T(8,128)(2,1)S(1)}, bf16[192,1152]{1,0:T(8,128)(2,1)S(1)}, u32[]{:S(2)}, u32[]{:S(2)}) collective-permute-start(bf16[192,1152]{1,0:T(8,128)(2,1)S(1)} %add_convert_fusion), channel_id=1, source_target_pairs={{0,384},{1,129},{2,386},{3,131},{4,388},{5,133},{6,390},{7,135},{8... | collective-permute-start | bytes 1327112 | tf_op jit(solution)/shard_map/ppermute | solution.py:337
  110.7 0.0 collective-permute-done.13.refs_1_
  110.8 0.0 copy-start.9
  110.8 26.9 %while.32 = (s32[]{:T(128)}, f32[4,1152]{1,0:T(4,128)S(1)}, s32[]{:T(128)}, s32[]{:T(128)}) while((s32[]{:T(128)}, f32[4,1152]{1,0:T(4,128)S(1)}, s32[]{:T(128)}, s32[]{:T(128)}) %tuple.63), condition=%wide.region_5.6_spmd, body=%wide.region_4.5_spmd.sunk | while | flops 18434 | bytes 516309 | solution.py:341
  110.8 5.1 %collective-permute-start.5 = (f32[4,1152]{1,0:T(4,128)S(1)}, f32[4,1152]{1,0:T(4,128)S(1)}, u32[]{:S(2)}, u32[]{:S(2)}) collective-permute-start(f32[4,1152]{1,0:T(4,128)S(1)} %get-tuple-element.211), channel_id=1, source_target_pairs={{0,518},{1,519},{2,512},{3,513},{4,514},{5,515},{6,516},{7,517},{8... | collective-permute-start | bytes 55304 | tf_op jit(solution)/shard_map/while/body/ppermute | solution.py:337
  115.9 1.7 %collective-permute-done.5 = f32[4,1152]{1,0:T(4,128)S(1)} collective-permute-done((f32[4,1152]{1,0:T(4,128)S(1)}, f32[4,1152]{1,0:T(4,128)S(1)}, u32[]{:S(2)}, u32[]{:S(2)}) %collective-permute-start.5) | collective-permute-done | bytes 18464 | tf_op jit(solution)/shard_map/while/body/ppermute | solution.py:337
  117.7 4.4 %collective-permute-start.6 = (f32[4,1152]{1,0:T(4,128)S(1)}, f32[4,1152]{1,0:T(4,128)S(1)}, u32[]{:S(2)}, u32[]{:S(2)}) collective-permute-start(f32[4,1152]{1,0:T(4,128)S(1)} %add.64), channel_id=1, source_target_pairs={{0,514},{1,515},{2,516},{3,517},{4,518},{5,519},{6,512},{7,513},{8... | collective-permute-start | bytes 55304 | tf_op jit(solution)/shard_map/while/body/ppermute | solution.py:337
  122.0 3.1 %collective-permute-done.6 = f32[4,1152]{1,0:T(4,128)S(1)} collective-permute-done((f32[4,1152]{1,0:T(4,128)S(1)}, f32[4,1152]{1,0:T(4,128)S(1)}, u32[]{:S(2)}, u32[]{:S(2)}) %collective-permute-start.6) | collective-permute-done | bytes 18464 | tf_op jit(solution)/shard_map/while/body/ppermute | solution.py:337
  125.1 1.9 %collective-permute-start.7 = (f32[4,1152]{1,0:T(4,128)S(1)}, f32[4,1152]{1,0:T(4,128)S(1)}, u32[]{:S(2)}, u32[]{:S(2)}) collective-permute-start(f32[4,1152]{1,0:T(4,128)S(1)} %add.65), channel_id=1, source_target_pairs={{0,32},{1,33},{2,34},{3,35},{4,36},{5,37},{6,38},{7,39},{8,40},{9,... | collective-permute-start | bytes 55304 | tf_op jit(solution)/shard_map/while/body/ppermute | solution.py:337
  127.0 3.7 %collective-permute-done.7 = f32[4,1152]{1,0:T(4,128)S(1)} collective-permute-done((f32[4,1152]{1,0:T(4,128)S(1)}, f32[4,1152]{1,0:T(4,128)S(1)}, u32[]{:S(2)}, u32[]{:S(2)}) %collective-permute-start.7) | collective-permute-done | bytes 18464 | tf_op jit(solution)/shard_map/while/body/ppermute | solution.py:337
  130.8 4.5 %collective-permute-start.8 = (f32[4,1152]{1,0:T(4,128)S(1)}, f32[4,1152]{1,0:T(4,128)S(1)}, u32[]{:S(2)}, u32[]{:S(2)}) collective-permute-start(f32[4,1152]{1,0:T(4,128)S(1)} %add.66), channel_id=1, source_target_pairs={{0,480},{1,481},{2,482},{3,483},{4,484},{5,485},{6,486},{7,487},{8... | collective-permute-start | bytes 55304 | tf_op jit(solution)/shard_map/while/body/ppermute | solution.py:337
  135.2 2.4 %collective-permute-done.8 = f32[4,1152]{1,0:T(4,128)S(1)} collective-permute-done((f32[4,1152]{1,0:T(4,128)S(1)}, f32[4,1152]{1,0:T(4,128)S(1)}, u32[]{:S(2)}, u32[]{:S(2)}) %collective-permute-start.8) | collective-permute-done | bytes 18464 | tf_op jit(solution)/shard_map/while/body/ppermute | solution.py:337
  137.6 0.0 collective-permute-done.14.refs_2_
  137.6 0.0 copy-start.10
  137.6 3.6 %collective-permute-start.15 = (f32[4,1152]{1,0:T(4,128)S(1)}, f32[4,1152]{1,0:T(4,128)S(1)}, u32[]{:S(2)}, u32[]{:S(2)}) collective-permute-start(f32[4,1152]{1,0:T(4,128)S(1)} %get-tuple-element.92), channel_id=1, source_target_pairs={{0,96},{1,97},{2,98},{3,99},{4,100},{5,101},{6,102},{7,103},{8,104... | collective-permute-start | bytes 55304 | tf_op jit(solution)/shard_map/ppermute | solution.py:337
  141.2 0.0 copy-done.9
  141.2 3.2 %backward_norm.2 = (bf16[192,1152]{1,0:T(8,128)(2,1)}, f32[1,192]{1,0:T(1,128)}) custom-call(bf16[192,1152]{1,0:T(8,128)(2,1)} %bitcast.6, f32[2,1152]{1,0:T(2,128)} %gains_ref.11, f32[2,1152]{1,0:T(2,128)} %shifts_ref.11, f32[1]{0:T(128)S(6)} %exp.3.scale_ref, f32[192,1152]{1,0:T(8,128)} %copy-done.2, bf16[200,1152]{1,0:T(8,128)(2,1)} %copy-done.9, ...), custom_call_target="tpu_custom_call" | custom-call | flops 8847360 | bytes 2654208 | tf_op jit(solution)/shard_map/backward_norm/pallas_call | solution.py:249
  144.4 0.9 collective-permute-done.15
  145.3 7.3 %collective-permute-start.16 = (f32[4,1152]{1,0:T(4,128)S(1)}, f32[4,1152]{1,0:T(4,128)S(1)}, u32[]{:S(2)}, u32[]{:S(2)}) collective-permute-start(f32[4,1152]{1,0:T(4,128)S(1)} %add.43), channel_id=1, source_target_pairs={{0,352},{1,353},{2,354},{3,355},{4,356},{5,357},{6,358},{7,359},{8... | collective-permute-start | bytes 55304 | tf_op jit(solution)/shard_map/ppermute | solution.py:337
  152.6 0.0 copy-done.7
  152.7 3.5 %backward_norm.3 = bf16[192,1152]{1,0:T(8,128)(2,1)} custom-call(bf16[192,1152]{1,0:T(8,128)(2,1)} %bitcast.8, f32[2,1152]{1,0:T(2,128)} %gains_ref.11, f32[2,1152]{1,0:T(2,128)} %shifts_ref.11, f32[1]{0:T(128)S(6)} %exp.3.scale_ref, f32[192,1152]{1,0:T(8,128)} %copy-done.1, bf16[384,1152]{1,0:T(8,128)(2,1)} %copy-done.7, bf16[192,1152]{1,0:T(8,128)(2,1)} %copy-done.10), custom_call_target="tpu_custom_call" | custom-call | flops 8847360 | bytes 2654208 | tf_op jit(solution)/shard_map/backward_norm/pallas_call | solution.py:249
  156.1 0.8 collective-permute-done.16
  157.0 0.6 fusion
  (16 shorter events, 0.1 us)
Async XLA Ops:
  0.6 62.3 %copy-start.4 = (f32[2,1152]{1,0:T(2,128)S(1)}, f32[2,1152]{1,0:T(2,128)}, u32[]{:S(2)}) copy-start(f32[2,1152]{1,0:T(2,128)} %gains_ref.11) | copy-start | bytes 27652
  0.6 62.3 %copy-start.5 = (f32[2,1152]{1,0:T(2,128)S(1)}, f32[2,1152]{1,0:T(2,128)}, u32[]{:S(2)}) copy-start(f32[2,1152]{1,0:T(2,128)} %shifts_ref.11) | copy-start | bytes 27652
  3.6 59.3 %copy-start = (bf16[200,1152]{1,0:T(8,128)(2,1)S(1)}, bf16[200,1152]{1,0:T(8,128)(2,1)}, u32[]{:S(2)}) copy-start(bf16[200,1152]{1,0:T(8,128)(2,1)} %forward_norm.3.refs_1_) | copy-start | bytes 1382404
  3.6 39.7 %collective-permute-start.9 = (bf16[200,1152]{1,0:T(8,128)(2,1)}, bf16[200,1152]{1,0:T(8,128)(2,1)S(1)}, u32[]{:S(2)}, u32[]{:S(2)}) collective-permute-start(bf16[200,1152]{1,0:T(8,128)(2,1)} %forward_norm.3.refs_1_), channel_id=1, source_target_pairs={{0,384},{1,129},{2,386},{3,131},{4,388},{5,133},{6,390},{7,135},{8... | collective-permute-start | bytes 1382408 | tf_op jit(solution)/shard_map/ppermute | solution.py:337
  21.9 41.0 %collective-permute-start.11 = (bf16[200,1152]{1,0:T(8,128)(2,1)}, bf16[200,1152]{1,0:T(8,128)(2,1)S(1)}, u32[]{:S(2)}, u32[]{:S(2)}) collective-permute-start(bf16[200,1152]{1,0:T(8,128)(2,1)} %forward_norm.3.refs_1_), channel_id=1, source_target_pairs={{0,512},{1,513},{2,514},{3,515},{4,516},{5,517},{6,518},{7,519},{8... | collective-permute-start | bytes 1382408 | tf_op jit(solution)/shard_map/ppermute | solution.py:337
  28.3 34.6 %copy-start.3 = (bf16[200,1152]{1,0:T(8,128)(2,1)S(1)}, bf16[200,1152]{1,0:T(8,128)(2,1)}, u32[]{:S(2)}) copy-start(bf16[200,1152]{1,0:T(8,128)(2,1)} %forward_norm.2.refs_0_) | copy-start | bytes 1382404
  43.2 25.0 %collective-permute-start.10 = (bf16[200,1152]{1,0:T(8,128)(2,1)}, bf16[200,1152]{1,0:T(8,128)(2,1)S(1)}, u32[]{:S(2)}, u32[]{:S(2)}) collective-permute-start(bf16[200,1152]{1,0:T(8,128)(2,1)} %forward_norm.2.refs_0_), channel_id=1, source_target_pairs={{0,128},{1,385},{2,130},{3,387},{4,132},{5,389},{6,134},{7,391},{8... | collective-permute-start | bytes 1382408 | tf_op jit(solution)/shard_map/ppermute | solution.py:337
  48.8 13.2 %collective-permute-start = (bf16[200,1152]{1,0:T(8,128)(2,1)}, bf16[200,1152]{1,0:T(8,128)(2,1)S(1)}, u32[]{:S(2)}, u32[]{:S(2)}) collective-permute-start(bf16[200,1152]{1,0:T(8,128)(2,1)} %get-tuple-element.187), channel_id=1, source_target_pairs={{0,512},{1,513},{2,514},{3,515},{4,516},{5,517},{6,518},{7,519},{8... | collective-permute-start | bytes 1382408 | tf_op jit(solution)/shard_map/while/body/ppermute | solution.py:337
  62.9 5.4 %copy-start.8 = (bf16[200,1152]{1,0:T(8,128)(2,1)S(1)}, bf16[200,1152]{1,0:T(8,128)(2,1)}, u32[]{:S(2)}) copy-start(bf16[200,1152]{1,0:T(8,128)(2,1)} %get-tuple-element.81.refs_4_) | copy-start | bytes 1382404
  67.3 0.9 copy-start.2
  68.3 4.8 %copy-start.6 = (f32[1,192]{1,0:T(1,128)}, f32[1,192]{1,0:T(1,128)S(1)}, u32[]{:S(2)}) copy-start(f32[1,192]{1,0:T(1,128)S(1)} %get-tuple-element.95.refs_2_) | copy-start | bytes 2308
  73.1 0.9 copy-start.1
  74.0 30.8 %collective-permute-start.12 = (bf16[384,1152]{1,0:T(8,128)(2,1)}, bf16[384,1152]{1,0:T(8,128)(2,1)S(1)}, u32[]{:S(2)}, u32[]{:S(2)}) collective-permute-start(bf16[384,1152]{1,0:T(8,128)(2,1)} %get-tuple-element.86), channel_id=1, source_target_pairs={{0,512},{1,513},{2,514},{3,515},{4,516},{5,517},{6,518},{7,519},{8... | collective-permute-start | bytes 2654216 | tf_op jit(solution)/shard_map/ppermute | solution.py:337
  77.5 33.3 %collective-permute-start.13 = (bf16[200,1152]{1,0:T(8,128)(2,1)S(1)}, bf16[200,1152]{1,0:T(8,128)(2,1)S(1)}, u32[]{:S(2)}, u32[]{:S(2)}) collective-permute-start(bf16[200,1152]{1,0:T(8,128)(2,1)S(1)} %get-tuple-element.89), channel_id=1, source_target_pairs={{0,128},{1,385},{2,130},{3,387},{4,132},{5,389},{6,134},{7,391},{8... | collective-permute-start | bytes 1382408 | tf_op jit(solution)/shard_map/ppermute | solution.py:337
  83.5 3.1 %collective-permute-start.1 = (f32[4,1152]{1,0:T(4,128)S(1)}, f32[4,1152]{1,0:T(4,128)S(1)}, u32[]{:S(2)}, u32[]{:S(2)}) collective-permute-start(f32[4,1152]{1,0:T(4,128)S(1)} %get-tuple-element.199), channel_id=1, source_target_pairs={{0,1},{1,0},{2,3},{3,2},{4,5},{5,4},{6,7},{7,6},{8,9},{9,8},{10,11... | collective-permute-start | bytes 55304 | tf_op jit(solution)/shard_map/while/body/ppermute | solution.py:337
  86.6 5.6 %collective-permute-start.2 = (f32[4,1152]{1,0:T(4,128)S(1)}, f32[4,1152]{1,0:T(4,128)S(1)}, u32[]{:S(2)}, u32[]{:S(2)}) collective-permute-start(f32[4,1152]{1,0:T(4,128)S(1)} %add.59), channel_id=1, source_target_pairs={{0,8},{1,9},{2,10},{3,11},{4,12},{5,13},{6,14},{7,15},{8,0},{9,1},... | collective-permute-start | bytes 55304 | tf_op jit(solution)/shard_map/while/body/ppermute | solution.py:337
  92.3 6.9 %collective-permute-start.3 = (f32[4,1152]{1,0:T(4,128)S(1)}, f32[4,1152]{1,0:T(4,128)S(1)}, u32[]{:S(2)}, u32[]{:S(2)}) collective-permute-start(f32[4,1152]{1,0:T(4,128)S(1)} %add.60), channel_id=1, source_target_pairs={{0,24},{1,25},{2,26},{3,27},{4,28},{5,29},{6,30},{7,31},{8,16},{9,... | collective-permute-start | bytes 55304 | tf_op jit(solution)/shard_map/while/body/ppermute | solution.py:337
  99.1 5.6 %collective-permute-start.4 = (f32[4,1152]{1,0:T(4,128)S(1)}, f32[4,1152]{1,0:T(4,128)S(1)}, u32[]{:S(2)}, u32[]{:S(2)}) collective-permute-start(f32[4,1152]{1,0:T(4,128)S(1)} %add.61), channel_id=1, source_target_pairs={{0,512},{1,513},{2,514},{3,515},{4,516},{5,517},{6,518},{7,519},{8... | collective-permute-start | bytes 55304 | tf_op jit(solution)/shard_map/while/body/ppermute | solution.py:337
  104.8 47.8 %copy-start.7 = (bf16[384,1152]{1,0:T(8,128)(2,1)}, bf16[384,1152]{1,0:T(8,128)(2,1)S(1)}, u32[]{:S(2)}) copy-start(bf16[384,1152]{1,0:T(8,128)(2,1)S(1)} %collective-permute-done.12.refs_1_) | copy-start | bytes 2654212
  104.9 32.7 %collective-permute-start.14 = (bf16[192,1152]{1,0:T(8,128)(2,1)S(1)}, bf16[192,1152]{1,0:T(8,128)(2,1)S(1)}, u32[]{:S(2)}, u32[]{:S(2)}) collective-permute-start(bf16[192,1152]{1,0:T(8,128)(2,1)S(1)} %add_convert_fusion), channel_id=1, source_target_pairs={{0,384},{1,129},{2,386},{3,131},{4,388},{5,133},{6,390},{7,135},{8... | collective-permute-start | bytes 1327112 | tf_op jit(solution)/shard_map/ppermute | solution.py:337
  110.8 30.5 %copy-start.9 = (bf16[200,1152]{1,0:T(8,128)(2,1)}, bf16[200,1152]{1,0:T(8,128)(2,1)S(1)}, u32[]{:S(2)}) copy-start(bf16[200,1152]{1,0:T(8,128)(2,1)S(1)} %collective-permute-done.13.refs_1_) | copy-start | bytes 1382404
  110.8 6.9 %collective-permute-start.5 = (f32[4,1152]{1,0:T(4,128)S(1)}, f32[4,1152]{1,0:T(4,128)S(1)}, u32[]{:S(2)}, u32[]{:S(2)}) collective-permute-start(f32[4,1152]{1,0:T(4,128)S(1)} %get-tuple-element.211), channel_id=1, source_target_pairs={{0,518},{1,519},{2,512},{3,513},{4,514},{5,515},{6,516},{7,517},{8... | collective-permute-start | bytes 55304 | tf_op jit(solution)/shard_map/while/body/ppermute | solution.py:337
  117.7 7.4 %collective-permute-start.6 = (f32[4,1152]{1,0:T(4,128)S(1)}, f32[4,1152]{1,0:T(4,128)S(1)}, u32[]{:S(2)}, u32[]{:S(2)}) collective-permute-start(f32[4,1152]{1,0:T(4,128)S(1)} %add.64), channel_id=1, source_target_pairs={{0,514},{1,515},{2,516},{3,517},{4,518},{5,519},{6,512},{7,513},{8... | collective-permute-start | bytes 55304 | tf_op jit(solution)/shard_map/while/body/ppermute | solution.py:337
  125.1 5.6 %collective-permute-start.7 = (f32[4,1152]{1,0:T(4,128)S(1)}, f32[4,1152]{1,0:T(4,128)S(1)}, u32[]{:S(2)}, u32[]{:S(2)}) collective-permute-start(f32[4,1152]{1,0:T(4,128)S(1)} %add.65), channel_id=1, source_target_pairs={{0,32},{1,33},{2,34},{3,35},{4,36},{5,37},{6,38},{7,39},{8,40},{9,... | collective-permute-start | bytes 55304 | tf_op jit(solution)/shard_map/while/body/ppermute | solution.py:337
  130.8 6.9 %collective-permute-start.8 = (f32[4,1152]{1,0:T(4,128)S(1)}, f32[4,1152]{1,0:T(4,128)S(1)}, u32[]{:S(2)}, u32[]{:S(2)}) collective-permute-start(f32[4,1152]{1,0:T(4,128)S(1)} %add.66), channel_id=1, source_target_pairs={{0,480},{1,481},{2,482},{3,483},{4,484},{5,485},{6,486},{7,487},{8... | collective-permute-start | bytes 55304 | tf_op jit(solution)/shard_map/while/body/ppermute | solution.py:337
  137.6 15.0 %copy-start.10 = (bf16[192,1152]{1,0:T(8,128)(2,1)}, bf16[192,1152]{1,0:T(8,128)(2,1)S(1)}, u32[]{:S(2)}) copy-start(bf16[192,1152]{1,0:T(8,128)(2,1)S(1)} %collective-permute-done.14.refs_2_) | copy-start | bytes 1327108
  137.6 7.7 %collective-permute-start.15 = (f32[4,1152]{1,0:T(4,128)S(1)}, f32[4,1152]{1,0:T(4,128)S(1)}, u32[]{:S(2)}, u32[]{:S(2)}) collective-permute-start(f32[4,1152]{1,0:T(4,128)S(1)} %get-tuple-element.92), channel_id=1, source_target_pairs={{0,96},{1,97},{2,98},{3,99},{4,100},{5,101},{6,102},{7,103},{8,104... | collective-permute-start | bytes 55304 | tf_op jit(solution)/shard_map/ppermute | solution.py:337
  145.3 11.7 %collective-permute-start.16 = (f32[4,1152]{1,0:T(4,128)S(1)}, f32[4,1152]{1,0:T(4,128)S(1)}, u32[]{:S(2)}, u32[]{:S(2)}) collective-permute-start(f32[4,1152]{1,0:T(4,128)S(1)} %add.43), channel_id=1, source_target_pairs={{0,352},{1,353},{2,354},{3,355},{4,356},{5,357},{6,358},{7,359},{8... | collective-permute-start | bytes 55304 | tf_op jit(solution)/shard_map/ppermute | solution.py:337

commit v8 on v7

--- a/solution.py
+++ b/solution.py
@@ -181,10 +181,10 @@
         return jax.ShapeDtypeStruct((count, width), kind)
 
     if final:
-        outs = [wide(rows, jnp.float32)] * 2
+        outs = [pltpu.HBM((rows, width), jnp.float32)] * 2
         outs += [wide(2 * rows, jnp.bfloat16), wide(rows + EXTRA, jnp.bfloat16)]
     else:
-        outs = [wide(4 * rows, jnp.float32), wide(rows, jnp.float32)]
+        outs = [wide(4 * rows, jnp.float32), pltpu.HBM((rows, width), jnp.float32)]
         outs += [jax.ShapeDtypeStruct((1, rows), jnp.float32)]
     outs += [wide(4, jnp.float32)]
     return pl.pallas_call(

time: 158 us -> 159 us (level)
  starting transfers between devices: 80.1 us -> 84.9 us
  waiting for transfers between devices: 49.2 us -> 45.2 us
  local copies, waits for them, and re-layouts: 4.08 us -> 1.28 us
    ppermute x17, starting transfers between devices: 80.1 us -> 84.9 us  [send(): return lax.ppermute(value, AXES, pairs)]
    ppermute x17, waiting for transfers between devices: 49.2 us -> 45.2 us  [send(): return lax.ppermute(value, AXES, pairs)]
    unnamed x23 -> x19, local copies, waits for them, and re-layouts: 2.67 us -> 0.63 us
  transfers between devices with their start and end apart: 17 -> 17, of which waited for: 12 -> 11; matrix products, arithmetic and copies ran while one was open for 1% -> 1% of each run, Pallas kernels for 9% -> 9%
where the time goes in v8:
time: 159 us; the launch traced here: 158 us
  starting transfers between devices  84.9 us (53%)
  waiting for transfers between devices  45.2 us (28%)
  Pallas kernels  22.3 us (14%)
  between operations  2.19 us (1%)
  other arithmetic  1.7 us (1%)
    ppermute x17, starting transfers between devices, send(): return lax.ppermute(value, AXES, pairs)  84.9 us
    ppermute x17, waiting for transfers between devices, send(): return lax.ppermute(value, AXES, pairs)  45.2 us
    pallas_call x2, Pallas kernels, tile(): pl.pallas_call(functools.partial(tile_kernel, final), out_shape=tuple(out...  9.84 us
    pallas_call x2, Pallas kernels, backward_norm(): pl.pallas_call(functools.partial(backward_kernel, tower, firsts), out_sha...  6.65 us
    pallas_call x2, Pallas kernels, forward_norm(): pl.pallas_call(functools.partial(forward_kernel, tower), out_shape=jax.Sh...  5.83 us
  transfers between devices with their start and end apart: 17, of which 11 were waited for; matrix products, arithmetic and copies ran while one was open for 1% of the time, Pallas kernels for 9%

profile of v8, /device:TPU:6, one launch (start us, length us, event | category | flops | bytes accessed | tf_op | source)
XLA Modules:
  0.0 157.7 jit_solution(14114540941088162697)
XLA Ops:
  0.6 0.0 copy-start.2
  0.6 0.0 copy-start.3
  0.7 2.9 %forward_norm.3.refs_1_ = bf16[200,1152]{1,0:T(8,128)(2,1)} custom-call(bf16[192,1152]{1,0:T(8,128)(2,1)} %bitcast.7, f32[2,1152]{1,0:T(2,128)} %gains_ref.11, f32[2,1152]{1,0:T(2,128)} %shifts_ref.11), custom_call_target="tpu_custom_call" | custom-call | flops 4423680 | bytes 884736 | tf_op jit(solution)/shard_map/forward_norm/pallas_call | solution.py:88
  3.6 0.0 copy-start
  3.6 18.3 %collective-permute-start.9 = (bf16[200,1152]{1,0:T(8,128)(2,1)}, bf16[200,1152]{1,0:T(8,128)(2,1)S(1)}, u32[]{:S(2)}, u32[]{:S(2)}) collective-permute-start(bf16[200,1152]{1,0:T(8,128)(2,1)} %forward_norm.3.refs_1_), channel_id=1, source_target_pairs={{0,384},{1,129},{2,386},{3,131},{4,388},{5,133},{6,390},{7,135},{8... | collective-permute-start | bytes 1382408 | tf_op jit(solution)/shard_map/ppermute | solution.py:337
  21.9 3.5 %collective-permute-start.11 = (bf16[200,1152]{1,0:T(8,128)(2,1)}, bf16[200,1152]{1,0:T(8,128)(2,1)S(1)}, u32[]{:S(2)}, u32[]{:S(2)}) collective-permute-start(bf16[200,1152]{1,0:T(8,128)(2,1)} %forward_norm.3.refs_1_), channel_id=1, source_target_pairs={{0,512},{1,513},{2,514},{3,515},{4,516},{5,517},{6,518},{7,519},{8... | collective-permute-start | bytes 1382408 | tf_op jit(solution)/shard_map/ppermute | solution.py:337
  25.4 2.9 %forward_norm.2.refs_0_ = bf16[200,1152]{1,0:T(8,128)(2,1)} custom-call(bf16[192,1152]{1,0:T(8,128)(2,1)} %bitcast.5, f32[2,1152]{1,0:T(2,128)} %gains_ref.11, f32[2,1152]{1,0:T(2,128)} %shifts_ref.11), custom_call_target="tpu_custom_call" | custom-call | flops 4423680 | bytes 884736 | tf_op jit(solution)/shard_map/forward_norm/pallas_call | solution.py:88
  28.3 0.0 copy-start.1
  28.3 14.9 %collective-permute-done.9.refs_2_ = bf16[200,1152]{1,0:T(8,128)(2,1)S(1)} collective-permute-done((bf16[200,1152]{1,0:T(8,128)(2,1)}, bf16[200,1152]{1,0:T(8,128)(2,1)S(1)}, u32[]{:S(2)}, u32[]{:S(2)}) %collective-permute-start.9) | collective-permute-done | bytes 460832 | tf_op jit(solution)/shard_map/ppermute | solution.py:337
  43.2 3.4 %collective-permute-start.10 = (bf16[200,1152]{1,0:T(8,128)(2,1)}, bf16[200,1152]{1,0:T(8,128)(2,1)S(1)}, u32[]{:S(2)}, u32[]{:S(2)}) collective-permute-start(bf16[200,1152]{1,0:T(8,128)(2,1)} %forward_norm.2.refs_0_), channel_id=1, source_target_pairs={{0,128},{1,385},{2,130},{3,387},{4,132},{5,389},{6,134},{7,391},{8... | collective-permute-start | bytes 1382408 | tf_op jit(solution)/shard_map/ppermute | solution.py:337
  47.9 0.1 pad_maximum_fusion.scalars_ref
  48.1 13.1 %while.30 = (s32[]{:T(128)}, bf16[200,1152]{1,0:T(8,128)(2,1)S(1)}, s32[]{:T(128)}, s32[]{:T(128)}) while((s32[]{:T(128)}, bf16[200,1152]{1,0:T(8,128)(2,1)S(1)}, s32[]{:T(128)}, s32[]{:T(128)}) %tuple.57), condition=%wide.region_1.2_spmd, body=%wide.region_0.1_spmd.sunk | while | flops 2 | bytes 2764893 | solution.py:341
  48.1 3.5 %collective-permute-start = (bf16[200,1152]{1,0:T(8,128)(2,1)S(1)}, bf16[200,1152]{1,0:T(8,128)(2,1)S(1)}, u32[]{:S(2)}, u32[]{:S(2)}) collective-permute-start(bf16[200,1152]{1,0:T(8,128)(2,1)S(1)} %get-tuple-element.187), channel_id=1, source_target_pairs={{0,512},{1,513},{2,514},{3,515},{4,516},{5,517},{6,518},{7,519},{8... | collective-permute-start | bytes 1382408 | tf_op jit(solution)/shard_map/while/body/ppermute | solution.py:337
  51.6 9.6 %collective-permute-done = bf16[200,1152]{1,0:T(8,128)(2,1)S(1)} collective-permute-done((bf16[200,1152]{1,0:T(8,128)(2,1)S(1)}, bf16[200,1152]{1,0:T(8,128)(2,1)S(1)}, u32[]{:S(2)}, u32[]{:S(2)}) %collective-permute-start) | collective-permute-done | bytes 460832 | tf_op jit(solution)/shard_map/while/body/ppermute | solution.py:337
  61.2 0.0 copy-start.6
  61.2 0.0 collective-permute-done.11.refs_3_
  61.2 0.0 copy-done.2
  61.2 0.0 copy-done.3
  61.2 0.0 copy-done
  61.2 0.0 copy-done.1
  61.2 4.6 %first_tile.1 = (f32[768,1152]{1,0:T(8,128)S(1)}, f32[192,1152]{1,0:T(8,128)}, f32[1,192]{1,0:T(1,128)S(1)}, f32[4,1152]{1,0:T(4,128)S(1)}) custom-call(f32[2]{0:T(128)S(1)} %pad_maximum_fusion.scalars_ref, f32[2,1152]{1,0:T(2,128)S(1)} %copy-done.2, f32[2,1152]{1,0:T(2,128)S(1)} %copy-done.3, bf16[200,1152]{1,0:T(8,128)(2,1)S(1)} %copy-done.1, ...), custom_call_target="tpu_custom_call" | custom-call | flops 1019215872 | bytes 5308416 | tf_op jit(solution)/shard_map/first_tile/pallas_call | solution.py:190
  65.8 0.0 copy-start.4
  65.8 0.6 copy-done.4
  66.4 0.0 collective-permute-done.10.refs_0_
  66.4 0.0 copy-done.6
  66.4 5.2 %last_tile.1 = (f32[192,1152]{1,0:T(8,128)}, f32[192,1152]{1,0:T(8,128)}, bf16[384,1152]{1,0:T(8,128)(2,1)S(1)}, bf16[200,1152]{1,0:T(8,128)(2,1)S(1)}, f32[4,1152]{1,0:T(4,128)S(1)}) custom-call(f32[2]{0:T(128)S(1)} %pad_maximum_fusion.scalars_ref, f32[2,1152]{1,0:T(2,128)S(1)} %copy-done.2, f32[2,1152]{1,0:T(2,128)S(1)} %copy-done.3, ...), custom_call_target="tpu_custom_call" | custom-call | flops 1019215872 | bytes 5308416 | tf_op jit(solution)/shard_map/last_tile/pallas_call | solution.py:190
  71.6 3.5 %collective-permute-start.12 = (bf16[384,1152]{1,0:T(8,128)(2,1)S(1)}, bf16[384,1152]{1,0:T(8,128)(2,1)S(1)}, u32[]{:S(2)}, u32[]{:S(2)}) collective-permute-start(bf16[384,1152]{1,0:T(8,128)(2,1)S(1)} %get-tuple-element.86), channel_id=1, source_target_pairs={{0,512},{1,513},{2,514},{3,515},{4,516},{5,517},{6,518},{7,519},{8... | collective-permute-start | bytes 2654216 | tf_op jit(solution)/shard_map/ppermute | solution.py:337
  75.1 6.1 %collective-permute-start.13 = (bf16[200,1152]{1,0:T(8,128)(2,1)S(1)}, bf16[200,1152]{1,0:T(8,128)(2,1)S(1)}, u32[]{:S(2)}, u32[]{:S(2)}) collective-permute-start(bf16[200,1152]{1,0:T(8,128)(2,1)S(1)} %get-tuple-element.89), channel_id=1, source_target_pairs={{0,128},{1,385},{2,130},{3,387},{4,132},{5,389},{6,134},{7,391},{8... | collective-permute-start | bytes 1382408 | tf_op jit(solution)/shard_map/ppermute | solution.py:337
  81.2 21.3 %while.31 = (s32[]{:T(128)}, f32[4,1152]{1,0:T(4,128)S(1)}, s32[]{:T(128)}, s32[]{:T(128)}) while((s32[]{:T(128)}, f32[4,1152]{1,0:T(4,128)S(1)}, s32[]{:T(128)}, s32[]{:T(128)}) %tuple.60), condition=%wide.region_3.4_spmd, body=%wide.region_2.3_spmd.sunk | while | flops 18434 | bytes 516309 | solution.py:341
  81.2 1.9 %collective-permute-start.1 = (f32[4,1152]{1,0:T(4,128)S(1)}, f32[4,1152]{1,0:T(4,128)S(1)}, u32[]{:S(2)}, u32[]{:S(2)}) collective-permute-start(f32[4,1152]{1,0:T(4,128)S(1)} %get-tuple-element.199), channel_id=1, source_target_pairs={{0,1},{1,0},{2,3},{3,2},{4,5},{5,4},{6,7},{7,6},{8,9},{9,8},{10,11... | collective-permute-start | bytes 55304 | tf_op jit(solution)/shard_map/while/body/ppermute | solution.py:337
  83.1 1.2 collective-permute-done.1
  84.3 2.7 %collective-permute-start.2 = (f32[4,1152]{1,0:T(4,128)S(1)}, f32[4,1152]{1,0:T(4,128)S(1)}, u32[]{:S(2)}, u32[]{:S(2)}) collective-permute-start(f32[4,1152]{1,0:T(4,128)S(1)} %add.59), channel_id=1, source_target_pairs={{0,8},{1,9},{2,10},{3,11},{4,12},{5,13},{6,14},{7,15},{8,0},{9,1},... | collective-permute-start | bytes 55304 | tf_op jit(solution)/shard_map/while/body/ppermute | solution.py:337
  87.0 2.9 %collective-permute-done.2 = f32[4,1152]{1,0:T(4,128)S(1)} collective-permute-done((f32[4,1152]{1,0:T(4,128)S(1)}, f32[4,1152]{1,0:T(4,128)S(1)}, u32[]{:S(2)}, u32[]{:S(2)}) %collective-permute-start.2) | collective-permute-done | bytes 18464 | tf_op jit(solution)/shard_map/while/body/ppermute | solution.py:337
  89.9 2.4 %collective-permute-start.3 = (f32[4,1152]{1,0:T(4,128)S(1)}, f32[4,1152]{1,0:T(4,128)S(1)}, u32[]{:S(2)}, u32[]{:S(2)}) collective-permute-start(f32[4,1152]{1,0:T(4,128)S(1)} %add.60), channel_id=1, source_target_pairs={{0,24},{1,25},{2,26},{3,27},{4,28},{5,29},{6,30},{7,31},{8,16},{9,... | collective-permute-start | bytes 55304 | tf_op jit(solution)/shard_map/while/body/ppermute | solution.py:337
  92.3 4.5 %collective-permute-done.3 = f32[4,1152]{1,0:T(4,128)S(1)} collective-permute-done((f32[4,1152]{1,0:T(4,128)S(1)}, f32[4,1152]{1,0:T(4,128)S(1)}, u32[]{:S(2)}, u32[]{:S(2)}) %collective-permute-start.3) | collective-permute-done | bytes 18464 | tf_op jit(solution)/shard_map/while/body/ppermute | solution.py:337
  96.8 2.3 %collective-permute-start.4 = (f32[4,1152]{1,0:T(4,128)S(1)}, f32[4,1152]{1,0:T(4,128)S(1)}, u32[]{:S(2)}, u32[]{:S(2)}) collective-permute-start(f32[4,1152]{1,0:T(4,128)S(1)} %add.61), channel_id=1, source_target_pairs={{0,512},{1,513},{2,514},{3,515},{4,516},{5,517},{6,518},{7,519},{8... | collective-permute-start | bytes 55304 | tf_op jit(solution)/shard_map/while/body/ppermute | solution.py:337
  99.2 3.3 %collective-permute-done.4 = f32[4,1152]{1,0:T(4,128)S(1)} collective-permute-done((f32[4,1152]{1,0:T(4,128)S(1)}, f32[4,1152]{1,0:T(4,128)S(1)}, u32[]{:S(2)}, u32[]{:S(2)}) %collective-permute-start.4) | collective-permute-done | bytes 18464 | tf_op jit(solution)/shard_map/while/body/ppermute | solution.py:337
  102.5 0.0 collective-permute-done.12.refs_1_
  102.5 0.0 copy-start.5
  102.5 1.6 add_convert_fusion
  104.0 5.8 %collective-permute-start.14 = (bf16[192,1152]{1,0:T(8,128)(2,1)S(1)}, bf16[192,1152]{1,0:T(8,128)(2,1)S(1)}, u32[]{:S(2)}, u32[]{:S(2)}) collective-permute-start(bf16[192,1152]{1,0:T(8,128)(2,1)S(1)} %add_convert_fusion), channel_id=1, source_target_pairs={{0,384},{1,129},{2,386},{3,131},{4,388},{5,133},{6,390},{7,135},{8... | collective-permute-start | bytes 1327112 | tf_op jit(solution)/shard_map/ppermute | solution.py:337
  109.9 0.0 collective-permute-done.13.refs_1_
  109.9 0.0 copy-start.7
  109.9 28.1 %while.32 = (s32[]{:T(128)}, f32[4,1152]{1,0:T(4,128)S(1)}, s32[]{:T(128)}, s32[]{:T(128)}) while((s32[]{:T(128)}, f32[4,1152]{1,0:T(4,128)S(1)}, s32[]{:T(128)}, s32[]{:T(128)}) %tuple.63), condition=%wide.region_5.6_spmd, body=%wide.region_4.5_spmd.sunk | while | flops 18434 | bytes 516309 | solution.py:341
  109.9 5.2 %collective-permute-start.5 = (f32[4,1152]{1,0:T(4,128)S(1)}, f32[4,1152]{1,0:T(4,128)S(1)}, u32[]{:S(2)}, u32[]{:S(2)}) collective-permute-start(f32[4,1152]{1,0:T(4,128)S(1)} %get-tuple-element.211), channel_id=1, source_target_pairs={{0,518},{1,519},{2,512},{3,513},{4,514},{5,515},{6,516},{7,517},{8... | collective-permute-start | bytes 55304 | tf_op jit(solution)/shard_map/while/body/ppermute | solution.py:337
  115.1 1.7 %collective-permute-done.5 = f32[4,1152]{1,0:T(4,128)S(1)} collective-permute-done((f32[4,1152]{1,0:T(4,128)S(1)}, f32[4,1152]{1,0:T(4,128)S(1)}, u32[]{:S(2)}, u32[]{:S(2)}) %collective-permute-start.5) | collective-permute-done | bytes 18464 | tf_op jit(solution)/shard_map/while/body/ppermute | solution.py:337
  116.8 4.4 %collective-permute-start.6 = (f32[4,1152]{1,0:T(4,128)S(1)}, f32[4,1152]{1,0:T(4,128)S(1)}, u32[]{:S(2)}, u32[]{:S(2)}) collective-permute-start(f32[4,1152]{1,0:T(4,128)S(1)} %add.64), channel_id=1, source_target_pairs={{0,514},{1,515},{2,516},{3,517},{4,518},{5,519},{6,512},{7,513},{8... | collective-permute-start | bytes 55304 | tf_op jit(solution)/shard_map/while/body/ppermute | solution.py:337
  121.2 3.1 %collective-permute-done.6 = f32[4,1152]{1,0:T(4,128)S(1)} collective-permute-done((f32[4,1152]{1,0:T(4,128)S(1)}, f32[4,1152]{1,0:T(4,128)S(1)}, u32[]{:S(2)}, u32[]{:S(2)}) %collective-permute-start.6) | collective-permute-done | bytes 18464 | tf_op jit(solution)/shard_map/while/body/ppermute | solution.py:337
  124.2 3.5 %collective-permute-start.7 = (f32[4,1152]{1,0:T(4,128)S(1)}, f32[4,1152]{1,0:T(4,128)S(1)}, u32[]{:S(2)}, u32[]{:S(2)}) collective-permute-start(f32[4,1152]{1,0:T(4,128)S(1)} %add.65), channel_id=1, source_target_pairs={{0,32},{1,33},{2,34},{3,35},{4,36},{5,37},{6,38},{7,39},{8,40},{9,... | collective-permute-start | bytes 55304 | tf_op jit(solution)/shard_map/while/body/ppermute | solution.py:337
  127.7 2.2 %collective-permute-done.7 = f32[4,1152]{1,0:T(4,128)S(1)} collective-permute-done((f32[4,1152]{1,0:T(4,128)S(1)}, f32[4,1152]{1,0:T(4,128)S(1)}, u32[]{:S(2)}, u32[]{:S(2)}) %collective-permute-start.7) | collective-permute-done | bytes 18464 | tf_op jit(solution)/shard_map/while/body/ppermute | solution.py:337
  129.9 6.3 %collective-permute-start.8 = (f32[4,1152]{1,0:T(4,128)S(1)}, f32[4,1152]{1,0:T(4,128)S(1)}, u32[]{:S(2)}, u32[]{:S(2)}) collective-permute-start(f32[4,1152]{1,0:T(4,128)S(1)} %add.66), channel_id=1, source_target_pairs={{0,480},{1,481},{2,482},{3,483},{4,484},{5,485},{6,486},{7,487},{8... | collective-permute-start | bytes 55304 | tf_op jit(solution)/shard_map/while/body/ppermute | solution.py:337
  136.2 1.7 %collective-permute-done.8 = f32[4,1152]{1,0:T(4,128)S(1)} collective-permute-done((f32[4,1152]{1,0:T(4,128)S(1)}, f32[4,1152]{1,0:T(4,128)S(1)}, u32[]{:S(2)}, u32[]{:S(2)}) %collective-permute-start.8) | collective-permute-done | bytes 18464 | tf_op jit(solution)/shard_map/while/body/ppermute | solution.py:337
  138.0 0.0 collective-permute-done.14.refs_2_
  138.0 0.0 copy-start.8
  138.0 4.1 %collective-permute-start.15 = (f32[4,1152]{1,0:T(4,128)S(1)}, f32[4,1152]{1,0:T(4,128)S(1)}, u32[]{:S(2)}, u32[]{:S(2)}) collective-permute-start(f32[4,1152]{1,0:T(4,128)S(1)} %get-tuple-element.92), channel_id=1, source_target_pairs={{0,96},{1,97},{2,98},{3,99},{4,100},{5,101},{6,102},{7,103},{8,104... | collective-permute-start | bytes 55304 | tf_op jit(solution)/shard_map/ppermute | solution.py:337
  142.1 0.0 copy-done.7
  142.1 3.2 %backward_norm.2 = (bf16[192,1152]{1,0:T(8,128)(2,1)}, f32[1,192]{1,0:T(1,128)}) custom-call(bf16[192,1152]{1,0:T(8,128)(2,1)} %bitcast.6, f32[2,1152]{1,0:T(2,128)} %gains_ref.11, f32[2,1152]{1,0:T(2,128)} %shifts_ref.11, f32[1]{0:T(128)S(6)} %exp.3.scale_ref, f32[192,1152]{1,0:T(8,128)} %get-tuple-element.93.refs_0_, bf16[200,1152]{1,0:T(8,128)(2,1)} %copy-done.7, ...), custom_call_target="tpu_custom_call" | custom-call | flops 8847360 | bytes 2654208 | tf_op jit(solution)/shard_map/backward_norm/pallas_call | solution.py:249
  145.3 0.2 collective-permute-done.15
  145.5 8.1 %collective-permute-start.16 = (f32[4,1152]{1,0:T(4,128)S(1)}, f32[4,1152]{1,0:T(4,128)S(1)}, u32[]{:S(2)}, u32[]{:S(2)}) collective-permute-start(f32[4,1152]{1,0:T(4,128)S(1)} %add.43), channel_id=1, source_target_pairs={{0,352},{1,353},{2,354},{3,355},{4,356},{5,357},{6,358},{7,359},{8... | collective-permute-start | bytes 55304 | tf_op jit(solution)/shard_map/ppermute | solution.py:337
  153.6 0.0 copy-done.5
  153.6 0.0 copy-done.8
  153.6 3.5 %backward_norm.3 = bf16[192,1152]{1,0:T(8,128)(2,1)} custom-call(bf16[192,1152]{1,0:T(8,128)(2,1)} %bitcast.8, f32[2,1152]{1,0:T(2,128)} %gains_ref.11, f32[2,1152]{1,0:T(2,128)} %shifts_ref.11, f32[1]{0:T(128)S(6)} %exp.3.scale_ref, f32[192,1152]{1,0:T(8,128)} %get-tuple-element.98.refs_0_, bf16[384,1152]{1,0:T(8,128)(2,1)} %copy-done.5, ...), custom_call_target="tpu_custom_call" | custom-call | flops 8847360 | bytes 2654208 | tf_op jit(solution)/shard_map/backward_norm/pallas_call | solution.py:249
  157.1 0.0 collective-permute-done.16
  157.1 0.6 fusion
  (12 shorter events, 0.1 us)
Async XLA Ops:
  0.6 60.6 %copy-start.2 = (f32[2,1152]{1,0:T(2,128)S(1)}, f32[2,1152]{1,0:T(2,128)}, u32[]{:S(2)}) copy-start(f32[2,1152]{1,0:T(2,128)} %gains_ref.11) | copy-start | bytes 27652
  0.6 60.6 %copy-start.3 = (f32[2,1152]{1,0:T(2,128)S(1)}, f32[2,1152]{1,0:T(2,128)}, u32[]{:S(2)}) copy-start(f32[2,1152]{1,0:T(2,128)} %shifts_ref.11) | copy-start | bytes 27652
  3.6 57.7 %copy-start = (bf16[200,1152]{1,0:T(8,128)(2,1)S(1)}, bf16[200,1152]{1,0:T(8,128)(2,1)}, u32[]{:S(2)}) copy-start(bf16[200,1152]{1,0:T(8,128)(2,1)} %forward_norm.3.refs_1_) | copy-start | bytes 1382404
  3.6 39.7 %collective-permute-start.9 = (bf16[200,1152]{1,0:T(8,128)(2,1)}, bf16[200,1152]{1,0:T(8,128)(2,1)S(1)}, u32[]{:S(2)}, u32[]{:S(2)}) collective-permute-start(bf16[200,1152]{1,0:T(8,128)(2,1)} %forward_norm.3.refs_1_), channel_id=1, source_target_pairs={{0,384},{1,129},{2,386},{3,131},{4,388},{5,133},{6,390},{7,135},{8... | collective-permute-start | bytes 1382408 | tf_op jit(solution)/shard_map/ppermute | solution.py:337
  21.9 39.3 %collective-permute-start.11 = (bf16[200,1152]{1,0:T(8,128)(2,1)}, bf16[200,1152]{1,0:T(8,128)(2,1)S(1)}, u32[]{:S(2)}, u32[]{:S(2)}) collective-permute-start(bf16[200,1152]{1,0:T(8,128)(2,1)} %forward_norm.3.refs_1_), channel_id=1, source_target_pairs={{0,512},{1,513},{2,514},{3,515},{4,516},{5,517},{6,518},{7,519},{8... | collective-permute-start | bytes 1382408 | tf_op jit(solution)/shard_map/ppermute | solution.py:337
  28.3 32.9 %copy-start.1 = (bf16[200,1152]{1,0:T(8,128)(2,1)S(1)}, bf16[200,1152]{1,0:T(8,128)(2,1)}, u32[]{:S(2)}) copy-start(bf16[200,1152]{1,0:T(8,128)(2,1)} %forward_norm.2.refs_0_) | copy-start | bytes 1382404
  43.2 23.2 %collective-permute-start.10 = (bf16[200,1152]{1,0:T(8,128)(2,1)}, bf16[200,1152]{1,0:T(8,128)(2,1)S(1)}, u32[]{:S(2)}, u32[]{:S(2)}) collective-permute-start(bf16[200,1152]{1,0:T(8,128)(2,1)} %forward_norm.2.refs_0_), channel_id=1, source_target_pairs={{0,128},{1,385},{2,130},{3,387},{4,132},{5,389},{6,134},{7,391},{8... | collective-permute-start | bytes 1382408 | tf_op jit(solution)/shard_map/ppermute | solution.py:337
  48.1 13.1 %collective-permute-start = (bf16[200,1152]{1,0:T(8,128)(2,1)S(1)}, bf16[200,1152]{1,0:T(8,128)(2,1)S(1)}, u32[]{:S(2)}, u32[]{:S(2)}) collective-permute-start(bf16[200,1152]{1,0:T(8,128)(2,1)S(1)} %get-tuple-element.187), channel_id=1, source_target_pairs={{0,512},{1,513},{2,514},{3,515},{4,516},{5,517},{6,518},{7,519},{8... | collective-permute-start | bytes 1382408 | tf_op jit(solution)/shard_map/while/body/ppermute | solution.py:337
  61.2 5.2 %copy-start.6 = (bf16[200,1152]{1,0:T(8,128)(2,1)}, bf16[200,1152]{1,0:T(8,128)(2,1)S(1)}, u32[]{:S(2)}) copy-start(bf16[200,1152]{1,0:T(8,128)(2,1)S(1)} %get-tuple-element.81.refs_4_) | copy-start | bytes 1382404
  65.8 0.6 copy-start.4
  71.6 30.8 %collective-permute-start.12 = (bf16[384,1152]{1,0:T(8,128)(2,1)S(1)}, bf16[384,1152]{1,0:T(8,128)(2,1)S(1)}, u32[]{:S(2)}, u32[]{:S(2)}) collective-permute-start(bf16[384,1152]{1,0:T(8,128)(2,1)S(1)} %get-tuple-element.86), channel_id=1, source_target_pairs={{0,512},{1,513},{2,514},{3,515},{4,516},{5,517},{6,518},{7,519},{8... | collective-permute-start | bytes 2654216 | tf_op jit(solution)/shard_map/ppermute | solution.py:337
  75.1 34.7 %collective-permute-start.13 = (bf16[200,1152]{1,0:T(8,128)(2,1)S(1)}, bf16[200,1152]{1,0:T(8,128)(2,1)S(1)}, u32[]{:S(2)}, u32[]{:S(2)}) collective-permute-start(bf16[200,1152]{1,0:T(8,128)(2,1)S(1)} %get-tuple-element.89), channel_id=1, source_target_pairs={{0,128},{1,385},{2,130},{3,387},{4,132},{5,389},{6,134},{7,391},{8... | collective-permute-start | bytes 1382408 | tf_op jit(solution)/shard_map/ppermute | solution.py:337
  81.2 3.1 %collective-permute-start.1 = (f32[4,1152]{1,0:T(4,128)S(1)}, f32[4,1152]{1,0:T(4,128)S(1)}, u32[]{:S(2)}, u32[]{:S(2)}) collective-permute-start(f32[4,1152]{1,0:T(4,128)S(1)} %get-tuple-element.199), channel_id=1, source_target_pairs={{0,1},{1,0},{2,3},{3,2},{4,5},{5,4},{6,7},{7,6},{8,9},{9,8},{10,11... | collective-permute-start | bytes 55304 | tf_op jit(solution)/shard_map/while/body/ppermute | solution.py:337
  84.3 5.6 %collective-permute-start.2 = (f32[4,1152]{1,0:T(4,128)S(1)}, f32[4,1152]{1,0:T(4,128)S(1)}, u32[]{:S(2)}, u32[]{:S(2)}) collective-permute-start(f32[4,1152]{1,0:T(4,128)S(1)} %add.59), channel_id=1, source_target_pairs={{0,8},{1,9},{2,10},{3,11},{4,12},{5,13},{6,14},{7,15},{8,0},{9,1},... | collective-permute-start | bytes 55304 | tf_op jit(solution)/shard_map/while/body/ppermute | solution.py:337
  89.9 6.9 %collective-permute-start.3 = (f32[4,1152]{1,0:T(4,128)S(1)}, f32[4,1152]{1,0:T(4,128)S(1)}, u32[]{:S(2)}, u32[]{:S(2)}) collective-permute-start(f32[4,1152]{1,0:T(4,128)S(1)} %add.60), channel_id=1, source_target_pairs={{0,24},{1,25},{2,26},{3,27},{4,28},{5,29},{6,30},{7,31},{8,16},{9,... | collective-permute-start | bytes 55304 | tf_op jit(solution)/shard_map/while/body/ppermute | solution.py:337
  96.8 5.6 %collective-permute-start.4 = (f32[4,1152]{1,0:T(4,128)S(1)}, f32[4,1152]{1,0:T(4,128)S(1)}, u32[]{:S(2)}, u32[]{:S(2)}) collective-permute-start(f32[4,1152]{1,0:T(4,128)S(1)} %add.61), channel_id=1, source_target_pairs={{0,512},{1,513},{2,514},{3,515},{4,516},{5,517},{6,518},{7,519},{8... | collective-permute-start | bytes 55304 | tf_op jit(solution)/shard_map/while/body/ppermute | solution.py:337
  102.5 51.1 %copy-start.5 = (bf16[384,1152]{1,0:T(8,128)(2,1)}, bf16[384,1152]{1,0:T(8,128)(2,1)S(1)}, u32[]{:S(2)}) copy-start(bf16[384,1152]{1,0:T(8,128)(2,1)S(1)} %collective-permute-done.12.refs_1_) | copy-start | bytes 2654212
  104.0 33.9 %collective-permute-start.14 = (bf16[192,1152]{1,0:T(8,128)(2,1)S(1)}, bf16[192,1152]{1,0:T(8,128)(2,1)S(1)}, u32[]{:S(2)}, u32[]{:S(2)}) collective-permute-start(bf16[192,1152]{1,0:T(8,128)(2,1)S(1)} %add_convert_fusion), channel_id=1, source_target_pairs={{0,384},{1,129},{2,386},{3,131},{4,388},{5,133},{6,390},{7,135},{8... | collective-permute-start | bytes 1327112 | tf_op jit(solution)/shard_map/ppermute | solution.py:337
  109.9 32.2 %copy-start.7 = (bf16[200,1152]{1,0:T(8,128)(2,1)}, bf16[200,1152]{1,0:T(8,128)(2,1)S(1)}, u32[]{:S(2)}) copy-start(bf16[200,1152]{1,0:T(8,128)(2,1)S(1)} %collective-permute-done.13.refs_1_) | copy-start | bytes 1382404
  109.9 6.9 %collective-permute-start.5 = (f32[4,1152]{1,0:T(4,128)S(1)}, f32[4,1152]{1,0:T(4,128)S(1)}, u32[]{:S(2)}, u32[]{:S(2)}) collective-permute-start(f32[4,1152]{1,0:T(4,128)S(1)} %get-tuple-element.211), channel_id=1, source_target_pairs={{0,518},{1,519},{2,512},{3,513},{4,514},{5,515},{6,516},{7,517},{8... | collective-permute-start | bytes 55304 | tf_op jit(solution)/shard_map/while/body/ppermute | solution.py:337
  116.8 7.4 %collective-permute-start.6 = (f32[4,1152]{1,0:T(4,128)S(1)}, f32[4,1152]{1,0:T(4,128)S(1)}, u32[]{:S(2)}, u32[]{:S(2)}) collective-permute-start(f32[4,1152]{1,0:T(4,128)S(1)} %add.64), channel_id=1, source_target_pairs={{0,514},{1,515},{2,516},{3,517},{4,518},{5,519},{6,512},{7,513},{8... | collective-permute-start | bytes 55304 | tf_op jit(solution)/shard_map/while/body/ppermute | solution.py:337
  124.2 5.6 %collective-permute-start.7 = (f32[4,1152]{1,0:T(4,128)S(1)}, f32[4,1152]{1,0:T(4,128)S(1)}, u32[]{:S(2)}, u32[]{:S(2)}) collective-permute-start(f32[4,1152]{1,0:T(4,128)S(1)} %add.65), channel_id=1, source_target_pairs={{0,32},{1,33},{2,34},{3,35},{4,36},{5,37},{6,38},{7,39},{8,40},{9,... | collective-permute-start | bytes 55304 | tf_op jit(solution)/shard_map/while/body/ppermute | solution.py:337
  129.9 8.1 %collective-permute-start.8 = (f32[4,1152]{1,0:T(4,128)S(1)}, f32[4,1152]{1,0:T(4,128)S(1)}, u32[]{:S(2)}, u32[]{:S(2)}) collective-permute-start(f32[4,1152]{1,0:T(4,128)S(1)} %add.66), channel_id=1, source_target_pairs={{0,480},{1,481},{2,482},{3,483},{4,484},{5,485},{6,486},{7,487},{8... | collective-permute-start | bytes 55304 | tf_op jit(solution)/shard_map/while/body/ppermute | solution.py:337
  138.0 15.6 %copy-start.8 = (bf16[192,1152]{1,0:T(8,128)(2,1)}, bf16[192,1152]{1,0:T(8,128)(2,1)S(1)}, u32[]{:S(2)}) copy-start(bf16[192,1152]{1,0:T(8,128)(2,1)S(1)} %collective-permute-done.14.refs_2_) | copy-start | bytes 1327108
  138.0 7.5 %collective-permute-start.15 = (f32[4,1152]{1,0:T(4,128)S(1)}, f32[4,1152]{1,0:T(4,128)S(1)}, u32[]{:S(2)}, u32[]{:S(2)}) collective-permute-start(f32[4,1152]{1,0:T(4,128)S(1)} %get-tuple-element.92), channel_id=1, source_target_pairs={{0,96},{1,97},{2,98},{3,99},{4,100},{5,101},{6,102},{7,103},{8,104... | collective-permute-start | bytes 55304 | tf_op jit(solution)/shard_map/ppermute | solution.py:337
  145.5 11.7 %collective-permute-start.16 = (f32[4,1152]{1,0:T(4,128)S(1)}, f32[4,1152]{1,0:T(4,128)S(1)}, u32[]{:S(2)}, u32[]{:S(2)}) collective-permute-start(f32[4,1152]{1,0:T(4,128)S(1)} %add.43), channel_id=1, source_target_pairs={{0,352},{1,353},{2,354},{3,355},{4,356},{5,357},{6,358},{7,359},{8... | collective-permute-start | bytes 55304 | tf_op jit(solution)/shard_map/ppermute | solution.py:337
